TPU v7x, 256 devices: a whole 4x4x8 slice. The times are simulated.
256 devices in a mesh: seq: 32 (over y_hi, z, core), head: 8 (over y_lo, x).
Axes of the slice: x: 4, y: 4 (y_hi: 2, y_lo: 2; y = y_hi * 2 + y_lo), z: 8, core: 2. Of those that a mesh axis runs over, the one named last changes fastest.
Arguments:
- query_proj: bfloat16 [12288, 2048], P('seq', 'head'), may hold values from -100 to 100
- key_proj: bfloat16 [12288, 2048], P('seq', 'head'), may hold values from -4 to 4
- value_proj: bfloat16 [12288, 2048], P('seq', 'head'), may hold values from -6 to 6
- query_tangent: bfloat16 [12288, 2048], P('seq', 'head'), may hold values from -6 to 6
- key_tangent: bfloat16 [12288, 2048], P('seq', 'head'), may hold values from -6 to 6
- value_tangent: bfloat16 [12288, 2048], P('seq', 'head'), may hold values from -16 to 16
Outputs:
- attended: bfloat16 [12288, 2048], P('seq', 'head')
- tangent_unit: bfloat16 [12288, 2048], P('seq', 'head')
All inputs are finite; a program needn't handle non-finite values.
Results may differ from a plain program's by a relative error of at most 0.0095.
Values may be sent and summed in bfloat16 or wider, within the bound.
No kernel may reach another device: no remote copies, remote signals or barrier semaphores. Data moves between devices by JAX's collectives and lax.ppermute only.
A program may use at most 128 MiB of HBM per device.

v0:
```python
import functools
import math

import jax
import jax.numpy as jnp
from jax import lax
from jax.experimental import pallas as pl
from jax.experimental.pallas import tpu as pltpu
from jax.sharding import Mesh
from jax.sharding import PartitionSpec as P

HEADS = 16
DH = 128
SCALE = 1.0 / math.sqrt(DH)
LOG2E = math.log2(math.e)
LIMIT = 2.0**40
TILE = 256
SMALL = 128
F32 = jnp.float32
BF16 = jnp.bfloat16
SWAP = ((0, 1), (1, 0))
PARAMS = pltpu.CompilerParams(vmem_limit_bytes=28 << 20)


def nt(a, b):
    return lax.dot_general(a, b, (((1,), (1,)), ((), ())), preferred_element_type=F32)


def nn(a, b):
    return lax.dot_general(a, b, (((1,), (0,)), ((), ())), preferred_element_type=F32)


def pack_kernel(q, k, v, qt, kt, vt, own_kv, own_q, other_kv, other_q):
    flip = lax.axis_index("yh") == 1
    spots = ((kt, 0, 0), (k, 0, 1), (v, 0, 2), (vt, 0, 3), (q, 1, 0), (qt, 1, 1))
    for ref, which, at in spots:
        low, high = ref[:, :DH], ref[:, DH:]
        cols = slice(at * DH, (at + 1) * DH)
        (own_kv, own_q)[which][:, cols] = jnp.where(flip, high, low)
        (other_kv, other_q)[which][:, cols] = jnp.where(flip, low, high)


def pack(*arrays):
    rows = arrays[0].shape[0]
    row = lambda width: pl.BlockSpec((rows // 2, width), lambda i: (i, 0))
    shapes = [jax.ShapeDtypeStruct((rows, n * DH), BF16) for n in (4, 2, 4, 2)]
    return pl.pallas_call(
        pack_kernel,
        grid=(2,),
        in_specs=[row(2 * DH)] * 6,
        out_specs=[row(n * DH) for n in (4, 2, 4, 2)],
        out_shape=shapes,
        compiler_params=pltpu.CompilerParams(vmem_limit_bytes=60 << 20),
        cost_estimate=pl.CostEstimate(flops=0, bytes_accessed=12 * rows * 2 * DH * 2, transcendentals=0),
        name="pack",
    )(*arrays)


def lanes(x):
    out = x[:, :DH]
    for i in range(1, x.shape[1] // DH):
        out = out + x[:, i * DH : (i + 1) * DH]
    return out


def wide(x, times):
    return jnp.concatenate([x] * times, axis=1)


def dots(query, kv):
    return nt(query[:, :DH], kv[:, DH : 2 * DH]), nt(query, kv[:, : 2 * DH])


def part(products, kv, old, exact):
    scores, tangent = products
    rows, keys = scores.shape
    scores = scores * (SCALE * LOG2E)
    if exact:
        top = jnp.broadcast_to(jnp.max(scores, axis=1, keepdims=True), (rows, DH))
        if old is not None:
            top = jnp.maximum(top, old[4])
    else:
        top = old[4]
    weights = jnp.exp2(scores - wide(top, keys // DH))
    tilted = weights * tangent
    total, cross = lanes(weights), lanes(tilted)
    both = nn(weights.astype(BF16), kv[:, 2 * DH :])
    moved = both[:, DH:] + nn(tilted.astype(BF16), kv[:, 2 * DH : 3 * DH]) * SCALE
    new = (both[:, :DH], moved, total, cross)
    if old is None:
        return (*new, top)
    if exact:
        factor = jnp.exp2(old[4] - top)
        return (*(n + o * factor for n, o in zip(new, old[:4])), top)
    return (*(n + o for n, o in zip(new, old[:4])), top)


def read(ref, rows):
    return tuple(ref[rows, i * DH : (i + 1) * DH] for i in range(5))


def write(ref, state, rows):
    for i, piece in enumerate(state):
        ref[rows, i * DH : (i + 1) * DH] = piece


def begin_kernel(own_kv, peer_kv, own_q, core_q, state, query, kv):
    rows = own_kv.shape[0]
    kv[:rows, :] = own_kv[...]
    kv[rows:, :] = peer_kv[...]
    query[: 2 * rows, :] = own_q[...]
    query[2 * rows :, :] = core_q[...]

    def body(i, carry):
        at = pl.multiple_of(i * 2 * TILE, 2 * TILE)
        spans = [pl.ds(at, TILE), pl.ds(at + TILE, TILE)]
        products = [dots(query[span, :], kv) for span in spans]
        for span, product in zip(spans, products):
            write(state, part(product, kv, None, True), span)
        return carry

    lax.fori_loop(0, query.shape[0] // (2 * TILE), body, 0)


def attend_kernel(blocks, base, last, q_ref, *refs):
    kv_refs = refs[:blocks]
    old_ref = refs[blocks]
    outs = refs[blocks + 1 : blocks + (3 if last else 2)]
    rest = list(refs[blocks + 1 + len(outs) :])
    kv = kv_refs[0]
    if blocks > 1:
        kv = rest.pop(0)
        at = 0
        for ref in kv_refs:
            kv[at : at + ref.shape[0], :] = ref[...]
            at += ref.shape[0]
    new_ref = rest.pop(0) if last else outs[0]
    rows, keys = new_ref.shape[0], kv.shape[0]
    each = 2 if rows % (2 * TILE) == 0 else rows // TILE

    def body(i, worst):
        starts = [pl.multiple_of(i * each * TILE, TILE) + n * TILE for n in range(each)]
        ahead = dots(q_ref[pl.ds(base + starts[0], TILE), :], kv)
        for n, at in enumerate(starts):
            now = ahead
            if n + 1 < each:
                ahead = dots(q_ref[pl.ds(base + starts[n + 1], TILE), :], kv)
            state = part(now, kv, read(old_ref, pl.ds(base + at, TILE)), False)
            write(new_ref, state, pl.ds(at, TILE))
            worst = jnp.maximum(worst, jnp.max(state[2].reshape(TILE // 8, 8, DH), axis=0))
        return worst

    worst = lax.fori_loop(0, rows // (each * TILE), body, jnp.zeros((8, DH), F32))

    @pl.when(jnp.logical_not(jnp.max(worst) < LIMIT))
    def _():
        def again(i, carry):
            at = pl.multiple_of(i * SMALL, SMALL)
            here, there = pl.ds(at, SMALL), pl.ds(base + at, SMALL)
            new_ref[here, :] = old_ref[there, :]

            def some(j, inner):
                block = kv[pl.ds(pl.multiple_of(j * 3 * DH, 3 * DH), 3 * DH), :]
                write(new_ref, part(dots(q_ref[there, :], block), block, read(new_ref, here), True), here)
                return inner

            return lax.fori_loop(0, keys // (3 * DH), some, carry)

        lax.fori_loop(0, rows // SMALL, again, 0)

    if last:
        out, stats = outs
        primal, moved, total, cross, top = read(new_ref, slice(0, rows))
        total = jnp.sum(total, axis=1, keepdims=True)
        cross = jnp.sum(cross, axis=1, keepdims=True)
        inverse = 1.0 / total
        out[:, :DH] = (primal * inverse).astype(out.dtype)
        out[:, DH:] = (moved * inverse).astype(out.dtype)
        lane = lax.broadcasted_iota(jnp.int32, top.shape, 1)
        stats[...] = jnp.where(lane == 0, top + jnp.log2(total), cross * (SCALE * inverse))


def cost(rows, keys):
    return pl.CostEstimate(
        flops=2 * 8 * rows * keys * DH, bytes_accessed=keys * 4 * DH * 2, transcendentals=rows * keys
    )


def begin(*arrays):
    rows, keys = 4 * arrays[0].shape[0], 2 * arrays[0].shape[0]
    return pl.pallas_call(
        begin_kernel,
        out_shape=[jax.ShapeDtypeStruct((rows, 5 * DH), F32), jax.ShapeDtypeStruct((rows, 2 * DH), BF16)],
        scratch_shapes=[pltpu.VMEM((keys, 4 * DH), BF16)],
        compiler_params=PARAMS,
        cost_estimate=cost(rows, keys),
        name="begin",
    )(*arrays)


def attend(query, kvs, state, span=None, kind=None):
    base, end = span or (0, query.shape[0])
    rows = end - base
    keys = sum(kv.shape[0] for kv in kvs)
    scratch = [pltpu.VMEM((keys, 4 * DH), BF16)] if len(kvs) > 1 else []
    if kind is None:
        shapes = jax.ShapeDtypeStruct((rows, 5 * DH), F32)
    else:
        shapes = [jax.ShapeDtypeStruct((rows, 2 * DH), kind), jax.ShapeDtypeStruct((rows, DH), F32)]
        scratch.append(pltpu.VMEM((rows, 5 * DH), F32))
    return pl.pallas_call(
        functools.partial(attend_kernel, len(kvs), base, kind is not None),
        out_shape=shapes,
        scratch_shapes=scratch,
        compiler_params=PARAMS,
        cost_estimate=cost(rows, keys),
        name="attend",
    )(query, *kvs, state)


def join_kernel(mine, mine_stat, other, other_stat, keep, send, squares):
    yh = lax.axis_index("yh")
    half = keep.shape[0]
    for step, rows in enumerate((slice(0, half), slice(half, 2 * half))):
        top_a, top_b = mine_stat[rows, 0:1], other_stat[rows, 0:1]
        top = jnp.maximum(top_a, top_b)
        part_a, part_b = jnp.exp2(top_a - top), jnp.exp2(top_b - top)
        inverse = 1.0 / (part_a + part_b)
        part_a, part_b = part_a * inverse, part_b * inverse
        both = mine[rows, :] * part_a + other[rows, :].astype(F32) * part_b
        cross = mine_stat[rows, 1:2] * part_a + other_stat[rows, 1:2] * part_b
        out = both[:, :DH]
        moved = both[:, DH:] - cross * out
        kept = (keep, send)[step]
        kept[:, :DH] = out.astype(kept.dtype)
        kept[:, DH:] = moved.astype(kept.dtype)
        sums = lax.dot_general(
            jnp.ones((8, DH), F32),
            moved * moved,
            (((1,), (1,)), ((), ())),
            precision=lax.Precision.HIGHEST,
            preferred_element_type=F32,
        )
        row = lax.broadcasted_iota(jnp.int32, (8, DH), 0)
        slab = jnp.zeros((8, DH), F32)
        for i in range(half // DH):
            slab = jnp.where(row == i, sums[:, i * DH : (i + 1) * DH], slab)
        owner = yh if step == 0 else 1 - yh
        for i in range(8):
            squares[owner * 8 + i] = slab


def join(*arrays):
    half = arrays[0].shape[0] // 2
    return pl.pallas_call(
        join_kernel,
        out_shape=[
            jax.ShapeDtypeStruct((half, 2 * DH), F32),
            jax.ShapeDtypeStruct((half, 2 * DH), BF16),
            jax.ShapeDtypeStruct((16, 8, DH), F32),
        ],
        compiler_params=PARAMS,
        name="join",
    )(*arrays)


def finish_kernel(keep, come, squares, attended, unit):
    flip = lax.axis_index("yh") == 1
    sums = squares[0]
    for i in range(1, 16):
        sums = sums + squares[i]
    row = lax.broadcasted_iota(jnp.int32, (8, DH), 0)
    for i in range(keep.shape[0] // DH):
        rows = slice(i * DH, (i + 1) * DH)
        mean = lax.dot_general(
            jnp.where(row == i, sums, 0.0),
            jnp.full((8, DH), 1.0 / (HEADS * DH), F32),
            (((0,), (0,)), ((), ())),
            precision=lax.Precision.HIGHEST,
            preferred_element_type=F32,
        )
        inverse = 1.0 / jnp.sqrt(mean + 1e-06)
        mine, other = keep[rows, :DH].astype(BF16), come[rows, :DH]
        attended[rows, :DH] = jnp.where(flip, other, mine)
        attended[rows, DH:] = jnp.where(flip, mine, other)
        mine = (keep[rows, DH:] * inverse).astype(BF16)
        other = (come[rows, DH:].astype(F32) * inverse).astype(BF16)
        unit[rows, :DH] = jnp.where(flip, other, mine)
        unit[rows, DH:] = jnp.where(flip, mine, other)


def finish(*arrays):
    out = jax.ShapeDtypeStruct(arrays[1].shape, BF16)
    return pl.pallas_call(finish_kernel, out_shape=(out, out), compiler_params=PARAMS, name="finish")(*arrays)


def on_device(ring, q, k, v, qt, kt, vt):
    tokens = q.shape[0]
    hop_pairs = [(z * 2 + c, (z + 1 - 2 * c) % ring * 2 + c) for z in range(ring) for c in range(2)]
    hop = lambda a: lax.ppermute(a, ("z", "core"), hop_pairs)
    over_y = lambda a: lax.ppermute(a, "yh", SWAP)
    over_core = lambda a: lax.ppermute(a, "core", SWAP)
    def after(block, state):
        return lax.optimization_barrier((block, state))

    own_kv, own_q, other_kv, other_q = pack(q, k, v, qt, kt, vt)
    peer_kv = over_y(other_kv)
    other_q, peer_kv = after(other_q, peer_kv)
    peer_q = over_y(other_q)
    near = hop(jnp.concatenate([own_kv, over_core(own_kv)], axis=0))
    far = hop(jnp.concatenate([peer_kv, over_core(peer_kv)], axis=0))
    near_next = hop(near)
    pair_q = jnp.concatenate([own_q, peer_q], axis=0)
    state, query = begin(own_kv, peer_kv, pair_q, over_core(pair_q))
    near_two, state = after(near_next, state)
    near_next = hop(near_two)
    state = attend(query, [near], state)
    state = attend(query, [near_two], state)
    far, state = after(far, state)
    far_next = hop(far)
    state = attend(query, [far], state)
    near, state = after(near_next, state)
    part, state = after(near[:tokens], state)
    last_near = hop(part)
    state = attend(query, [near], state)
    far, state = after(far_next, state)
    far_next = hop(far)
    state = attend(query, [far], state)
    last_near, state = after(last_near, state)
    state = attend(query, [last_near], state)
    far, state = after(far_next, state)
    far_next = hop(far[:tokens])
    state = attend(query, [far], state)
    rows = query.shape[0]
    there, there_stat = attend(query, [far_next], state, (rows // 2, rows), BF16)
    come, come_stat = over_core(there), over_core(there_stat)
    here, here_stat = attend(query, [far_next], state, (0, rows // 2), F32)
    keep, send, squares = join(here, here_stat, come, come_stat)
    come = over_y(send)
    squares = lax.all_to_all(squares, ("yh", "yl", "x"), 0, 0, tiled=True)
    return finish(keep, come, squares)


def solution(mesh):
    fine = Mesh(mesh.devices.reshape(2, -1, 2, 2, mesh.shape["head"] // 2), ("yh", "z", "core", "yl", "x"))
    spec = P(("yh", "z", "core"), ("yl", "x"))
    return jax.shard_map(
        functools.partial(on_device, fine.shape["z"]),
        mesh=fine,
        in_specs=(spec,) * 6,
        out_specs=(spec, spec),
        check_vma=False,
    )
```

profile of v0, /device:TPU:1, one launch (start us, length us, event | category | flops | bytes accessed | tf_op | source)
XLA Modules:
  0.0 112.7 jit_solution(6577063023248772979)
XLA Ops:
  0.6 2.3 %pack.1 = (bf16[384,512]{1,0:T(8,128)(2,1)}, bf16[384,256]{1,0:T(8,128)(2,1)}, bf16[384,512]{1,0:T(8,128)(2,1)}, bf16[384,256]{1,0:T(8,128)(2,1)}) custom-call(bf16[384,256]{1,0:T(8,128)(2,1)} %q.1, bf16[384,256]{1,0:T(8,128)(2,1)} %k.1, bf16[384,256]{1,0:T(8,128)(2,1)} %v.1, bf16[384,256]{1,0:T(8,128)(2,1)} %qt.1, bf16[384,256]{1,0:T(8,128)(2,1)} %kt.1, ...), custom_call_target="tpu_custom_call" | custom-call | bytes 2359296 | tf_op jit(solution)/shard_map/pack/pallas_call | solution.py:47
  2.9 0.0 copy-start
  2.9 3.3 %collective-permute-start.5 = (bf16[384,512]{1,0:T(8,128)(2,1)}, bf16[384,512]{1,0:T(8,128)(2,1)S(1)}, u32[]{:S(2)}, u32[]{:S(2)}) collective-permute-start(bf16[384,512]{1,0:T(8,128)(2,1)} %get-tuple-element.31.own_kv), channel_id=1, source_target_pairs={{0,8},{8,0},{1,9},{9,1},{2,10},{10,2},{3,11},{11,3},{4,12},{12,4},... | collective-permute-start | bytes 1179656 | tf_op jit(solution)/shard_map/ppermute | solution.py:302
  6.2 1.6 %collective-permute-done.5 = bf16[384,512]{1,0:T(8,128)(2,1)S(1)} collective-permute-done((bf16[384,512]{1,0:T(8,128)(2,1)}, bf16[384,512]{1,0:T(8,128)(2,1)S(1)}, u32[]{:S(2)}, u32[]{:S(2)}) %collective-permute-start.5) | collective-permute-done | bytes 393248 | tf_op jit(solution)/shard_map/ppermute | solution.py:302
  7.8 1.0 pad_maximum_fusion.1
  8.8 3.9 %collective-permute-start.6 = (bf16[768,512]{1,0:T(8,128)(2,1)S(1)}, bf16[768,512]{1,0:T(8,128)(2,1)S(1)}, u32[]{:S(2)}, u32[]{:S(2)}) collective-permute-start(bf16[768,512]{1,0:T(8,128)(2,1)S(1)} %pad_maximum_fusion.1), channel_id=1, source_target_pairs={{0,16},{8,120},{16,32},{24,8},{32,48},{40,24},{48,64},{56,40},{64,... | collective-permute-start | bytes 2359304 | tf_op jit(solution)/shard_map/ppermute | solution.py:300
  12.8 2.9 %collective-permute-start = (bf16[384,512]{1,0:T(8,128)(2,1)}, bf16[384,512]{1,0:T(8,128)(2,1)S(1)}, u32[]{:S(2)}, u32[]{:S(2)}) collective-permute-start(bf16[384,512]{1,0:T(8,128)(2,1)} %get-tuple-element.33), channel_id=1, source_target_pairs={{0,128},{128,0},{1,129},{129,1},{2,130},{130,2},{3,131},{131,3},{4... | collective-permute-start | bytes 1179656 | tf_op jit(solution)/shard_map/ppermute | solution.py:301
  15.7 6.8 %collective-permute-done.peer_kv = bf16[384,512]{1,0:T(8,128)(2,1)S(1)} collective-permute-done((bf16[384,512]{1,0:T(8,128)(2,1)}, bf16[384,512]{1,0:T(8,128)(2,1)S(1)}, u32[]{:S(2)}, u32[]{:S(2)}) %collective-permute-start) | collective-permute-done | bytes 393248 | tf_op jit(solution)/shard_map/ppermute | solution.py:301
  22.5 3.2 %collective-permute-start.1 = (bf16[384,256]{1,0:T(8,128)(2,1)}, bf16[384,256]{1,0:T(8,128)(2,1)S(1)}, u32[]{:S(2)}, u32[]{:S(2)}) collective-permute-start(bf16[384,256]{1,0:T(8,128)(2,1)} %get-tuple-element.36), channel_id=1, source_target_pairs={{0,128},{128,0},{1,129},{129,1},{2,130},{130,2},{3,131},{131,3},{4... | collective-permute-start | bytes 589832 | tf_op jit(solution)/shard_map/ppermute | solution.py:301
  25.7 0.0 collective-permute-start.3
  25.7 0.0 collective-permute-done.6.refs_0_
  25.7 4.2 %collective-permute-start.7 = (bf16[768,512]{1,0:T(8,128)(2,1)S(1)}, bf16[768,512]{1,0:T(8,128)(2,1)S(1)}, u32[]{:S(2)}, u32[]{:S(2)}) collective-permute-start(bf16[768,512]{1,0:T(8,128)(2,1)S(1)} %collective-permute-done.6.refs_0_), channel_id=1, source_target_pairs={{0,16},{8,120},{16,32},{24,8},{32,48},{40,24},{48,64},{56,40},{64,... | collective-permute-start | bytes 2359304 | tf_op jit(solution)/shard_map/ppermute | solution.py:300
  29.9 0.9 constant_dynamic-update-slice_fusion.1
  30.9 0.0 collective-permute-done.1
  30.9 0.1 collective-permute-start.2
  31.0 0.0 collective-permute-done.3
  31.0 0.1 pad_maximum_fusion
  31.1 4.3 %collective-permute-start.4 = (bf16[768,512]{1,0:T(8,128)(2,1)S(1)}, bf16[768,512]{1,0:T(8,128)(2,1)S(1)}, u32[]{:S(2)}, u32[]{:S(2)}) collective-permute-start(bf16[768,512]{1,0:T(8,128)(2,1)S(1)} %pad_maximum_fusion), channel_id=1, source_target_pairs={{0,16},{8,120},{16,32},{24,8},{32,48},{40,24},{48,64},{56,40},{64,... | collective-permute-start | bytes 2359304 | tf_op jit(solution)/shard_map/ppermute | solution.py:300
  35.4 0.0 collective-permute-done.2.core_q
  35.4 0.0 copy-done
  35.4 3.7 %begin.1 = (f32[1536,640]{1,0:T(8,128)S(1)}, bf16[1536,256]{1,0:T(8,128)(2,1)S(1)}) custom-call(bf16[384,512]{1,0:T(8,128)(2,1)S(1)} %copy-done, bf16[384,512]{1,0:T(8,128)(2,1)S(1)} %collective-permute-done.peer_kv, bf16[768,256]{1,0:T(8,128)(2,1)S(1)} %constant_dynamic-update-slice_fusion.own_q, bf16[768,256]{1,0:T(8,128)(2,1)S(1)} %collective-permute-done.2.core_q), custom_call_target="tpu_custom_call" | custom-call | flops 2415919104 | bytes 786432 | tf_op jit(solution)/shard_map/begin/pallas_call | solution.py:191
  39.2 0.0 collective-permute-done.7.refs_0_
  39.2 2.8 %collective-permute-start.9 = (bf16[768,512]{1,0:T(8,128)(2,1)S(1)}, bf16[768,512]{1,0:T(8,128)(2,1)S(1)}, u32[]{:S(2)}, u32[]{:S(2)}) collective-permute-start(bf16[768,512]{1,0:T(8,128)(2,1)S(1)} %collective-permute-done.7.refs_0_), channel_id=1, source_target_pairs={{0,16},{8,120},{16,32},{24,8},{32,48},{40,24},{48,64},{56,40},{64,... | collective-permute-start | bytes 2359304 | tf_op jit(solution)/shard_map/ppermute | solution.py:300
  42.0 3.2 %attend.9.refs_1_ = f32[1536,640]{1,0:T(8,128)S(1)} custom-call(bf16[1536,256]{1,0:T(8,128)(2,1)S(1)} %get-tuple-element.37.q_ref, bf16[768,512]{1,0:T(8,128)(2,1)S(1)} %collective-permute-done.6.refs_0_, f32[1536,640]{1,0:T(8,128)S(1)} %get-tuple-element.40.refs_1_), custom_call_target="tpu_custom_call" | custom-call | flops 2415919104 | bytes 786432 | tf_op jit(solution)/shard_map/attend/pallas_call | solution.py:211
  45.2 3.3 %attend.10.refs_1_ = f32[1536,640]{1,0:T(8,128)S(1)} custom-call(bf16[1536,256]{1,0:T(8,128)(2,1)S(1)} %get-tuple-element.37.q_ref, bf16[768,512]{1,0:T(8,128)(2,1)S(1)} %collective-permute-done.7.refs_0_, f32[1536,640]{1,0:T(8,128)S(1)} %attend.9.refs_1_), custom_call_target="tpu_custom_call" | custom-call | flops 2415919104 | bytes 786432 | tf_op jit(solution)/shard_map/attend/pallas_call | solution.py:211
  48.5 0.0 collective-permute-done.4.refs_0_
  48.5 1.9 %collective-permute-start.8 = (bf16[768,512]{1,0:T(8,128)(2,1)S(1)}, bf16[768,512]{1,0:T(8,128)(2,1)S(1)}, u32[]{:S(2)}, u32[]{:S(2)}) collective-permute-start(bf16[768,512]{1,0:T(8,128)(2,1)S(1)} %collective-permute-done.4.refs_0_), channel_id=1, source_target_pairs={{0,16},{8,120},{16,32},{24,8},{32,48},{40,24},{48,64},{56,40},{64,... | collective-permute-start | bytes 2359304 | tf_op jit(solution)/shard_map/ppermute | solution.py:300
  50.4 3.4 %attend.11.refs_1_ = f32[1536,640]{1,0:T(8,128)S(1)} custom-call(bf16[1536,256]{1,0:T(8,128)(2,1)S(1)} %get-tuple-element.37.q_ref, bf16[768,512]{1,0:T(8,128)(2,1)S(1)} %collective-permute-done.4.refs_0_, f32[1536,640]{1,0:T(8,128)S(1)} %attend.10.refs_1_), custom_call_target="tpu_custom_call" | custom-call | flops 2415919104 | bytes 786432 | tf_op jit(solution)/shard_map/attend/pallas_call | solution.py:211
  53.9 1.9 %collective-permute-done.9.refs_0_ = bf16[768,512]{1,0:T(8,128)(2,1)S(1)} collective-permute-done((bf16[768,512]{1,0:T(8,128)(2,1)S(1)}, bf16[768,512]{1,0:T(8,128)(2,1)S(1)}, u32[]{:S(2)}, u32[]{:S(2)}) %collective-permute-start.9) | collective-permute-done | bytes 786464 | tf_op jit(solution)/shard_map/ppermute | solution.py:300
  55.8 3.3 %attend.12.refs_1_ = f32[1536,640]{1,0:T(8,128)S(1)} custom-call(bf16[1536,256]{1,0:T(8,128)(2,1)S(1)} %get-tuple-element.37.q_ref, bf16[768,512]{1,0:T(8,128)(2,1)S(1)} %collective-permute-done.9.refs_0_, f32[1536,640]{1,0:T(8,128)S(1)} %attend.11.refs_1_), custom_call_target="tpu_custom_call" | custom-call | flops 2415919104 | bytes 786432 | tf_op jit(solution)/shard_map/attend/pallas_call | solution.py:211
  59.0 5.1 %collective-permute-done.8.refs_0_ = bf16[768,512]{1,0:T(8,128)(2,1)S(1)} collective-permute-done((bf16[768,512]{1,0:T(8,128)(2,1)S(1)}, bf16[768,512]{1,0:T(8,128)(2,1)S(1)}, u32[]{:S(2)}, u32[]{:S(2)}) %collective-permute-start.8) | collective-permute-done | bytes 786464 | tf_op jit(solution)/shard_map/ppermute | solution.py:300
  64.2 3.1 %collective-permute-start.10 = (bf16[768,512]{1,0:T(8,128)(2,1)S(1)}, bf16[768,512]{1,0:T(8,128)(2,1)S(1)}, u32[]{:S(2)}, u32[]{:S(2)}) collective-permute-start(bf16[768,512]{1,0:T(8,128)(2,1)S(1)} %collective-permute-done.8.refs_0_), channel_id=1, source_target_pairs={{0,16},{8,120},{16,32},{24,8},{32,48},{40,24},{48,64},{56,40},{64,... | collective-permute-start | bytes 2359304 | tf_op jit(solution)/shard_map/ppermute | solution.py:300
  67.3 0.0 collective-permute-start.11
  67.3 3.3 %attend.13.refs_1_ = f32[1536,640]{1,0:T(8,128)S(1)} custom-call(bf16[1536,256]{1,0:T(8,128)(2,1)S(1)} %get-tuple-element.37.q_ref, bf16[768,512]{1,0:T(8,128)(2,1)S(1)} %collective-permute-done.8.refs_0_, f32[1536,640]{1,0:T(8,128)S(1)} %attend.12.refs_1_), custom_call_target="tpu_custom_call" | custom-call | flops 2415919104 | bytes 786432 | tf_op jit(solution)/shard_map/attend/pallas_call | solution.py:211
  70.6 9.9 %collective-permute-done.11.refs_0_ = bf16[384,512]{1,0:T(8,128)(2,1)S(1)} collective-permute-done((bf16[384,512]{1,0:T(8,128)(2,1)S(1)}, bf16[384,512]{1,0:T(8,128)(2,1)S(1)}, u32[]{:S(2)}, u32[]{:S(2)}) %collective-permute-start.11) | collective-permute-done | bytes 393248 | tf_op jit(solution)/shard_map/ppermute | solution.py:300
  80.4 2.1 %attend.14.refs_1_ = f32[1536,640]{1,0:T(8,128)S(1)} custom-call(bf16[1536,256]{1,0:T(8,128)(2,1)S(1)} %get-tuple-element.37.q_ref, bf16[384,512]{1,0:T(8,128)(2,1)S(1)} %collective-permute-done.11.refs_0_, f32[1536,640]{1,0:T(8,128)S(1)} %attend.13.refs_1_), custom_call_target="tpu_custom_call" | custom-call | flops 1207959552 | bytes 393216 | tf_op jit(solution)/shard_map/attend/pallas_call | solution.py:211
  82.5 0.0 collective-permute-done.10.refs_0_
  82.6 3.2 %collective-permute-start.12 = (bf16[384,512]{1,0:T(8,128)(2,1)S(1)}, bf16[384,512]{1,0:T(8,128)(2,1)S(1)}, u32[]{:S(2)}, u32[]{:S(2)}) collective-permute-start(bf16[384,512]{1,0:T(8,128)(2,1)S(1)} %slice.7), channel_id=1, source_target_pairs={{0,16},{8,120},{16,32},{24,8},{32,48},{40,24},{48,64},{56,40},{64,... | collective-permute-start | bytes 1179656 | tf_op jit(solution)/shard_map/ppermute | solution.py:300
  85.8 3.2 %attend.15.refs_1_ = f32[1536,640]{1,0:T(8,128)S(1)} custom-call(bf16[1536,256]{1,0:T(8,128)(2,1)S(1)} %get-tuple-element.37.q_ref, bf16[768,512]{1,0:T(8,128)(2,1)S(1)} %collective-permute-done.10.refs_0_, f32[1536,640]{1,0:T(8,128)S(1)} %attend.14.refs_1_), custom_call_target="tpu_custom_call" | custom-call | flops 2415919104 | bytes 786432 | tf_op jit(solution)/shard_map/attend/pallas_call | solution.py:211
  89.0 1.5 %collective-permute-done.12.refs_0_ = bf16[384,512]{1,0:T(8,128)(2,1)S(1)} collective-permute-done((bf16[384,512]{1,0:T(8,128)(2,1)S(1)}, bf16[384,512]{1,0:T(8,128)(2,1)S(1)}, u32[]{:S(2)}, u32[]{:S(2)}) %collective-permute-start.12) | collective-permute-done | bytes 393248 | tf_op jit(solution)/shard_map/ppermute | solution.py:300
  90.5 1.2 %attend.17 = (bf16[768,256]{1,0:T(8,128)(2,1)S(1)}, f32[768,128]{1,0:T(8,128)S(1)}) custom-call(bf16[1536,256]{1,0:T(8,128)(2,1)S(1)} %get-tuple-element.37.q_ref, bf16[384,512]{1,0:T(8,128)(2,1)S(1)} %collective-permute-done.12.refs_0_, f32[1536,640]{1,0:T(8,128)S(1)} %attend.15.refs_1_), custom_call_target="tpu_custom_call" | custom-call | flops 603979776 | bytes 393216 | tf_op jit(solution)/shard_map/attend/pallas_call | solution.py:211
  91.7 3.7 %collective-permute-start.13 = (bf16[768,256]{1,0:T(8,128)(2,1)S(1)}, bf16[768,256]{1,0:T(8,128)(2,1)S(1)}, u32[]{:S(2)}, u32[]{:S(2)}) collective-permute-start(bf16[768,256]{1,0:T(8,128)(2,1)S(1)} %get-tuple-element.55), channel_id=1, source_target_pairs={{0,8},{8,0},{1,9},{9,1},{2,10},{10,2},{3,11},{11,3},{4,12},{12,4},... | collective-permute-start | bytes 1179656 | tf_op jit(solution)/shard_map/ppermute | solution.py:302
  95.4 0.1 collective-permute-start.14
  95.5 1.2 %attend.16 = (f32[768,256]{1,0:T(8,128)S(1)}, f32[768,128]{1,0:T(8,128)S(1)}) custom-call(bf16[1536,256]{1,0:T(8,128)(2,1)S(1)} %get-tuple-element.37.q_ref, bf16[384,512]{1,0:T(8,128)(2,1)S(1)} %collective-permute-done.12.refs_0_, f32[1536,640]{1,0:T(8,128)S(1)} %attend.15.refs_1_), custom_call_target="tpu_custom_call" | custom-call | flops 603979776 | bytes 393216 | tf_op jit(solution)/shard_map/attend/pallas_call | solution.py:211
  96.7 0.0 collective-permute-done.13.other
  96.8 0.6 collective-permute-done.14.other_stat
  97.3 1.0 join.1
  98.3 0.1 collective-permute-start.15
  98.4 13.1 %all_to_all.5.squares = f32[16,8,128]{2,1,0:T(8,128)S(1)} all-to-all(f32[16,8,128]{2,1,0:T(8,128)S(1)} %get-tuple-element.59), channel_id=1, replica_groups=mesh['yh'=2,'z'=8,'core'=2,'yl'=2,'x'=4] {'yh','yl','x'}, dimensions={0} | all-to-all | bytes 131072 | tf_op jit(solution)/shard_map/all_to_all | solution.py:340
  111.5 0.0 collective-permute-done.15.come
  111.5 1.2 %finish.1 = (bf16[384,256]{1,0:T(8,128)(2,1)}, bf16[384,256]{1,0:T(8,128)(2,1)}) custom-call(f32[384,256]{1,0:T(8,128)S(1)} %get-tuple-element.57.keep, bf16[384,256]{1,0:T(8,128)(2,1)S(1)} %collective-permute-done.15.come, f32[16,8,128]{2,1,0:T(8,128)S(1)} %all_to_all.5.squares), custom_call_target="tpu_custom_call" | custom-call | tf_op jit(solution)/shard_map/finish/pallas_call | solution.py:294
  (3 shorter events, 0.1 us)
Async XLA Ops:
  2.9 32.5 %copy-start = (bf16[384,512]{1,0:T(8,128)(2,1)S(1)}, bf16[384,512]{1,0:T(8,128)(2,1)}, u32[]{:S(2)}) copy-start(bf16[384,512]{1,0:T(8,128)(2,1)} %get-tuple-element.31.own_kv) | copy-start | bytes 1179652
  2.9 4.9 %collective-permute-start.5 = (bf16[384,512]{1,0:T(8,128)(2,1)}, bf16[384,512]{1,0:T(8,128)(2,1)S(1)}, u32[]{:S(2)}, u32[]{:S(2)}) collective-permute-start(bf16[384,512]{1,0:T(8,128)(2,1)} %get-tuple-element.31.own_kv), channel_id=1, source_target_pairs={{0,8},{8,0},{1,9},{9,1},{2,10},{10,2},{3,11},{11,3},{4,12},{12,4},... | collective-permute-start | bytes 1179656 | tf_op jit(solution)/shard_map/ppermute | solution.py:302
  8.8 16.9 %collective-permute-start.6 = (bf16[768,512]{1,0:T(8,128)(2,1)S(1)}, bf16[768,512]{1,0:T(8,128)(2,1)S(1)}, u32[]{:S(2)}, u32[]{:S(2)}) collective-permute-start(bf16[768,512]{1,0:T(8,128)(2,1)S(1)} %pad_maximum_fusion.1), channel_id=1, source_target_pairs={{0,16},{8,120},{16,32},{24,8},{32,48},{40,24},{48,64},{56,40},{64,... | collective-permute-start | bytes 2359304 | tf_op jit(solution)/shard_map/ppermute | solution.py:300
  12.8 9.7 %collective-permute-start = (bf16[384,512]{1,0:T(8,128)(2,1)}, bf16[384,512]{1,0:T(8,128)(2,1)S(1)}, u32[]{:S(2)}, u32[]{:S(2)}) collective-permute-start(bf16[384,512]{1,0:T(8,128)(2,1)} %get-tuple-element.33), channel_id=1, source_target_pairs={{0,128},{128,0},{1,129},{129,1},{2,130},{130,2},{3,131},{131,3},{4... | collective-permute-start | bytes 1179656 | tf_op jit(solution)/shard_map/ppermute | solution.py:301
  22.5 8.4 %collective-permute-start.1 = (bf16[384,256]{1,0:T(8,128)(2,1)}, bf16[384,256]{1,0:T(8,128)(2,1)S(1)}, u32[]{:S(2)}, u32[]{:S(2)}) collective-permute-start(bf16[384,256]{1,0:T(8,128)(2,1)} %get-tuple-element.36), channel_id=1, source_target_pairs={{0,128},{128,0},{1,129},{129,1},{2,130},{130,2},{3,131},{131,3},{4... | collective-permute-start | bytes 589832 | tf_op jit(solution)/shard_map/ppermute | solution.py:301
  25.7 5.3 %collective-permute-start.3 = (bf16[384,512]{1,0:T(8,128)(2,1)S(1)}, bf16[384,512]{1,0:T(8,128)(2,1)S(1)}, u32[]{:S(2)}, u32[]{:S(2)}) collective-permute-start(bf16[384,512]{1,0:T(8,128)(2,1)S(1)} %collective-permute-done.peer_kv), channel_id=1, source_target_pairs={{0,8},{8,0},{1,9},{9,1},{2,10},{10,2},{3,11},{11,3},{4,12},{12,4},... | collective-permute-start | bytes 1179656 | tf_op jit(solution)/shard_map/ppermute | solution.py:302
  25.7 13.5 %collective-permute-start.7 = (bf16[768,512]{1,0:T(8,128)(2,1)S(1)}, bf16[768,512]{1,0:T(8,128)(2,1)S(1)}, u32[]{:S(2)}, u32[]{:S(2)}) collective-permute-start(bf16[768,512]{1,0:T(8,128)(2,1)S(1)} %collective-permute-done.6.refs_0_), channel_id=1, source_target_pairs={{0,16},{8,120},{16,32},{24,8},{32,48},{40,24},{48,64},{56,40},{64,... | collective-permute-start | bytes 2359304 | tf_op jit(solution)/shard_map/ppermute | solution.py:300
  30.9 4.5 %collective-permute-start.2 = (bf16[768,256]{1,0:T(8,128)(2,1)S(1)}, bf16[768,256]{1,0:T(8,128)(2,1)S(1)}, u32[]{:S(2)}, u32[]{:S(2)}) collective-permute-start(bf16[768,256]{1,0:T(8,128)(2,1)S(1)} %constant_dynamic-update-slice_fusion.own_q), channel_id=1, source_target_pairs={{0,8},{8,0},{1,9},{9,1},{2,10},{10,2},{3,11},{11,3},{4,12},{12,4},... | collective-permute-start | bytes 1179656 | tf_op jit(solution)/shard_map/ppermute | solution.py:302
  31.1 17.4 %collective-permute-start.4 = (bf16[768,512]{1,0:T(8,128)(2,1)S(1)}, bf16[768,512]{1,0:T(8,128)(2,1)S(1)}, u32[]{:S(2)}, u32[]{:S(2)}) collective-permute-start(bf16[768,512]{1,0:T(8,128)(2,1)S(1)} %pad_maximum_fusion), channel_id=1, source_target_pairs={{0,16},{8,120},{16,32},{24,8},{32,48},{40,24},{48,64},{56,40},{64,... | collective-permute-start | bytes 2359304 | tf_op jit(solution)/shard_map/ppermute | solution.py:300
  39.2 16.6 %collective-permute-start.9 = (bf16[768,512]{1,0:T(8,128)(2,1)S(1)}, bf16[768,512]{1,0:T(8,128)(2,1)S(1)}, u32[]{:S(2)}, u32[]{:S(2)}) collective-permute-start(bf16[768,512]{1,0:T(8,128)(2,1)S(1)} %collective-permute-done.7.refs_0_), channel_id=1, source_target_pairs={{0,16},{8,120},{16,32},{24,8},{32,48},{40,24},{48,64},{56,40},{64,... | collective-permute-start | bytes 2359304 | tf_op jit(solution)/shard_map/ppermute | solution.py:300
  48.5 15.6 %collective-permute-start.8 = (bf16[768,512]{1,0:T(8,128)(2,1)S(1)}, bf16[768,512]{1,0:T(8,128)(2,1)S(1)}, u32[]{:S(2)}, u32[]{:S(2)}) collective-permute-start(bf16[768,512]{1,0:T(8,128)(2,1)S(1)} %collective-permute-done.4.refs_0_), channel_id=1, source_target_pairs={{0,16},{8,120},{16,32},{24,8},{32,48},{40,24},{48,64},{56,40},{64,... | collective-permute-start | bytes 2359304 | tf_op jit(solution)/shard_map/ppermute | solution.py:300
  64.2 18.4 %collective-permute-start.10 = (bf16[768,512]{1,0:T(8,128)(2,1)S(1)}, bf16[768,512]{1,0:T(8,128)(2,1)S(1)}, u32[]{:S(2)}, u32[]{:S(2)}) collective-permute-start(bf16[768,512]{1,0:T(8,128)(2,1)S(1)} %collective-permute-done.8.refs_0_), channel_id=1, source_target_pairs={{0,16},{8,120},{16,32},{24,8},{32,48},{40,24},{48,64},{56,40},{64,... | collective-permute-start | bytes 2359304 | tf_op jit(solution)/shard_map/ppermute | solution.py:300
  67.3 13.1 %collective-permute-start.11 = (bf16[384,512]{1,0:T(8,128)(2,1)S(1)}, bf16[384,512]{1,0:T(8,128)(2,1)S(1)}, u32[]{:S(2)}, u32[]{:S(2)}) collective-permute-start(bf16[384,512]{1,0:T(8,128)(2,1)S(1)} %slice.6), channel_id=1, source_target_pairs={{0,16},{8,120},{16,32},{24,8},{32,48},{40,24},{48,64},{56,40},{64,... | collective-permute-start | bytes 1179656 | tf_op jit(solution)/shard_map/ppermute | solution.py:300
  82.6 7.9 %collective-permute-start.12 = (bf16[384,512]{1,0:T(8,128)(2,1)S(1)}, bf16[384,512]{1,0:T(8,128)(2,1)S(1)}, u32[]{:S(2)}, u32[]{:S(2)}) collective-permute-start(bf16[384,512]{1,0:T(8,128)(2,1)S(1)} %slice.7), channel_id=1, source_target_pairs={{0,16},{8,120},{16,32},{24,8},{32,48},{40,24},{48,64},{56,40},{64,... | collective-permute-start | bytes 1179656 | tf_op jit(solution)/shard_map/ppermute | solution.py:300
  91.7 5.1 %collective-permute-start.13 = (bf16[768,256]{1,0:T(8,128)(2,1)S(1)}, bf16[768,256]{1,0:T(8,128)(2,1)S(1)}, u32[]{:S(2)}, u32[]{:S(2)}) collective-permute-start(bf16[768,256]{1,0:T(8,128)(2,1)S(1)} %get-tuple-element.55), channel_id=1, source_target_pairs={{0,8},{8,0},{1,9},{9,1},{2,10},{10,2},{3,11},{11,3},{4,12},{12,4},... | collective-permute-start | bytes 1179656 | tf_op jit(solution)/shard_map/ppermute | solution.py:302
  95.4 1.9 %collective-permute-start.14 = (f32[768,128]{1,0:T(8,128)S(1)}, f32[768,128]{1,0:T(8,128)S(1)}, u32[]{:S(2)}, u32[]{:S(2)}) collective-permute-start(f32[768,128]{1,0:T(8,128)S(1)} %get-tuple-element.56), channel_id=1, source_target_pairs={{0,8},{8,0},{1,9},{9,1},{2,10},{10,2},{3,11},{11,3},{4,12},{12,4},... | collective-permute-start | bytes 1179656 | tf_op jit(solution)/shard_map/ppermute | solution.py:302
  98.3 13.1 %collective-permute-start.15 = (bf16[384,256]{1,0:T(8,128)(2,1)S(1)}, bf16[384,256]{1,0:T(8,128)(2,1)S(1)}, u32[]{:S(2)}, u32[]{:S(2)}) collective-permute-start(bf16[384,256]{1,0:T(8,128)(2,1)S(1)} %get-tuple-element.58), channel_id=1, source_target_pairs={{0,128},{128,0},{1,129},{129,1},{2,130},{130,2},{3,131},{131,3},{4... | collective-permute-start | bytes 589832 | tf_op jit(solution)/shard_map/ppermute | solution.py:301
where the time goes:
time: 113 us
  starting transfers between devices  37 us (33%)
  Pallas kernels  32.4 us (29%)
  waiting for transfers between devices  27.3 us (24%)
  blocking collectives  13.1 us (12%)
    pallas_call x9, Pallas kernels, attend(): pl.pallas_call(functools.partial(attend_kernel, len(kvs), base, kind is n...  24.2 us
    ppermute x8, starting transfers between devices, on_device(): hop = lambda a: lax.ppermute(a, ('z', 'core'), hop_pairs)  23.5 us
    ppermute x8, waiting for transfers between devices, on_device(): hop = lambda a: lax.ppermute(a, ('z', 'core'), hop_pairs)  18.3 us
    all_to_all x1, blocking collectives, on_device(): squares = lax.all_to_all(squares, ('yh', 'yl', 'x'), 0, 0, tiled=True)  13.1 us
    ppermute x5, starting transfers between devices, on_device(): over_core = lambda a: lax.ppermute(a, 'core', SWAP)  7.22 us
    ppermute x3, waiting for transfers between devices, on_device(): over_y = lambda a: lax.ppermute(a, 'yh', SWAP)  6.82 us
    ppermute x3, starting transfers between devices, on_device(): over_y = lambda a: lax.ppermute(a, 'yh', SWAP)  6.21 us
    pallas_call x1, Pallas kernels, begin(): pl.pallas_call(begin_kernel, out_shape=[jax.ShapeDtypeStruct((rows, 5 * D...  3.74 us
  transfers between devices with their start and end apart: 16, of which 7 were waited for; matrix products, arithmetic and copies ran while one was open for 1% of the time, Pallas kernels for 24%

commit v1 on v0

--- a/solution.py
+++ b/solution.py
@@ -180,10 +180,8 @@
         stats[...] = jnp.where(lane == 0, top + jnp.log2(total), cross * (SCALE * inverse))
 
 
-def cost(rows, keys):
-    return pl.CostEstimate(
-        flops=2 * 8 * rows * keys * DH, bytes_accessed=keys * 4 * DH * 2, transcendentals=rows * keys
-    )
+def cost():
+    return pl.CostEstimate(flops=1024, bytes_accessed=1024, transcendentals=0)
 
 
 def begin(*arrays):
@@ -193,7 +191,7 @@
         out_shape=[jax.ShapeDtypeStruct((rows, 5 * DH), F32), jax.ShapeDtypeStruct((rows, 2 * DH), BF16)],
         scratch_shapes=[pltpu.VMEM((keys, 4 * DH), BF16)],
         compiler_params=PARAMS,
-        cost_estimate=cost(rows, keys),
+        cost_estimate=cost(),
         name="begin",
     )(*arrays)
 
@@ -213,7 +211,7 @@
         out_shape=shapes,
         scratch_shapes=scratch,
         compiler_params=PARAMS,
-        cost_estimate=cost(rows, keys),
+        cost_estimate=cost(),
         name="attend",
     )(query, *kvs, state)
 
@@ -304,33 +302,36 @@
         return lax.optimization_barrier((block, state))
 
     own_kv, own_q, other_kv, other_q = pack(q, k, v, qt, kt, vt)
-    peer_kv = over_y(other_kv)
-    other_q, peer_kv = after(other_q, peer_kv)
-    peer_q = over_y(other_q)
-    near = hop(jnp.concatenate([own_kv, over_core(own_kv)], axis=0))
-    far = hop(jnp.concatenate([peer_kv, over_core(peer_kv)], axis=0))
-    near_next = hop(near)
+    peer_q, peer_kv = over_y(other_q), over_y(other_kv)
+    core_kv = over_core(own_kv)
+    near = [hop(own_kv), hop(core_kv)]
+    near[0], near[1], peer_kv, peer_q = lax.optimization_barrier((near[0], near[1], peer_kv, peer_q))
+    far = [hop(peer_kv), hop(over_core(peer_kv))]
+    near_next = [hop(a) for a in near]
     pair_q = jnp.concatenate([own_q, peer_q], axis=0)
     state, query = begin(own_kv, peer_kv, pair_q, over_core(pair_q))
-    near_two, state = after(near_next, state)
-    near_next = hop(near_two)
-    state = attend(query, [near], state)
-    state = attend(query, [near_two], state)
-    far, state = after(far, state)
-    far_next = hop(far)
-    state = attend(query, [far], state)
-    near, state = after(near_next, state)
-    part, state = after(near[:tokens], state)
-    last_near = hop(part)
-    state = attend(query, [near], state)
-    far, state = after(far_next, state)
-    far_next = hop(far)
-    state = attend(query, [far], state)
-    last_near, state = after(last_near, state)
-    state = attend(query, [last_near], state)
-    far, state = after(far_next, state)
-    far_next = hop(far[:tokens])
-    state = attend(query, [far], state)
+
+    def turn(pair, state, count):
+        sent, kept = [], []
+        for i, block in enumerate(pair):
+            block, state = after(block, state)
+            kept.append(block)
+            if i < count:
+                sent.append(hop(block))
+        return kept, sent, state
+
+    near_two, near_three, state = turn(near_next, state, 2)
+    state = attend(query, near, state)
+    state = attend(query, near_two, state)
+    far, far_next, state = turn(far, state, 2)
+    state = attend(query, far, state)
+    near, near_last, state = turn(near_three, state, 1)
+    state = attend(query, near, state)
+    far, far_next, state = turn(far_next, state, 2)
+    state = attend(query, far, state)
+    far, far_last, state = turn(far_next, state, 1)
+    state = attend(query, near_last + far, state)
+    far_next = far_last[0]
     rows = query.shape[0]
     there, there_stat = attend(query, [far_next], state, (rows // 2, rows), BF16)
     come, come_stat = over_core(there), over_core(there_stat)

time: 113 us -> 102 us (0.903)
  waiting for transfers between devices: 27.3 us -> 20.6 us
  blocking collectives: 13.1 us -> 10.9 us
  starting transfers between devices: 37 us -> 35.1 us
    ppermute x8 -> x14, waiting for transfers between devices: 18.3 us -> 11.7 us  [on_device(): hop = lambda a: lax.ppermute(a, ('z', 'core'), hop_pairs)]
    all_to_all x1, blocking collectives: 13.1 us -> 10.9 us  [on_device(): squares = lax.all_to_all(squares, ('yh', 'yl', 'x'), 0, 0, tiled=True)]
    ppermute x5, waiting for transfers between devices: 2.15 us -> 0.6 us  [on_device(): over_core = lambda a: lax.ppermute(a, 'core', SWAP)]
    ppermute x8 -> x14, starting transfers between devices: 23.5 us -> 22 us  [on_device(): hop = lambda a: lax.ppermute(a, ('z', 'core'), hop_pairs)]
    ppermute x3, waiting for transfers between devices: 6.82 us -> 8.25 us  [on_device(): over_y = lambda a: lax.ppermute(a, 'yh', SWAP)]
    pallas_call x9 -> x8, Pallas kernels: 24.2 us -> 24.4 us  [attend(): pl.pallas_call(functools.partial(attend_kernel, len(kvs), base, kind is n...]
  transfers between devices with their start and end apart: 16 -> 22, of which waited for: 7 -> 8; matrix products, arithmetic and copies ran while one was open for 1% -> 1% of each run, Pallas kernels for 24% -> 26%
where the time goes in v1:
time: 102 us
  starting transfers between devices  35.1 us (34%)
  Pallas kernels  32.6 us (32%)
  waiting for transfers between devices  20.6 us (20%)
  blocking collectives  10.9 us (11%)
  local copies, waits for them, and re-layouts  1.95 us (2%)
    pallas_call x8, Pallas kernels, attend(): pl.pallas_call(functools.partial(attend_kernel, len(kvs), base, kind is n...  24.4 us
    ppermute x14, starting transfers between devices, on_device(): hop = lambda a: lax.ppermute(a, ('z', 'core'), hop_pairs)  22 us
    ppermute x14, waiting for transfers between devices, on_device(): hop = lambda a: lax.ppermute(a, ('z', 'core'), hop_pairs)  11.7 us
    all_to_all x1, blocking collectives, on_device(): squares = lax.all_to_all(squares, ('yh', 'yl', 'x'), 0, 0, tiled=True)  10.9 us
    ppermute x3, waiting for transfers between devices, on_device(): over_y = lambda a: lax.ppermute(a, 'yh', SWAP)  8.25 us
    ppermute x3, starting transfers between devices, on_device(): over_y = lambda a: lax.ppermute(a, 'yh', SWAP)  6.67 us
    ppermute x5, starting transfers between devices, on_device(): over_core = lambda a: lax.ppermute(a, 'core', SWAP)  6.36 us
    pallas_call x1, Pallas kernels, begin(): pl.pallas_call(begin_kernel, out_shape=[jax.ShapeDtypeStruct((rows, 5 * D...  3.73 us
  transfers between devices with their start and end apart: 22, of which 8 were waited for; matrix products, arithmetic and copies ran while one was open for 1% of the time, Pallas kernels for 26%

profile of v1, /device:TPU:1, one launch (start us, length us, event | category | flops | bytes accessed | tf_op | source)
XLA Modules:
  0.0 101.9 jit_solution(1939474850871649352)
XLA Ops:
  0.6 2.3 %pack.1 = (bf16[384,512]{1,0:T(8,128)(2,1)}, bf16[384,256]{1,0:T(8,128)(2,1)}, bf16[384,512]{1,0:T(8,128)(2,1)}, bf16[384,256]{1,0:T(8,128)(2,1)}) custom-call(bf16[384,256]{1,0:T(8,128)(2,1)} %q.1, bf16[384,256]{1,0:T(8,128)(2,1)} %k.1, bf16[384,256]{1,0:T(8,128)(2,1)} %v.1, bf16[384,256]{1,0:T(8,128)(2,1)} %qt.1, bf16[384,256]{1,0:T(8,128)(2,1)} %kt.1, ...), custom_call_target="tpu_custom_call" | custom-call | bytes 2359296 | tf_op jit(solution)/shard_map/pack/pallas_call | solution.py:47
  2.9 3.3 %collective-permute-start.1 = (bf16[384,512]{1,0:T(8,128)(2,1)}, bf16[384,512]{1,0:T(8,128)(2,1)S(1)}, u32[]{:S(2)}, u32[]{:S(2)}) collective-permute-start(bf16[384,512]{1,0:T(8,128)(2,1)} %get-tuple-element.39.own_kv), channel_id=1, source_target_pairs={{0,8},{8,0},{1,9},{9,1},{2,10},{10,2},{3,11},{11,3},{4,12},{12,4},... | collective-permute-start | bytes 1179656 | tf_op jit(solution)/shard_map/ppermute | solution.py:300
  6.2 3.8 %collective-permute-start = (bf16[384,512]{1,0:T(8,128)(2,1)}, bf16[384,512]{1,0:T(8,128)(2,1)S(1)}, u32[]{:S(2)}, u32[]{:S(2)}) collective-permute-start(bf16[384,512]{1,0:T(8,128)(2,1)} %get-tuple-element.39.own_kv), channel_id=1, source_target_pairs={{0,16},{8,120},{16,32},{24,8},{32,48},{40,24},{48,64},{56,40},{64,... | collective-permute-start | bytes 1179656 | tf_op jit(solution)/shard_map/ppermute | solution.py:298
  10.1 2.9 %collective-permute-start.3 = (bf16[384,512]{1,0:T(8,128)(2,1)}, bf16[384,512]{1,0:T(8,128)(2,1)S(1)}, u32[]{:S(2)}, u32[]{:S(2)}) collective-permute-start(bf16[384,512]{1,0:T(8,128)(2,1)} %get-tuple-element.40), channel_id=1, source_target_pairs={{0,128},{128,0},{1,129},{129,1},{2,130},{130,2},{3,131},{131,3},{4... | collective-permute-start | bytes 1179656 | tf_op jit(solution)/shard_map/ppermute | solution.py:299
  13.0 0.0 collective-permute-done.1
  13.0 0.7 collective-permute-start.2
  13.7 0.8 collective-permute-start.4
  14.5 0.9 constant_dynamic-update-slice_fusion.1
  15.5 8.2 %collective-permute-done.4 = bf16[384,256]{1,0:T(8,128)(2,1)S(1)} collective-permute-done((bf16[384,256]{1,0:T(8,128)(2,1)}, bf16[384,256]{1,0:T(8,128)(2,1)S(1)}, u32[]{:S(2)}, u32[]{:S(2)}) %collective-permute-start.4) | collective-permute-done | bytes 196640 | tf_op jit(solution)/shard_map/ppermute | solution.py:299
  23.7 0.0 collective-permute-done.refs_0_
  23.7 0.0 collective-permute-done.3.peer_kv
  23.7 0.0 collective-permute-done.2.refs_1_
  23.8 0.1 collective-permute-start.5
  23.9 0.5 collective-permute-start.11
  24.4 4.0 %collective-permute-start.7 = (bf16[384,512]{1,0:T(8,128)(2,1)S(1)}, bf16[384,512]{1,0:T(8,128)(2,1)S(1)}, u32[]{:S(2)}, u32[]{:S(2)}) collective-permute-start(bf16[384,512]{1,0:T(8,128)(2,1)S(1)} %collective-permute-done.refs_0_), channel_id=1, source_target_pairs={{0,16},{8,120},{16,32},{24,8},{32,48},{40,24},{48,64},{56,40},{64,... | collective-permute-start | bytes 1179656 | tf_op jit(solution)/shard_map/ppermute | solution.py:298
  28.3 0.9 collective-permute-start.8
  29.2 0.7 collective-permute-start.6
  29.9 0.0 collective-permute-done.5.core_q
  29.9 0.0 copy-start
  29.9 1.0 copy-done
  30.9 3.7 %begin.1 = (f32[1536,640]{1,0:T(8,128)S(1)}, bf16[1536,256]{1,0:T(8,128)(2,1)S(1)}) custom-call(bf16[384,512]{1,0:T(8,128)(2,1)S(1)} %copy-done, bf16[384,512]{1,0:T(8,128)(2,1)S(1)} %collective-permute-done.3.peer_kv, bf16[768,256]{1,0:T(8,128)(2,1)S(1)} %constant_dynamic-update-slice_fusion.own_q, bf16[768,256]{1,0:T(8,128)(2,1)S(1)} %collective-permute-done.5.core_q), custom_call_target="tpu_custom_call" | custom-call | flops 1024 | bytes 1024 | tf_op jit(solution)/shard_map/begin/pallas_call | solution.py:189
  34.7 0.0 collective-permute-done.11
  34.7 0.1 collective-permute-start.12
  34.8 0.0 collective-permute-done.7.refs_0_
  34.8 2.4 %collective-permute-done.8.refs_1_ = bf16[384,512]{1,0:T(8,128)(2,1)S(1)} collective-permute-done((bf16[384,512]{1,0:T(8,128)(2,1)S(1)}, bf16[384,512]{1,0:T(8,128)(2,1)S(1)}, u32[]{:S(2)}, u32[]{:S(2)}) %collective-permute-start.8) | collective-permute-done | bytes 393248 | tf_op jit(solution)/shard_map/ppermute | solution.py:298
  37.3 3.1 %collective-permute-start.10 = (bf16[384,512]{1,0:T(8,128)(2,1)S(1)}, bf16[384,512]{1,0:T(8,128)(2,1)S(1)}, u32[]{:S(2)}, u32[]{:S(2)}) collective-permute-start(bf16[384,512]{1,0:T(8,128)(2,1)S(1)} %collective-permute-done.7.refs_0_), channel_id=1, source_target_pairs={{0,16},{8,120},{16,32},{24,8},{32,48},{40,24},{48,64},{56,40},{64,... | collective-permute-start | bytes 1179656 | tf_op jit(solution)/shard_map/ppermute | solution.py:298
  40.4 0.0 collective-permute-start.13
  40.4 3.5 %attend.8.refs_2_ = f32[1536,640]{1,0:T(8,128)S(1)} custom-call(bf16[1536,256]{1,0:T(8,128)(2,1)S(1)} %get-tuple-element.45.q_ref, bf16[384,512]{1,0:T(8,128)(2,1)S(1)} %collective-permute-done.refs_0_, bf16[384,512]{1,0:T(8,128)(2,1)S(1)} %collective-permute-done.2.refs_1_, f32[1536,640]{1,0:T(8,128)S(1)} %get-tuple-element.52.refs_2_), custom_call_target="tpu_custom_call" | custom-call | flops 1024 | bytes 1024 | tf_op jit(solution)/shard_map/attend/pallas_call | solution.py:209
  43.9 3.3 %attend.9.refs_2_ = f32[1536,640]{1,0:T(8,128)S(1)} custom-call(bf16[1536,256]{1,0:T(8,128)(2,1)S(1)} %get-tuple-element.45.q_ref, bf16[384,512]{1,0:T(8,128)(2,1)S(1)} %collective-permute-done.7.refs_0_, bf16[384,512]{1,0:T(8,128)(2,1)S(1)} %collective-permute-done.8.refs_1_, f32[1536,640]{1,0:T(8,128)S(1)} %attend.8.refs_2_), custom_call_target="tpu_custom_call" | custom-call | flops 1024 | bytes 1024 | tf_op jit(solution)/shard_map/attend/pallas_call | solution.py:209
  47.3 0.0 collective-permute-done.6.refs_0_
  47.3 0.7 collective-permute-start.9
  48.0 0.0 collective-permute-done.12.refs_1_
  48.0 0.8 collective-permute-start.15
  48.8 3.3 %attend.10.refs_2_ = f32[1536,640]{1,0:T(8,128)S(1)} custom-call(bf16[1536,256]{1,0:T(8,128)(2,1)S(1)} %get-tuple-element.45.q_ref, bf16[384,512]{1,0:T(8,128)(2,1)S(1)} %collective-permute-done.6.refs_0_, bf16[384,512]{1,0:T(8,128)(2,1)S(1)} %collective-permute-done.12.refs_1_, f32[1536,640]{1,0:T(8,128)S(1)} %attend.9.refs_2_), custom_call_target="tpu_custom_call" | custom-call | flops 1024 | bytes 1024 | tf_op jit(solution)/shard_map/attend/pallas_call | solution.py:209
  52.1 0.0 collective-permute-done.10.refs_0_
  52.1 2.0 %collective-permute-done.13.refs_1_ = bf16[384,512]{1,0:T(8,128)(2,1)S(1)} collective-permute-done((bf16[384,512]{1,0:T(8,128)(2,1)S(1)}, bf16[384,512]{1,0:T(8,128)(2,1)S(1)}, u32[]{:S(2)}, u32[]{:S(2)}) %collective-permute-start.13) | collective-permute-done | bytes 393248 | tf_op jit(solution)/shard_map/ppermute | solution.py:298
  54.1 3.3 %attend.11.refs_2_ = f32[1536,640]{1,0:T(8,128)S(1)} custom-call(bf16[1536,256]{1,0:T(8,128)(2,1)S(1)} %get-tuple-element.45.q_ref, bf16[384,512]{1,0:T(8,128)(2,1)S(1)} %collective-permute-done.10.refs_0_, bf16[384,512]{1,0:T(8,128)(2,1)S(1)} %collective-permute-done.13.refs_1_, f32[1536,640]{1,0:T(8,128)S(1)} %attend.10.refs_2_), custom_call_target="tpu_custom_call" | custom-call | flops 1024 | bytes 1024 | tf_op jit(solution)/shard_map/attend/pallas_call | solution.py:209
  57.4 0.9 collective-permute-done.9.refs_0_
  58.3 3.1 %collective-permute-start.14 = (bf16[384,512]{1,0:T(8,128)(2,1)S(1)}, bf16[384,512]{1,0:T(8,128)(2,1)S(1)}, u32[]{:S(2)}, u32[]{:S(2)}) collective-permute-start(bf16[384,512]{1,0:T(8,128)(2,1)S(1)} %collective-permute-done.9.refs_0_), channel_id=1, source_target_pairs={{0,16},{8,120},{16,32},{24,8},{32,48},{40,24},{48,64},{56,40},{64,... | collective-permute-start | bytes 1179656 | tf_op jit(solution)/shard_map/ppermute | solution.py:298
  61.4 1.1 %collective-permute-done.15.refs_1_ = bf16[384,512]{1,0:T(8,128)(2,1)S(1)} collective-permute-done((bf16[384,512]{1,0:T(8,128)(2,1)S(1)}, bf16[384,512]{1,0:T(8,128)(2,1)S(1)}, u32[]{:S(2)}, u32[]{:S(2)}) %collective-permute-start.15) | collective-permute-done | bytes 393248 | tf_op jit(solution)/shard_map/ppermute | solution.py:298
  62.5 3.1 %collective-permute-start.18 = (bf16[384,512]{1,0:T(8,128)(2,1)S(1)}, bf16[384,512]{1,0:T(8,128)(2,1)S(1)}, u32[]{:S(2)}, u32[]{:S(2)}) collective-permute-start(bf16[384,512]{1,0:T(8,128)(2,1)S(1)} %collective-permute-done.15.refs_1_), channel_id=1, source_target_pairs={{0,16},{8,120},{16,32},{24,8},{32,48},{40,24},{48,64},{56,40},{64,... | collective-permute-start | bytes 1179656 | tf_op jit(solution)/shard_map/ppermute | solution.py:298
  65.7 0.0 collective-permute-start.17
  65.7 3.3 %attend.12.refs_3_ = f32[1536,640]{1,0:T(8,128)S(1)} custom-call(bf16[1536,256]{1,0:T(8,128)(2,1)S(1)} %get-tuple-element.45.q_ref, bf16[384,512]{1,0:T(8,128)(2,1)S(1)} %collective-permute-done.9.refs_0_, bf16[384,512]{1,0:T(8,128)(2,1)S(1)} %collective-permute-done.15.refs_1_, f32[1536,640]{1,0:T(8,128)S(1)} %attend.11.refs_2_), custom_call_target="tpu_custom_call" | custom-call | flops 1024 | bytes 1024 | tf_op jit(solution)/shard_map/attend/pallas_call | solution.py:209
  69.0 0.0 collective-permute-done.14.refs_1_
  69.0 0.8 collective-permute-start.16
  69.9 1.1 %collective-permute-done.18.refs_2_ = bf16[384,512]{1,0:T(8,128)(2,1)S(1)} collective-permute-done((bf16[384,512]{1,0:T(8,128)(2,1)S(1)}, bf16[384,512]{1,0:T(8,128)(2,1)S(1)}, u32[]{:S(2)}, u32[]{:S(2)}) %collective-permute-start.18) | collective-permute-done | bytes 393248 | tf_op jit(solution)/shard_map/ppermute | solution.py:298
  71.0 4.2 %collective-permute-done.17.refs_0_ = bf16[384,512]{1,0:T(8,128)(2,1)S(1)} collective-permute-done((bf16[384,512]{1,0:T(8,128)(2,1)S(1)}, bf16[384,512]{1,0:T(8,128)(2,1)S(1)}, u32[]{:S(2)}, u32[]{:S(2)}) %collective-permute-start.17) | collective-permute-done | bytes 393248 | tf_op jit(solution)/shard_map/ppermute | solution.py:298
  75.2 5.2 %attend.13.refs_1_ = f32[1536,640]{1,0:T(8,128)S(1)} custom-call(bf16[1536,256]{1,0:T(8,128)(2,1)S(1)} %get-tuple-element.45.q_ref, bf16[384,512]{1,0:T(8,128)(2,1)S(1)} %collective-permute-done.17.refs_0_, bf16[384,512]{1,0:T(8,128)(2,1)S(1)} %collective-permute-done.14.refs_1_, bf16[384,512]{1,0:T(8,128)(2,1)S(1)} %collective-permute-done.18.refs_2_, ...), custom_call_target="tpu_custom_call" | custom-call | flops 1024 | bytes 1024 | tf_op jit(solution)/shard_map/attend/pallas_call | solution.py:209
  80.4 0.0 collective-permute-done.16.refs_0_
  80.4 1.2 %attend.15 = (bf16[768,256]{1,0:T(8,128)(2,1)S(1)}, f32[768,128]{1,0:T(8,128)S(1)}) custom-call(bf16[1536,256]{1,0:T(8,128)(2,1)S(1)} %get-tuple-element.45.q_ref, bf16[384,512]{1,0:T(8,128)(2,1)S(1)} %collective-permute-done.16.refs_0_, f32[1536,640]{1,0:T(8,128)S(1)} %attend.13.refs_1_), custom_call_target="tpu_custom_call" | custom-call | flops 1024 | bytes 1024 | tf_op jit(solution)/shard_map/attend/pallas_call | solution.py:209
  81.6 2.4 %collective-permute-start.19 = (bf16[768,256]{1,0:T(8,128)(2,1)S(1)}, bf16[768,256]{1,0:T(8,128)(2,1)S(1)}, u32[]{:S(2)}, u32[]{:S(2)}) collective-permute-start(bf16[768,256]{1,0:T(8,128)(2,1)S(1)} %get-tuple-element.71), channel_id=1, source_target_pairs={{0,8},{8,0},{1,9},{9,1},{2,10},{10,2},{3,11},{11,3},{4,12},{12,4},... | collective-permute-start | bytes 1179656 | tf_op jit(solution)/shard_map/ppermute | solution.py:300
  84.0 0.1 collective-permute-start.20
  84.1 1.2 %attend.14 = (f32[768,256]{1,0:T(8,128)S(1)}, f32[768,128]{1,0:T(8,128)S(1)}) custom-call(bf16[1536,256]{1,0:T(8,128)(2,1)S(1)} %get-tuple-element.45.q_ref, bf16[384,512]{1,0:T(8,128)(2,1)S(1)} %collective-permute-done.16.refs_0_, f32[1536,640]{1,0:T(8,128)S(1)} %attend.13.refs_1_), custom_call_target="tpu_custom_call" | custom-call | flops 1024 | bytes 1024 | tf_op jit(solution)/shard_map/attend/pallas_call | solution.py:209
  85.3 0.0 collective-permute-done.19.other
  85.3 0.6 collective-permute-done.20.other_stat
  85.9 1.0 join.1
  86.9 2.9 %collective-permute-start.21 = (bf16[384,256]{1,0:T(8,128)(2,1)S(1)}, bf16[384,256]{1,0:T(8,128)(2,1)S(1)}, u32[]{:S(2)}, u32[]{:S(2)}) collective-permute-start(bf16[384,256]{1,0:T(8,128)(2,1)S(1)} %get-tuple-element.74), channel_id=1, source_target_pairs={{0,128},{128,0},{1,129},{129,1},{2,130},{130,2},{3,131},{131,3},{4... | collective-permute-start | bytes 589832 | tf_op jit(solution)/shard_map/ppermute | solution.py:299
  89.8 10.9 %all_to_all.5.squares = f32[16,8,128]{2,1,0:T(8,128)S(1)} all-to-all(f32[16,8,128]{2,1,0:T(8,128)S(1)} %get-tuple-element.75), channel_id=1, replica_groups=mesh['yh'=2,'z'=8,'core'=2,'yl'=2,'x'=4] {'yh','yl','x'}, dimensions={0} | all-to-all | bytes 131072 | tf_op jit(solution)/shard_map/all_to_all | solution.py:341
  100.7 0.0 collective-permute-done.21.come
  100.7 1.2 %finish.1 = (bf16[384,256]{1,0:T(8,128)(2,1)}, bf16[384,256]{1,0:T(8,128)(2,1)}) custom-call(f32[384,256]{1,0:T(8,128)S(1)} %get-tuple-element.73.keep, bf16[384,256]{1,0:T(8,128)(2,1)S(1)} %collective-permute-done.21.come, f32[16,8,128]{2,1,0:T(8,128)S(1)} %all_to_all.5.squares), custom_call_target="tpu_custom_call" | custom-call | tf_op jit(solution)/shard_map/finish/pallas_call | solution.py:292
  (1 shorter events, 0.0 us)
Async XLA Ops:
  2.9 10.1 %collective-permute-start.1 = (bf16[384,512]{1,0:T(8,128)(2,1)}, bf16[384,512]{1,0:T(8,128)(2,1)S(1)}, u32[]{:S(2)}, u32[]{:S(2)}) collective-permute-start(bf16[384,512]{1,0:T(8,128)(2,1)} %get-tuple-element.39.own_kv), channel_id=1, source_target_pairs={{0,8},{8,0},{1,9},{9,1},{2,10},{10,2},{3,11},{11,3},{4,12},{12,4},... | collective-permute-start | bytes 1179656 | tf_op jit(solution)/shard_map/ppermute | solution.py:300
  6.2 17.5 %collective-permute-start = (bf16[384,512]{1,0:T(8,128)(2,1)}, bf16[384,512]{1,0:T(8,128)(2,1)S(1)}, u32[]{:S(2)}, u32[]{:S(2)}) collective-permute-start(bf16[384,512]{1,0:T(8,128)(2,1)} %get-tuple-element.39.own_kv), channel_id=1, source_target_pairs={{0,16},{8,120},{16,32},{24,8},{32,48},{40,24},{48,64},{56,40},{64,... | collective-permute-start | bytes 1179656 | tf_op jit(solution)/shard_map/ppermute | solution.py:298
  10.1 13.7 %collective-permute-start.3 = (bf16[384,512]{1,0:T(8,128)(2,1)}, bf16[384,512]{1,0:T(8,128)(2,1)S(1)}, u32[]{:S(2)}, u32[]{:S(2)}) collective-permute-start(bf16[384,512]{1,0:T(8,128)(2,1)} %get-tuple-element.40), channel_id=1, source_target_pairs={{0,128},{128,0},{1,129},{129,1},{2,130},{130,2},{3,131},{131,3},{4... | collective-permute-start | bytes 1179656 | tf_op jit(solution)/shard_map/ppermute | solution.py:299
  13.0 10.8 %collective-permute-start.2 = (bf16[384,512]{1,0:T(8,128)(2,1)S(1)}, bf16[384,512]{1,0:T(8,128)(2,1)S(1)}, u32[]{:S(2)}, u32[]{:S(2)}) collective-permute-start(bf16[384,512]{1,0:T(8,128)(2,1)S(1)} %collective-permute-done.1), channel_id=1, source_target_pairs={{0,16},{8,120},{16,32},{24,8},{32,48},{40,24},{48,64},{56,40},{64,... | collective-permute-start | bytes 1179656 | tf_op jit(solution)/shard_map/ppermute | solution.py:298
  13.7 10.0 %collective-permute-start.4 = (bf16[384,256]{1,0:T(8,128)(2,1)}, bf16[384,256]{1,0:T(8,128)(2,1)S(1)}, u32[]{:S(2)}, u32[]{:S(2)}) collective-permute-start(bf16[384,256]{1,0:T(8,128)(2,1)} %get-tuple-element.41), channel_id=1, source_target_pairs={{0,128},{128,0},{1,129},{129,1},{2,130},{130,2},{3,131},{131,3},{4... | collective-permute-start | bytes 589832 | tf_op jit(solution)/shard_map/ppermute | solution.py:299
  23.8 6.2 %collective-permute-start.5 = (bf16[768,256]{1,0:T(8,128)(2,1)S(1)}, bf16[768,256]{1,0:T(8,128)(2,1)S(1)}, u32[]{:S(2)}, u32[]{:S(2)}) collective-permute-start(bf16[768,256]{1,0:T(8,128)(2,1)S(1)} %constant_dynamic-update-slice_fusion.own_q), channel_id=1, source_target_pairs={{0,8},{8,0},{1,9},{9,1},{2,10},{10,2},{3,11},{11,3},{4,12},{12,4},... | collective-permute-start | bytes 1179656 | tf_op jit(solution)/shard_map/ppermute | solution.py:300
  23.9 10.8 %collective-permute-start.11 = (bf16[384,512]{1,0:T(8,128)(2,1)S(1)}, bf16[384,512]{1,0:T(8,128)(2,1)S(1)}, u32[]{:S(2)}, u32[]{:S(2)}) collective-permute-start(bf16[384,512]{1,0:T(8,128)(2,1)S(1)} %collective-permute-done.3.peer_kv), channel_id=1, source_target_pairs={{0,8},{8,0},{1,9},{9,1},{2,10},{10,2},{3,11},{11,3},{4,12},{12,4},... | collective-permute-start | bytes 1179656 | tf_op jit(solution)/shard_map/ppermute | solution.py:300
  24.4 10.5 %collective-permute-start.7 = (bf16[384,512]{1,0:T(8,128)(2,1)S(1)}, bf16[384,512]{1,0:T(8,128)(2,1)S(1)}, u32[]{:S(2)}, u32[]{:S(2)}) collective-permute-start(bf16[384,512]{1,0:T(8,128)(2,1)S(1)} %collective-permute-done.refs_0_), channel_id=1, source_target_pairs={{0,16},{8,120},{16,32},{24,8},{32,48},{40,24},{48,64},{56,40},{64,... | collective-permute-start | bytes 1179656 | tf_op jit(solution)/shard_map/ppermute | solution.py:298
  28.3 8.9 %collective-permute-start.8 = (bf16[384,512]{1,0:T(8,128)(2,1)S(1)}, bf16[384,512]{1,0:T(8,128)(2,1)S(1)}, u32[]{:S(2)}, u32[]{:S(2)}) collective-permute-start(bf16[384,512]{1,0:T(8,128)(2,1)S(1)} %collective-permute-done.2.refs_1_), channel_id=1, source_target_pairs={{0,16},{8,120},{16,32},{24,8},{32,48},{40,24},{48,64},{56,40},{64,... | collective-permute-start | bytes 1179656 | tf_op jit(solution)/shard_map/ppermute | solution.py:298
  29.2 18.1 %collective-permute-start.6 = (bf16[384,512]{1,0:T(8,128)(2,1)S(1)}, bf16[384,512]{1,0:T(8,128)(2,1)S(1)}, u32[]{:S(2)}, u32[]{:S(2)}) collective-permute-start(bf16[384,512]{1,0:T(8,128)(2,1)S(1)} %collective-permute-done.3.peer_kv), channel_id=1, source_target_pairs={{0,16},{8,120},{16,32},{24,8},{32,48},{40,24},{48,64},{56,40},{64,... | collective-permute-start | bytes 1179656 | tf_op jit(solution)/shard_map/ppermute | solution.py:298
  29.9 1.0 copy-start
  34.7 13.3 %collective-permute-start.12 = (bf16[384,512]{1,0:T(8,128)(2,1)S(1)}, bf16[384,512]{1,0:T(8,128)(2,1)S(1)}, u32[]{:S(2)}, u32[]{:S(2)}) collective-permute-start(bf16[384,512]{1,0:T(8,128)(2,1)S(1)} %collective-permute-done.11), channel_id=1, source_target_pairs={{0,16},{8,120},{16,32},{24,8},{32,48},{40,24},{48,64},{56,40},{64,... | collective-permute-start | bytes 1179656 | tf_op jit(solution)/shard_map/ppermute | solution.py:298
  37.3 14.9 %collective-permute-start.10 = (bf16[384,512]{1,0:T(8,128)(2,1)S(1)}, bf16[384,512]{1,0:T(8,128)(2,1)S(1)}, u32[]{:S(2)}, u32[]{:S(2)}) collective-permute-start(bf16[384,512]{1,0:T(8,128)(2,1)S(1)} %collective-permute-done.7.refs_0_), channel_id=1, source_target_pairs={{0,16},{8,120},{16,32},{24,8},{32,48},{40,24},{48,64},{56,40},{64,... | collective-permute-start | bytes 1179656 | tf_op jit(solution)/shard_map/ppermute | solution.py:298
  40.4 13.7 %collective-permute-start.13 = (bf16[384,512]{1,0:T(8,128)(2,1)S(1)}, bf16[384,512]{1,0:T(8,128)(2,1)S(1)}, u32[]{:S(2)}, u32[]{:S(2)}) collective-permute-start(bf16[384,512]{1,0:T(8,128)(2,1)S(1)} %collective-permute-done.8.refs_1_), channel_id=1, source_target_pairs={{0,16},{8,120},{16,32},{24,8},{32,48},{40,24},{48,64},{56,40},{64,... | collective-permute-start | bytes 1179656 | tf_op jit(solution)/shard_map/ppermute | solution.py:298
  47.3 11.1 %collective-permute-start.9 = (bf16[384,512]{1,0:T(8,128)(2,1)S(1)}, bf16[384,512]{1,0:T(8,128)(2,1)S(1)}, u32[]{:S(2)}, u32[]{:S(2)}) collective-permute-start(bf16[384,512]{1,0:T(8,128)(2,1)S(1)} %collective-permute-done.6.refs_0_), channel_id=1, source_target_pairs={{0,16},{8,120},{16,32},{24,8},{32,48},{40,24},{48,64},{56,40},{64,... | collective-permute-start | bytes 1179656 | tf_op jit(solution)/shard_map/ppermute | solution.py:298
  48.0 14.5 %collective-permute-start.15 = (bf16[384,512]{1,0:T(8,128)(2,1)S(1)}, bf16[384,512]{1,0:T(8,128)(2,1)S(1)}, u32[]{:S(2)}, u32[]{:S(2)}) collective-permute-start(bf16[384,512]{1,0:T(8,128)(2,1)S(1)} %collective-permute-done.12.refs_1_), channel_id=1, source_target_pairs={{0,16},{8,120},{16,32},{24,8},{32,48},{40,24},{48,64},{56,40},{64,... | collective-permute-start | bytes 1179656 | tf_op jit(solution)/shard_map/ppermute | solution.py:298
  58.3 10.7 %collective-permute-start.14 = (bf16[384,512]{1,0:T(8,128)(2,1)S(1)}, bf16[384,512]{1,0:T(8,128)(2,1)S(1)}, u32[]{:S(2)}, u32[]{:S(2)}) collective-permute-start(bf16[384,512]{1,0:T(8,128)(2,1)S(1)} %collective-permute-done.9.refs_0_), channel_id=1, source_target_pairs={{0,16},{8,120},{16,32},{24,8},{32,48},{40,24},{48,64},{56,40},{64,... | collective-permute-start | bytes 1179656 | tf_op jit(solution)/shard_map/ppermute | solution.py:298
  62.5 8.4 %collective-permute-start.18 = (bf16[384,512]{1,0:T(8,128)(2,1)S(1)}, bf16[384,512]{1,0:T(8,128)(2,1)S(1)}, u32[]{:S(2)}, u32[]{:S(2)}) collective-permute-start(bf16[384,512]{1,0:T(8,128)(2,1)S(1)} %collective-permute-done.15.refs_1_), channel_id=1, source_target_pairs={{0,16},{8,120},{16,32},{24,8},{32,48},{40,24},{48,64},{56,40},{64,... | collective-permute-start | bytes 1179656 | tf_op jit(solution)/shard_map/ppermute | solution.py:298
  65.7 9.5 %collective-permute-start.17 = (bf16[384,512]{1,0:T(8,128)(2,1)S(1)}, bf16[384,512]{1,0:T(8,128)(2,1)S(1)}, u32[]{:S(2)}, u32[]{:S(2)}) collective-permute-start(bf16[384,512]{1,0:T(8,128)(2,1)S(1)} %collective-permute-done.10.refs_0_), channel_id=1, source_target_pairs={{0,16},{8,120},{16,32},{24,8},{32,48},{40,24},{48,64},{56,40},{64,... | collective-permute-start | bytes 1179656 | tf_op jit(solution)/shard_map/ppermute | solution.py:298
  69.0 11.4 %collective-permute-start.16 = (bf16[384,512]{1,0:T(8,128)(2,1)S(1)}, bf16[384,512]{1,0:T(8,128)(2,1)S(1)}, u32[]{:S(2)}, u32[]{:S(2)}) collective-permute-start(bf16[384,512]{1,0:T(8,128)(2,1)S(1)} %collective-permute-done.14.refs_1_), channel_id=1, source_target_pairs={{0,16},{8,120},{16,32},{24,8},{32,48},{40,24},{48,64},{56,40},{64,... | collective-permute-start | bytes 1179656 | tf_op jit(solution)/shard_map/ppermute | solution.py:298
  81.6 3.7 %collective-permute-start.19 = (bf16[768,256]{1,0:T(8,128)(2,1)S(1)}, bf16[768,256]{1,0:T(8,128)(2,1)S(1)}, u32[]{:S(2)}, u32[]{:S(2)}) collective-permute-start(bf16[768,256]{1,0:T(8,128)(2,1)S(1)} %get-tuple-element.71), channel_id=1, source_target_pairs={{0,8},{8,0},{1,9},{9,1},{2,10},{10,2},{3,11},{11,3},{4,12},{12,4},... | collective-permute-start | bytes 1179656 | tf_op jit(solution)/shard_map/ppermute | solution.py:300
  84.0 1.9 %collective-permute-start.20 = (f32[768,128]{1,0:T(8,128)S(1)}, f32[768,128]{1,0:T(8,128)S(1)}, u32[]{:S(2)}, u32[]{:S(2)}) collective-permute-start(f32[768,128]{1,0:T(8,128)S(1)} %get-tuple-element.72), channel_id=1, source_target_pairs={{0,8},{8,0},{1,9},{9,1},{2,10},{10,2},{3,11},{11,3},{4,12},{12,4},... | collective-permute-start | bytes 1179656 | tf_op jit(solution)/shard_map/ppermute | solution.py:300
  86.9 13.9 %collective-permute-start.21 = (bf16[384,256]{1,0:T(8,128)(2,1)S(1)}, bf16[384,256]{1,0:T(8,128)(2,1)S(1)}, u32[]{:S(2)}, u32[]{:S(2)}) collective-permute-start(bf16[384,256]{1,0:T(8,128)(2,1)S(1)} %get-tuple-element.74), channel_id=1, source_target_pairs={{0,128},{128,0},{1,129},{129,1},{2,130},{130,2},{3,131},{131,3},{4... | collective-permute-start | bytes 589832 | tf_op jit(solution)/shard_map/ppermute | solution.py:299

commit v2 on v1

--- a/solution.py
+++ b/solution.py
@@ -305,9 +305,9 @@
     peer_q, peer_kv = over_y(other_q), over_y(other_kv)
     core_kv = over_core(own_kv)
     near = [hop(own_kv), hop(core_kv)]
-    near[0], near[1], peer_kv, peer_q = lax.optimization_barrier((near[0], near[1], peer_kv, peer_q))
+    near_next = [hop(a) for a in near]
+    near_next[0], near_next[1], peer_kv, peer_q = lax.optimization_barrier((*near_next, peer_kv, peer_q))
     far = [hop(peer_kv), hop(over_core(peer_kv))]
-    near_next = [hop(a) for a in near]
     pair_q = jnp.concatenate([own_q, peer_q], axis=0)
     state, query = begin(own_kv, peer_kv, pair_q, over_core(pair_q))
 
@@ -330,12 +330,12 @@
     far, far_next, state = turn(far_next, state, 2)
     state = attend(query, far, state)
     far, far_last, state = turn(far_next, state, 1)
-    state = attend(query, near_last + far, state)
-    far_next = far_last[0]
+    state = attend(query, far, state)
+    ends = near_last + far_last
     rows = query.shape[0]
-    there, there_stat = attend(query, [far_next], state, (rows // 2, rows), BF16)
+    there, there_stat = attend(query, ends, state, (rows // 2, rows), BF16)
     come, come_stat = over_core(there), over_core(there_stat)
-    here, here_stat = attend(query, [far_next], state, (0, rows // 2), F32)
+    here, here_stat = attend(query, ends, state, (0, rows // 2), F32)
     keep, send, squares = join(here, here_stat, come, come_stat)
     come = over_y(send)
     squares = lax.all_to_all(squares, ("yh", "yl", "x"), 0, 0, tiled=True)

time: 102 us -> 99.6 us (0.976)
  waiting for transfers between devices: 20.6 us -> 13.6 us
  starting transfers between devices: 35.1 us -> 39.9 us
    ppermute x3, waiting for transfers between devices: 8.25 us -> 3.1 us  [on_device(): over_y = lambda a: lax.ppermute(a, 'yh', SWAP)]
    ppermute x14, starting transfers between devices: 22 us -> 25.1 us  [on_device(): hop = lambda a: lax.ppermute(a, ('z', 'core'), hop_pairs)]
    ppermute x3, starting transfers between devices: 6.67 us -> 8.59 us  [on_device(): over_y = lambda a: lax.ppermute(a, 'yh', SWAP)]
    ppermute x14, waiting for transfers between devices: 11.7 us -> 10.5 us  [on_device(): hop = lambda a: lax.ppermute(a, ('z', 'core'), hop_pairs)]
where the time goes in v2:
time: 99.6 us; the launch traced here: 99.4 us
  starting transfers between devices  39.9 us (40%)
  Pallas kernels  32.2 us (32%)
  waiting for transfers between devices  13.6 us (14%)
  blocking collectives  10.9 us (11%)
  local copies, waits for them, and re-layouts  1.95 us (2%)
    ppermute x14, starting transfers between devices, on_device(): hop = lambda a: lax.ppermute(a, ('z', 'core'), hop_pairs)  25.1 us
    pallas_call x8, Pallas kernels, attend(): pl.pallas_call(functools.partial(attend_kernel, len(kvs), base, kind is n...  24 us
    all_to_all x1, blocking collectives, on_device(): squares = lax.all_to_all(squares, ('yh', 'yl', 'x'), 0, 0, tiled=True)  10.9 us
    ppermute x14, waiting for transfers between devices, on_device(): hop = lambda a: lax.ppermute(a, ('z', 'core'), hop_pairs)  10.5 us
    ppermute x3, starting transfers between devices, on_device(): over_y = lambda a: lax.ppermute(a, 'yh', SWAP)  8.59 us
    ppermute x5, starting transfers between devices, on_device(): over_core = lambda a: lax.ppermute(a, 'core', SWAP)  6.27 us
    pallas_call x1, Pallas kernels, begin(): pl.pallas_call(begin_kernel, out_shape=[jax.ShapeDtypeStruct((rows, 5 * D...  3.74 us
    ppermute x3, waiting for transfers between devices, on_device(): over_y = lambda a: lax.ppermute(a, 'yh', SWAP)  3.1 us
  transfers between devices with their start and end apart: 22, of which 8 were waited for; matrix products, arithmetic and copies ran while one was open for 1% of the time, Pallas kernels for 26%

profile of v2, /device:TPU:1, one launch (start us, length us, event | category | flops | bytes accessed | tf_op | source)
XLA Modules:
  0.0 99.4 jit_solution(2010989848874184901)
XLA Ops:
  0.6 2.3 %pack.1 = (bf16[384,512]{1,0:T(8,128)(2,1)}, bf16[384,256]{1,0:T(8,128)(2,1)}, bf16[384,512]{1,0:T(8,128)(2,1)}, bf16[384,256]{1,0:T(8,128)(2,1)}) custom-call(bf16[384,256]{1,0:T(8,128)(2,1)} %q.1, bf16[384,256]{1,0:T(8,128)(2,1)} %k.1, bf16[384,256]{1,0:T(8,128)(2,1)} %v.1, bf16[384,256]{1,0:T(8,128)(2,1)} %qt.1, bf16[384,256]{1,0:T(8,128)(2,1)} %kt.1, ...), custom_call_target="tpu_custom_call" | custom-call | bytes 2359296 | tf_op jit(solution)/shard_map/pack/pallas_call | solution.py:47
  2.9 3.3 %collective-permute-start.2 = (bf16[384,512]{1,0:T(8,128)(2,1)}, bf16[384,512]{1,0:T(8,128)(2,1)S(1)}, u32[]{:S(2)}, u32[]{:S(2)}) collective-permute-start(bf16[384,512]{1,0:T(8,128)(2,1)} %get-tuple-element.39.own_kv), channel_id=1, source_target_pairs={{0,8},{8,0},{1,9},{9,1},{2,10},{10,2},{3,11},{11,3},{4,12},{12,4},... | collective-permute-start | bytes 1179656 | tf_op jit(solution)/shard_map/ppermute | solution.py:300
  6.2 3.8 %collective-permute-start = (bf16[384,512]{1,0:T(8,128)(2,1)}, bf16[384,512]{1,0:T(8,128)(2,1)S(1)}, u32[]{:S(2)}, u32[]{:S(2)}) collective-permute-start(bf16[384,512]{1,0:T(8,128)(2,1)} %get-tuple-element.39.own_kv), channel_id=1, source_target_pairs={{0,16},{8,120},{16,32},{24,8},{32,48},{40,24},{48,64},{56,40},{64,... | collective-permute-start | bytes 1179656 | tf_op jit(solution)/shard_map/ppermute | solution.py:298
  10.1 0.0 collective-permute-done.2
  10.1 1.6 %collective-permute-start.3 = (bf16[384,512]{1,0:T(8,128)(2,1)S(1)}, bf16[384,512]{1,0:T(8,128)(2,1)S(1)}, u32[]{:S(2)}, u32[]{:S(2)}) collective-permute-start(bf16[384,512]{1,0:T(8,128)(2,1)S(1)} %collective-permute-done.2), channel_id=1, source_target_pairs={{0,16},{8,120},{16,32},{24,8},{32,48},{40,24},{48,64},{56,40},{64,... | collective-permute-start | bytes 1179656 | tf_op jit(solution)/shard_map/ppermute | solution.py:298
  11.6 2.9 %collective-permute-start.5 = (bf16[384,512]{1,0:T(8,128)(2,1)}, bf16[384,512]{1,0:T(8,128)(2,1)S(1)}, u32[]{:S(2)}, u32[]{:S(2)}) collective-permute-start(bf16[384,512]{1,0:T(8,128)(2,1)} %get-tuple-element.40), channel_id=1, source_target_pairs={{0,128},{128,0},{1,129},{129,1},{2,130},{130,2},{3,131},{131,3},{4... | collective-permute-start | bytes 1179656 | tf_op jit(solution)/shard_map/ppermute | solution.py:299
  14.5 0.6 collective-permute-done.refs_0_
  15.1 3.3 %collective-permute-start.1 = (bf16[384,512]{1,0:T(8,128)(2,1)S(1)}, bf16[384,512]{1,0:T(8,128)(2,1)S(1)}, u32[]{:S(2)}, u32[]{:S(2)}) collective-permute-start(bf16[384,512]{1,0:T(8,128)(2,1)S(1)} %collective-permute-done.refs_0_), channel_id=1, source_target_pairs={{0,16},{8,120},{16,32},{24,8},{32,48},{40,24},{48,64},{56,40},{64,... | collective-permute-start | bytes 1179656 | tf_op jit(solution)/shard_map/ppermute | solution.py:298
  18.4 0.8 collective-permute-done.3.refs_1_
  19.2 3.4 %collective-permute-start.4 = (bf16[384,512]{1,0:T(8,128)(2,1)S(1)}, bf16[384,512]{1,0:T(8,128)(2,1)S(1)}, u32[]{:S(2)}, u32[]{:S(2)}) collective-permute-start(bf16[384,512]{1,0:T(8,128)(2,1)S(1)} %collective-permute-done.3.refs_1_), channel_id=1, source_target_pairs={{0,16},{8,120},{16,32},{24,8},{32,48},{40,24},{48,64},{56,40},{64,... | collective-permute-start | bytes 1179656 | tf_op jit(solution)/shard_map/ppermute | solution.py:298
  22.6 2.8 %collective-permute-start.6 = (bf16[384,256]{1,0:T(8,128)(2,1)}, bf16[384,256]{1,0:T(8,128)(2,1)S(1)}, u32[]{:S(2)}, u32[]{:S(2)}) collective-permute-start(bf16[384,256]{1,0:T(8,128)(2,1)} %get-tuple-element.41), channel_id=1, source_target_pairs={{0,128},{128,0},{1,129},{129,1},{2,130},{130,2},{3,131},{131,3},{4... | collective-permute-start | bytes 589832 | tf_op jit(solution)/shard_map/ppermute | solution.py:299
  25.4 0.9 constant_dynamic-update-slice_fusion.1
  26.3 3.1 %collective-permute-done.6 = bf16[384,256]{1,0:T(8,128)(2,1)S(1)} collective-permute-done((bf16[384,256]{1,0:T(8,128)(2,1)}, bf16[384,256]{1,0:T(8,128)(2,1)S(1)}, u32[]{:S(2)}, u32[]{:S(2)}) %collective-permute-start.6) | collective-permute-done | bytes 196640 | tf_op jit(solution)/shard_map/ppermute | solution.py:299
  29.4 0.0 collective-permute-done.5.peer_kv
  29.4 0.0 collective-permute-done.1.refs_0_
  29.4 0.0 collective-permute-done.4.refs_1_
  29.4 0.2 collective-permute-start.7
  29.7 0.3 collective-permute-start.10
  30.0 1.8 %collective-permute-start.9 = (bf16[384,512]{1,0:T(8,128)(2,1)S(1)}, bf16[384,512]{1,0:T(8,128)(2,1)S(1)}, u32[]{:S(2)}, u32[]{:S(2)}) collective-permute-start(bf16[384,512]{1,0:T(8,128)(2,1)S(1)} %collective-permute-done.5.peer_kv), channel_id=1, source_target_pairs={{0,16},{8,120},{16,32},{24,8},{32,48},{40,24},{48,64},{56,40},{64,... | collective-permute-start | bytes 1179656 | tf_op jit(solution)/shard_map/ppermute | solution.py:298
  31.9 0.0 collective-permute-done.7.core_q
  31.9 0.0 copy-start
  31.9 1.0 %copy-done = bf16[384,512]{1,0:T(8,128)(2,1)S(1)} copy-done((bf16[384,512]{1,0:T(8,128)(2,1)S(1)}, bf16[384,512]{1,0:T(8,128)(2,1)}, u32[]{:S(2)}) %copy-start) | copy-done | bytes 393240
  32.9 3.7 %begin.1 = (f32[1536,640]{1,0:T(8,128)S(1)}, bf16[1536,256]{1,0:T(8,128)(2,1)S(1)}) custom-call(bf16[384,512]{1,0:T(8,128)(2,1)S(1)} %copy-done, bf16[384,512]{1,0:T(8,128)(2,1)S(1)} %collective-permute-done.5.peer_kv, bf16[768,256]{1,0:T(8,128)(2,1)S(1)} %constant_dynamic-update-slice_fusion.own_q, bf16[768,256]{1,0:T(8,128)(2,1)S(1)} %collective-permute-done.7.core_q), custom_call_target="tpu_custom_call" | custom-call | flops 1024 | bytes 1024 | tf_op jit(solution)/shard_map/begin/pallas_call | solution.py:189
  36.6 0.0 collective-permute-done.10
  36.6 1.3 %collective-permute-start.11 = (bf16[384,512]{1,0:T(8,128)(2,1)S(1)}, bf16[384,512]{1,0:T(8,128)(2,1)S(1)}, u32[]{:S(2)}, u32[]{:S(2)}) collective-permute-start(bf16[384,512]{1,0:T(8,128)(2,1)S(1)} %collective-permute-done.10), channel_id=1, source_target_pairs={{0,16},{8,120},{16,32},{24,8},{32,48},{40,24},{48,64},{56,40},{64,... | collective-permute-start | bytes 1179656 | tf_op jit(solution)/shard_map/ppermute | solution.py:298
  37.9 0.2 collective-permute-start.8
  38.2 1.6 %collective-permute-start.14 = (bf16[384,512]{1,0:T(8,128)(2,1)S(1)}, bf16[384,512]{1,0:T(8,128)(2,1)S(1)}, u32[]{:S(2)}, u32[]{:S(2)}) collective-permute-start(bf16[384,512]{1,0:T(8,128)(2,1)S(1)} %collective-permute-done.4.refs_1_), channel_id=1, source_target_pairs={{0,16},{8,120},{16,32},{24,8},{32,48},{40,24},{48,64},{56,40},{64,... | collective-permute-start | bytes 1179656 | tf_op jit(solution)/shard_map/ppermute | solution.py:298
  39.8 3.5 %attend.8.refs_2_ = f32[1536,640]{1,0:T(8,128)S(1)} custom-call(bf16[1536,256]{1,0:T(8,128)(2,1)S(1)} %get-tuple-element.45.q_ref, bf16[384,512]{1,0:T(8,128)(2,1)S(1)} %collective-permute-done.refs_0_, bf16[384,512]{1,0:T(8,128)(2,1)S(1)} %collective-permute-done.3.refs_1_, f32[1536,640]{1,0:T(8,128)S(1)} %get-tuple-element.52.refs_2_), custom_call_target="tpu_custom_call" | custom-call | flops 1024 | bytes 1024 | tf_op jit(solution)/shard_map/attend/pallas_call | solution.py:209
  43.3 3.3 %attend.9.refs_2_ = f32[1536,640]{1,0:T(8,128)S(1)} custom-call(bf16[1536,256]{1,0:T(8,128)(2,1)S(1)} %get-tuple-element.45.q_ref, bf16[384,512]{1,0:T(8,128)(2,1)S(1)} %collective-permute-done.1.refs_0_, bf16[384,512]{1,0:T(8,128)(2,1)S(1)} %collective-permute-done.4.refs_1_, f32[1536,640]{1,0:T(8,128)S(1)} %attend.8.refs_2_), custom_call_target="tpu_custom_call" | custom-call | flops 1024 | bytes 1024 | tf_op jit(solution)/shard_map/attend/pallas_call | solution.py:209
  46.6 0.0 collective-permute-done.9.refs_0_
  46.6 1.4 %collective-permute-start.13 = (bf16[384,512]{1,0:T(8,128)(2,1)S(1)}, bf16[384,512]{1,0:T(8,128)(2,1)S(1)}, u32[]{:S(2)}, u32[]{:S(2)}) collective-permute-start(bf16[384,512]{1,0:T(8,128)(2,1)S(1)} %collective-permute-done.9.refs_0_), channel_id=1, source_target_pairs={{0,16},{8,120},{16,32},{24,8},{32,48},{40,24},{48,64},{56,40},{64,... | collective-permute-start | bytes 1179656 | tf_op jit(solution)/shard_map/ppermute | solution.py:298
  48.1 0.0 collective-permute-done.11.refs_1_
  48.1 1.2 %collective-permute-start.16 = (bf16[384,512]{1,0:T(8,128)(2,1)S(1)}, bf16[384,512]{1,0:T(8,128)(2,1)S(1)}, u32[]{:S(2)}, u32[]{:S(2)}) collective-permute-start(bf16[384,512]{1,0:T(8,128)(2,1)S(1)} %collective-permute-done.11.refs_1_), channel_id=1, source_target_pairs={{0,16},{8,120},{16,32},{24,8},{32,48},{40,24},{48,64},{56,40},{64,... | collective-permute-start | bytes 1179656 | tf_op jit(solution)/shard_map/ppermute | solution.py:298
  49.3 3.3 %attend.10.refs_2_ = f32[1536,640]{1,0:T(8,128)S(1)} custom-call(bf16[1536,256]{1,0:T(8,128)(2,1)S(1)} %get-tuple-element.45.q_ref, bf16[384,512]{1,0:T(8,128)(2,1)S(1)} %collective-permute-done.9.refs_0_, bf16[384,512]{1,0:T(8,128)(2,1)S(1)} %collective-permute-done.11.refs_1_, f32[1536,640]{1,0:T(8,128)S(1)} %attend.9.refs_2_), custom_call_target="tpu_custom_call" | custom-call | flops 1024 | bytes 1024 | tf_op jit(solution)/shard_map/attend/pallas_call | solution.py:209
  52.7 0.0 collective-permute-done.8.refs_0_
  52.7 0.0 collective-permute-done.14.refs_1_
  52.7 3.3 %attend.11.refs_2_ = f32[1536,640]{1,0:T(8,128)S(1)} custom-call(bf16[1536,256]{1,0:T(8,128)(2,1)S(1)} %get-tuple-element.45.q_ref, bf16[384,512]{1,0:T(8,128)(2,1)S(1)} %collective-permute-done.8.refs_0_, bf16[384,512]{1,0:T(8,128)(2,1)S(1)} %collective-permute-done.14.refs_1_, f32[1536,640]{1,0:T(8,128)S(1)} %attend.10.refs_2_), custom_call_target="tpu_custom_call" | custom-call | flops 1024 | bytes 1024 | tf_op jit(solution)/shard_map/attend/pallas_call | solution.py:209
  56.0 0.2 collective-permute-done.13.refs_0_
  56.3 2.2 %collective-permute-start.15 = (bf16[384,512]{1,0:T(8,128)(2,1)S(1)}, bf16[384,512]{1,0:T(8,128)(2,1)S(1)}, u32[]{:S(2)}, u32[]{:S(2)}) collective-permute-start(bf16[384,512]{1,0:T(8,128)(2,1)S(1)} %collective-permute-done.13.refs_0_), channel_id=1, source_target_pairs={{0,16},{8,120},{16,32},{24,8},{32,48},{40,24},{48,64},{56,40},{64,... | collective-permute-start | bytes 1179656 | tf_op jit(solution)/shard_map/ppermute | solution.py:298
  58.4 2.1 %collective-permute-done.16.refs_1_ = bf16[384,512]{1,0:T(8,128)(2,1)S(1)} collective-permute-done((bf16[384,512]{1,0:T(8,128)(2,1)S(1)}, bf16[384,512]{1,0:T(8,128)(2,1)S(1)}, u32[]{:S(2)}, u32[]{:S(2)}) %collective-permute-start.16) | collective-permute-done | bytes 393248 | tf_op jit(solution)/shard_map/ppermute | solution.py:298
  60.5 2.2 %collective-permute-start.18 = (bf16[384,512]{1,0:T(8,128)(2,1)S(1)}, bf16[384,512]{1,0:T(8,128)(2,1)S(1)}, u32[]{:S(2)}, u32[]{:S(2)}) collective-permute-start(bf16[384,512]{1,0:T(8,128)(2,1)S(1)} %collective-permute-done.16.refs_1_), channel_id=1, source_target_pairs={{0,16},{8,120},{16,32},{24,8},{32,48},{40,24},{48,64},{56,40},{64,... | collective-permute-start | bytes 1179656 | tf_op jit(solution)/shard_map/ppermute | solution.py:298
  62.6 0.0 collective-permute-start.12
  62.7 3.3 %attend.12.refs_2_ = f32[1536,640]{1,0:T(8,128)S(1)} custom-call(bf16[1536,256]{1,0:T(8,128)(2,1)S(1)} %get-tuple-element.45.q_ref, bf16[384,512]{1,0:T(8,128)(2,1)S(1)} %collective-permute-done.13.refs_0_, bf16[384,512]{1,0:T(8,128)(2,1)S(1)} %collective-permute-done.16.refs_1_, f32[1536,640]{1,0:T(8,128)S(1)} %attend.11.refs_2_), custom_call_target="tpu_custom_call" | custom-call | flops 1024 | bytes 1024 | tf_op jit(solution)/shard_map/attend/pallas_call | solution.py:209
  66.0 0.0 collective-permute-done.15.refs_0_
  66.0 0.9 collective-permute-start.17
  67.0 1.9 %collective-permute-done.18.refs_1_ = bf16[384,512]{1,0:T(8,128)(2,1)S(1)} collective-permute-done((bf16[384,512]{1,0:T(8,128)(2,1)S(1)}, bf16[384,512]{1,0:T(8,128)(2,1)S(1)}, u32[]{:S(2)}, u32[]{:S(2)}) %collective-permute-start.18) | collective-permute-done | bytes 393248 | tf_op jit(solution)/shard_map/ppermute | solution.py:298
  68.9 3.5 %attend.13.refs_2_ = f32[1536,640]{1,0:T(8,128)S(1)} custom-call(bf16[1536,256]{1,0:T(8,128)(2,1)S(1)} %get-tuple-element.45.q_ref, bf16[384,512]{1,0:T(8,128)(2,1)S(1)} %collective-permute-done.15.refs_0_, bf16[384,512]{1,0:T(8,128)(2,1)S(1)} %collective-permute-done.18.refs_1_, f32[1536,640]{1,0:T(8,128)S(1)} %attend.12.refs_2_), custom_call_target="tpu_custom_call" | custom-call | flops 1024 | bytes 1024 | tf_op jit(solution)/shard_map/attend/pallas_call | solution.py:209
  72.5 0.7 collective-permute-done.12.refs_0_
  73.1 4.2 %collective-permute-done.17.refs_1_ = bf16[384,512]{1,0:T(8,128)(2,1)S(1)} collective-permute-done((bf16[384,512]{1,0:T(8,128)(2,1)S(1)}, bf16[384,512]{1,0:T(8,128)(2,1)S(1)}, u32[]{:S(2)}, u32[]{:S(2)}) %collective-permute-start.17) | collective-permute-done | bytes 393248 | tf_op jit(solution)/shard_map/ppermute | solution.py:298
  77.3 1.8 %attend.15 = (bf16[768,256]{1,0:T(8,128)(2,1)S(1)}, f32[768,128]{1,0:T(8,128)S(1)}) custom-call(bf16[1536,256]{1,0:T(8,128)(2,1)S(1)} %get-tuple-element.45.q_ref, bf16[384,512]{1,0:T(8,128)(2,1)S(1)} %collective-permute-done.12.refs_0_, bf16[384,512]{1,0:T(8,128)(2,1)S(1)} %collective-permute-done.17.refs_1_, f32[1536,640]{1,0:T(8,128)S(1)} %attend.13.refs_2_), custom_call_target="tpu_custom_call" | custom-call | flops 1024 | bytes 1024 | tf_op jit(solution)/shard_map/attend/pallas_call | solution.py:209
  79.1 2.3 %collective-permute-start.19 = (bf16[768,256]{1,0:T(8,128)(2,1)S(1)}, bf16[768,256]{1,0:T(8,128)(2,1)S(1)}, u32[]{:S(2)}, u32[]{:S(2)}) collective-permute-start(bf16[768,256]{1,0:T(8,128)(2,1)S(1)} %get-tuple-element.71), channel_id=1, source_target_pairs={{0,8},{8,0},{1,9},{9,1},{2,10},{10,2},{3,11},{11,3},{4,12},{12,4},... | collective-permute-start | bytes 1179656 | tf_op jit(solution)/shard_map/ppermute | solution.py:300
  81.4 0.1 collective-permute-start.20
  81.5 1.8 %attend.14 = (f32[768,256]{1,0:T(8,128)S(1)}, f32[768,128]{1,0:T(8,128)S(1)}) custom-call(bf16[1536,256]{1,0:T(8,128)(2,1)S(1)} %get-tuple-element.45.q_ref, bf16[384,512]{1,0:T(8,128)(2,1)S(1)} %collective-permute-done.12.refs_0_, bf16[384,512]{1,0:T(8,128)(2,1)S(1)} %collective-permute-done.17.refs_1_, f32[1536,640]{1,0:T(8,128)S(1)} %attend.13.refs_2_), custom_call_target="tpu_custom_call" | custom-call | flops 1024 | bytes 1024 | tf_op jit(solution)/shard_map/attend/pallas_call | solution.py:209
  83.3 0.0 collective-permute-done.19.other
  83.3 0.0 collective-permute-done.20.other_stat
  83.3 1.0 %join.1 = (f32[384,256]{1,0:T(8,128)S(1)}, bf16[384,256]{1,0:T(8,128)(2,1)S(1)}, f32[16,8,128]{2,1,0:T(8,128)S(1)}) custom-call(f32[768,256]{1,0:T(8,128)S(1)} %get-tuple-element.69.mine, f32[768,128]{1,0:T(8,128)S(1)} %get-tuple-element.70.mine_stat, bf16[768,256]{1,0:T(8,128)(2,1)S(1)} %collective-permute-done.19.other, ...), custom_call_target="tpu_custom_call" | custom-call | tf_op jit(solution)/shard_map/join/pallas_call | solution.py:253
  84.3 2.9 %collective-permute-start.21 = (bf16[384,256]{1,0:T(8,128)(2,1)S(1)}, bf16[384,256]{1,0:T(8,128)(2,1)S(1)}, u32[]{:S(2)}, u32[]{:S(2)}) collective-permute-start(bf16[384,256]{1,0:T(8,128)(2,1)S(1)} %get-tuple-element.74), channel_id=1, source_target_pairs={{0,128},{128,0},{1,129},{129,1},{2,130},{130,2},{3,131},{131,3},{4... | collective-permute-start | bytes 589832 | tf_op jit(solution)/shard_map/ppermute | solution.py:299
  87.3 10.9 %all_to_all.5.squares = f32[16,8,128]{2,1,0:T(8,128)S(1)} all-to-all(f32[16,8,128]{2,1,0:T(8,128)S(1)} %get-tuple-element.75), channel_id=1, replica_groups=mesh['yh'=2,'z'=8,'core'=2,'yl'=2,'x'=4] {'yh','yl','x'}, dimensions={0} | all-to-all | bytes 131072 | tf_op jit(solution)/shard_map/all_to_all | solution.py:341
  98.2 0.0 collective-permute-done.21.come
  98.2 1.2 %finish.1 = (bf16[384,256]{1,0:T(8,128)(2,1)}, bf16[384,256]{1,0:T(8,128)(2,1)}) custom-call(f32[384,256]{1,0:T(8,128)S(1)} %get-tuple-element.73.keep, bf16[384,256]{1,0:T(8,128)(2,1)S(1)} %collective-permute-done.21.come, f32[16,8,128]{2,1,0:T(8,128)S(1)} %all_to_all.5.squares), custom_call_target="tpu_custom_call" | custom-call | tf_op jit(solution)/shard_map/finish/pallas_call | solution.py:292
  (1 shorter events, 0.0 us)
Async XLA Ops:
  2.9 7.2 %collective-permute-start.2 = (bf16[384,512]{1,0:T(8,128)(2,1)}, bf16[384,512]{1,0:T(8,128)(2,1)S(1)}, u32[]{:S(2)}, u32[]{:S(2)}) collective-permute-start(bf16[384,512]{1,0:T(8,128)(2,1)} %get-tuple-element.39.own_kv), channel_id=1, source_target_pairs={{0,8},{8,0},{1,9},{9,1},{2,10},{10,2},{3,11},{11,3},{4,12},{12,4},... | collective-permute-start | bytes 1179656 | tf_op jit(solution)/shard_map/ppermute | solution.py:300
  6.2 8.9 %collective-permute-start = (bf16[384,512]{1,0:T(8,128)(2,1)}, bf16[384,512]{1,0:T(8,128)(2,1)S(1)}, u32[]{:S(2)}, u32[]{:S(2)}) collective-permute-start(bf16[384,512]{1,0:T(8,128)(2,1)} %get-tuple-element.39.own_kv), channel_id=1, source_target_pairs={{0,16},{8,120},{16,32},{24,8},{32,48},{40,24},{48,64},{56,40},{64,... | collective-permute-start | bytes 1179656 | tf_op jit(solution)/shard_map/ppermute | solution.py:298
  10.1 9.1 %collective-permute-start.3 = (bf16[384,512]{1,0:T(8,128)(2,1)S(1)}, bf16[384,512]{1,0:T(8,128)(2,1)S(1)}, u32[]{:S(2)}, u32[]{:S(2)}) collective-permute-start(bf16[384,512]{1,0:T(8,128)(2,1)S(1)} %collective-permute-done.2), channel_id=1, source_target_pairs={{0,16},{8,120},{16,32},{24,8},{32,48},{40,24},{48,64},{56,40},{64,... | collective-permute-start | bytes 1179656 | tf_op jit(solution)/shard_map/ppermute | solution.py:298
  11.6 17.8 %collective-permute-start.5 = (bf16[384,512]{1,0:T(8,128)(2,1)}, bf16[384,512]{1,0:T(8,128)(2,1)S(1)}, u32[]{:S(2)}, u32[]{:S(2)}) collective-permute-start(bf16[384,512]{1,0:T(8,128)(2,1)} %get-tuple-element.40), channel_id=1, source_target_pairs={{0,128},{128,0},{1,129},{129,1},{2,130},{130,2},{3,131},{131,3},{4... | collective-permute-start | bytes 1179656 | tf_op jit(solution)/shard_map/ppermute | solution.py:299
  15.1 14.3 %collective-permute-start.1 = (bf16[384,512]{1,0:T(8,128)(2,1)S(1)}, bf16[384,512]{1,0:T(8,128)(2,1)S(1)}, u32[]{:S(2)}, u32[]{:S(2)}) collective-permute-start(bf16[384,512]{1,0:T(8,128)(2,1)S(1)} %collective-permute-done.refs_0_), channel_id=1, source_target_pairs={{0,16},{8,120},{16,32},{24,8},{32,48},{40,24},{48,64},{56,40},{64,... | collective-permute-start | bytes 1179656 | tf_op jit(solution)/shard_map/ppermute | solution.py:298
  19.2 10.2 %collective-permute-start.4 = (bf16[384,512]{1,0:T(8,128)(2,1)S(1)}, bf16[384,512]{1,0:T(8,128)(2,1)S(1)}, u32[]{:S(2)}, u32[]{:S(2)}) collective-permute-start(bf16[384,512]{1,0:T(8,128)(2,1)S(1)} %collective-permute-done.3.refs_1_), channel_id=1, source_target_pairs={{0,16},{8,120},{16,32},{24,8},{32,48},{40,24},{48,64},{56,40},{64,... | collective-permute-start | bytes 1179656 | tf_op jit(solution)/shard_map/ppermute | solution.py:298
  22.6 6.8 %collective-permute-start.6 = (bf16[384,256]{1,0:T(8,128)(2,1)}, bf16[384,256]{1,0:T(8,128)(2,1)S(1)}, u32[]{:S(2)}, u32[]{:S(2)}) collective-permute-start(bf16[384,256]{1,0:T(8,128)(2,1)} %get-tuple-element.41), channel_id=1, source_target_pairs={{0,128},{128,0},{1,129},{129,1},{2,130},{130,2},{3,131},{131,3},{4... | collective-permute-start | bytes 589832 | tf_op jit(solution)/shard_map/ppermute | solution.py:299
  29.4 2.4 %collective-permute-start.7 = (bf16[768,256]{1,0:T(8,128)(2,1)S(1)}, bf16[768,256]{1,0:T(8,128)(2,1)S(1)}, u32[]{:S(2)}, u32[]{:S(2)}) collective-permute-start(bf16[768,256]{1,0:T(8,128)(2,1)S(1)} %constant_dynamic-update-slice_fusion.own_q), channel_id=1, source_target_pairs={{0,8},{8,0},{1,9},{9,1},{2,10},{10,2},{3,11},{11,3},{4,12},{12,4},... | collective-permute-start | bytes 1179656 | tf_op jit(solution)/shard_map/ppermute | solution.py:300
  29.7 6.9 %collective-permute-start.10 = (bf16[384,512]{1,0:T(8,128)(2,1)S(1)}, bf16[384,512]{1,0:T(8,128)(2,1)S(1)}, u32[]{:S(2)}, u32[]{:S(2)}) collective-permute-start(bf16[384,512]{1,0:T(8,128)(2,1)S(1)} %collective-permute-done.5.peer_kv), channel_id=1, source_target_pairs={{0,8},{8,0},{1,9},{9,1},{2,10},{10,2},{3,11},{11,3},{4,12},{12,4},... | collective-permute-start | bytes 1179656 | tf_op jit(solution)/shard_map/ppermute | solution.py:300
  30.0 16.6 %collective-permute-start.9 = (bf16[384,512]{1,0:T(8,128)(2,1)S(1)}, bf16[384,512]{1,0:T(8,128)(2,1)S(1)}, u32[]{:S(2)}, u32[]{:S(2)}) collective-permute-start(bf16[384,512]{1,0:T(8,128)(2,1)S(1)} %collective-permute-done.5.peer_kv), channel_id=1, source_target_pairs={{0,16},{8,120},{16,32},{24,8},{32,48},{40,24},{48,64},{56,40},{64,... | collective-permute-start | bytes 1179656 | tf_op jit(solution)/shard_map/ppermute | solution.py:298
  31.9 1.0 %copy-start = (bf16[384,512]{1,0:T(8,128)(2,1)S(1)}, bf16[384,512]{1,0:T(8,128)(2,1)}, u32[]{:S(2)}) copy-start(bf16[384,512]{1,0:T(8,128)(2,1)} %get-tuple-element.39.own_kv) | copy-start | bytes 1179652
  36.6 11.5 %collective-permute-start.11 = (bf16[384,512]{1,0:T(8,128)(2,1)S(1)}, bf16[384,512]{1,0:T(8,128)(2,1)S(1)}, u32[]{:S(2)}, u32[]{:S(2)}) collective-permute-start(bf16[384,512]{1,0:T(8,128)(2,1)S(1)} %collective-permute-done.10), channel_id=1, source_target_pairs={{0,16},{8,120},{16,32},{24,8},{32,48},{40,24},{48,64},{56,40},{64,... | collective-permute-start | bytes 1179656 | tf_op jit(solution)/shard_map/ppermute | solution.py:298
  37.9 14.7 %collective-permute-start.8 = (bf16[384,512]{1,0:T(8,128)(2,1)S(1)}, bf16[384,512]{1,0:T(8,128)(2,1)S(1)}, u32[]{:S(2)}, u32[]{:S(2)}) collective-permute-start(bf16[384,512]{1,0:T(8,128)(2,1)S(1)} %collective-permute-done.1.refs_0_), channel_id=1, source_target_pairs={{0,16},{8,120},{16,32},{24,8},{32,48},{40,24},{48,64},{56,40},{64,... | collective-permute-start | bytes 1179656 | tf_op jit(solution)/shard_map/ppermute | solution.py:298
  38.2 14.5 %collective-permute-start.14 = (bf16[384,512]{1,0:T(8,128)(2,1)S(1)}, bf16[384,512]{1,0:T(8,128)(2,1)S(1)}, u32[]{:S(2)}, u32[]{:S(2)}) collective-permute-start(bf16[384,512]{1,0:T(8,128)(2,1)S(1)} %collective-permute-done.4.refs_1_), channel_id=1, source_target_pairs={{0,16},{8,120},{16,32},{24,8},{32,48},{40,24},{48,64},{56,40},{64,... | collective-permute-start | bytes 1179656 | tf_op jit(solution)/shard_map/ppermute | solution.py:298
  46.6 9.6 %collective-permute-start.13 = (bf16[384,512]{1,0:T(8,128)(2,1)S(1)}, bf16[384,512]{1,0:T(8,128)(2,1)S(1)}, u32[]{:S(2)}, u32[]{:S(2)}) collective-permute-start(bf16[384,512]{1,0:T(8,128)(2,1)S(1)} %collective-permute-done.9.refs_0_), channel_id=1, source_target_pairs={{0,16},{8,120},{16,32},{24,8},{32,48},{40,24},{48,64},{56,40},{64,... | collective-permute-start | bytes 1179656 | tf_op jit(solution)/shard_map/ppermute | solution.py:298
  48.1 12.4 %collective-permute-start.16 = (bf16[384,512]{1,0:T(8,128)(2,1)S(1)}, bf16[384,512]{1,0:T(8,128)(2,1)S(1)}, u32[]{:S(2)}, u32[]{:S(2)}) collective-permute-start(bf16[384,512]{1,0:T(8,128)(2,1)S(1)} %collective-permute-done.11.refs_1_), channel_id=1, source_target_pairs={{0,16},{8,120},{16,32},{24,8},{32,48},{40,24},{48,64},{56,40},{64,... | collective-permute-start | bytes 1179656 | tf_op jit(solution)/shard_map/ppermute | solution.py:298
  56.3 9.7 %collective-permute-start.15 = (bf16[384,512]{1,0:T(8,128)(2,1)S(1)}, bf16[384,512]{1,0:T(8,128)(2,1)S(1)}, u32[]{:S(2)}, u32[]{:S(2)}) collective-permute-start(bf16[384,512]{1,0:T(8,128)(2,1)S(1)} %collective-permute-done.13.refs_0_), channel_id=1, source_target_pairs={{0,16},{8,120},{16,32},{24,8},{32,48},{40,24},{48,64},{56,40},{64,... | collective-permute-start | bytes 1179656 | tf_op jit(solution)/shard_map/ppermute | solution.py:298
  60.5 8.4 %collective-permute-start.18 = (bf16[384,512]{1,0:T(8,128)(2,1)S(1)}, bf16[384,512]{1,0:T(8,128)(2,1)S(1)}, u32[]{:S(2)}, u32[]{:S(2)}) collective-permute-start(bf16[384,512]{1,0:T(8,128)(2,1)S(1)} %collective-permute-done.16.refs_1_), channel_id=1, source_target_pairs={{0,16},{8,120},{16,32},{24,8},{32,48},{40,24},{48,64},{56,40},{64,... | collective-permute-start | bytes 1179656 | tf_op jit(solution)/shard_map/ppermute | solution.py:298
  62.6 10.5 %collective-permute-start.12 = (bf16[384,512]{1,0:T(8,128)(2,1)S(1)}, bf16[384,512]{1,0:T(8,128)(2,1)S(1)}, u32[]{:S(2)}, u32[]{:S(2)}) collective-permute-start(bf16[384,512]{1,0:T(8,128)(2,1)S(1)} %collective-permute-done.8.refs_0_), channel_id=1, source_target_pairs={{0,16},{8,120},{16,32},{24,8},{32,48},{40,24},{48,64},{56,40},{64,... | collective-permute-start | bytes 1179656 | tf_op jit(solution)/shard_map/ppermute | solution.py:298
  66.0 11.3 %collective-permute-start.17 = (bf16[384,512]{1,0:T(8,128)(2,1)S(1)}, bf16[384,512]{1,0:T(8,128)(2,1)S(1)}, u32[]{:S(2)}, u32[]{:S(2)}) collective-permute-start(bf16[384,512]{1,0:T(8,128)(2,1)S(1)} %collective-permute-done.15.refs_0_), channel_id=1, source_target_pairs={{0,16},{8,120},{16,32},{24,8},{32,48},{40,24},{48,64},{56,40},{64,... | collective-permute-start | bytes 1179656 | tf_op jit(solution)/shard_map/ppermute | solution.py:298
  79.1 4.2 %collective-permute-start.19 = (bf16[768,256]{1,0:T(8,128)(2,1)S(1)}, bf16[768,256]{1,0:T(8,128)(2,1)S(1)}, u32[]{:S(2)}, u32[]{:S(2)}) collective-permute-start(bf16[768,256]{1,0:T(8,128)(2,1)S(1)} %get-tuple-element.71), channel_id=1, source_target_pairs={{0,8},{8,0},{1,9},{9,1},{2,10},{10,2},{3,11},{11,3},{4,12},{12,4},... | collective-permute-start | bytes 1179656 | tf_op jit(solution)/shard_map/ppermute | solution.py:300
  81.4 1.9 %collective-permute-start.20 = (f32[768,128]{1,0:T(8,128)S(1)}, f32[768,128]{1,0:T(8,128)S(1)}, u32[]{:S(2)}, u32[]{:S(2)}) collective-permute-start(f32[768,128]{1,0:T(8,128)S(1)} %get-tuple-element.72), channel_id=1, source_target_pairs={{0,8},{8,0},{1,9},{9,1},{2,10},{10,2},{3,11},{11,3},{4,12},{12,4},... | collective-permute-start | bytes 1179656 | tf_op jit(solution)/shard_map/ppermute | solution.py:300
  84.3 13.9 %collective-permute-start.21 = (bf16[384,256]{1,0:T(8,128)(2,1)S(1)}, bf16[384,256]{1,0:T(8,128)(2,1)S(1)}, u32[]{:S(2)}, u32[]{:S(2)}) collective-permute-start(bf16[384,256]{1,0:T(8,128)(2,1)S(1)} %get-tuple-element.74), channel_id=1, source_target_pairs={{0,128},{128,0},{1,129},{129,1},{2,130},{130,2},{3,131},{131,3},{4... | collective-permute-start | bytes 589832 | tf_op jit(solution)/shard_map/ppermute | solution.py:299

commit v3 on v2

--- a/solution.py
+++ b/solution.py
@@ -30,26 +30,41 @@
     return lax.dot_general(a, b, (((1,), (0,)), ((), ())), preferred_element_type=F32)
 
 
-def pack_kernel(q, k, v, qt, kt, vt, own_kv, own_q, other_kv, other_q):
+def pack_kernel(q, k, v, qt, kt, vt, own_kv, own_q, other):
+    step = pl.program_id(0)
     flip = lax.axis_index("yh") == 1
-    spots = ((kt, 0, 0), (k, 0, 1), (v, 0, 2), (vt, 0, 3), (q, 1, 0), (qt, 1, 1))
-    for ref, which, at in spots:
+    rows = q.shape[0]
+    for at, ref in enumerate((kt, k, v, vt, q, qt)):
         low, high = ref[:, :DH], ref[:, DH:]
-        cols = slice(at * DH, (at + 1) * DH)
-        (own_kv, own_q)[which][:, cols] = jnp.where(flip, high, low)
-        (other_kv, other_q)[which][:, cols] = jnp.where(flip, low, high)
+        mine, theirs = jnp.where(flip, high, low), jnp.where(flip, low, high)
+        if at < 4:
+            cols = slice(at * DH, (at + 1) * DH)
+            own_kv[:, cols] = mine
+            other[pl.ds(pl.multiple_of(step * rows, rows), rows), cols] = theirs
+        else:
+            own_q[:, (at - 4) * DH : (at - 3) * DH] = mine
+            for half in range(2):
+
+                @pl.when(step == half)
+                def _():
+                    first = (2 * half + at - 4) * DH
+                    other[2 * rows :, first : first + DH] = theirs
 
 
 def pack(*arrays):
     rows = arrays[0].shape[0]
-    row = lambda width: pl.BlockSpec((rows // 2, width), lambda i: (i, 0))
-    shapes = [jax.ShapeDtypeStruct((rows, n * DH), BF16) for n in (4, 2, 4, 2)]
+    half = rows // 2
+    row = lambda width: pl.BlockSpec((half, width), lambda i: (i, 0))
     return pl.pallas_call(
         pack_kernel,
         grid=(2,),
         in_specs=[row(2 * DH)] * 6,
-        out_specs=[row(n * DH) for n in (4, 2, 4, 2)],
-        out_shape=shapes,
+        out_specs=[row(4 * DH), row(2 * DH), pl.BlockSpec((rows + half, 4 * DH), lambda i: (0, 0))],
+        out_shape=[
+            jax.ShapeDtypeStruct((rows, 4 * DH), BF16),
+            jax.ShapeDtypeStruct((rows, 2 * DH), BF16),
+            jax.ShapeDtypeStruct((rows + half, 4 * DH), BF16),
+        ],
         compiler_params=pltpu.CompilerParams(vmem_limit_bytes=60 << 20),
         cost_estimate=pl.CostEstimate(flops=0, bytes_accessed=12 * rows * 2 * DH * 2, transcendentals=0),
         name="pack",
@@ -104,12 +119,16 @@
         ref[rows, i * DH : (i + 1) * DH] = piece
 
 
-def begin_kernel(own_kv, peer_kv, own_q, core_q, state, query, kv):
+def begin_kernel(own_kv, own_q, core_q, peer, peer_core, state, query, kv):
     rows = own_kv.shape[0]
+    half = rows // 2
     kv[:rows, :] = own_kv[...]
-    kv[rows:, :] = peer_kv[...]
-    query[: 2 * rows, :] = own_q[...]
-    query[2 * rows :, :] = core_q[...]
+    kv[rows:, :] = peer[:rows, :]
+    query[:rows, :] = own_q[...]
+    query[2 * rows : 3 * rows, :] = core_q[...]
+    for at, ref in ((rows, peer), (3 * rows, peer_core)):
+        query[at : at + half, :] = ref[rows:, : 2 * DH]
+        query[at + half : at + rows, :] = ref[rows:, 2 * DH :]
 
     def body(i, carry):
         at = pl.multiple_of(i * 2 * TILE, 2 * TILE)
@@ -301,15 +320,17 @@
     def after(block, state):
         return lax.optimization_barrier((block, state))
 
-    own_kv, own_q, other_kv, other_q = pack(q, k, v, qt, kt, vt)
-    peer_q, peer_kv = over_y(other_q), over_y(other_kv)
+    own_kv, own_q, other = pack(q, k, v, qt, kt, vt)
+    peer = over_y(other)
     core_kv = over_core(own_kv)
     near = [hop(own_kv), hop(core_kv)]
+    core_q = over_core(own_q)
     near_next = [hop(a) for a in near]
-    near_next[0], near_next[1], peer_kv, peer_q = lax.optimization_barrier((*near_next, peer_kv, peer_q))
-    far = [hop(peer_kv), hop(over_core(peer_kv))]
-    pair_q = jnp.concatenate([own_q, peer_q], axis=0)
-    state, query = begin(own_kv, peer_kv, pair_q, over_core(pair_q))
+    near_next[0], near_next[1], peer, core_q = lax.optimization_barrier((*near_next, peer, core_q))
+    peer_core = over_core(peer)
+    far = [hop(peer[:tokens]), hop(peer_core[:tokens])]
+    near_three = [hop(a) for a in near_next]
+    state, query = begin(own_kv, own_q, core_q, peer, peer_core)
 
     def turn(pair, state, count):
         sent, kept = [], []
@@ -320,9 +341,8 @@
                 sent.append(hop(block))
         return kept, sent, state
 
-    near_two, near_three, state = turn(near_next, state, 2)
     state = attend(query, near, state)
-    state = attend(query, near_two, state)
+    state = attend(query, near_next, state)
     far, far_next, state = turn(far, state, 2)
     state = attend(query, far, state)
     near, near_last, state = turn(near_three, state, 1)
@@ -331,7 +351,9 @@
     state = attend(query, far, state)
     far, far_last, state = turn(far_next, state, 1)
     state = attend(query, far, state)
-    ends = near_last + far_last
+    last_near, state = after(near_last[0], state)
+    state = attend(query, [last_near], state)
+    ends = far_last
     rows = query.shape[0]
     there, there_stat = attend(query, ends, state, (rows // 2, rows), BF16)
     come, come_stat = over_core(there), over_core(there_stat)

time: 99.6 us -> 99 us (level)
  starting transfers between devices: 39.9 us -> 38.1 us
  Pallas kernels: 32.2 us -> 33.3 us
    ppermute x5, starting transfers between devices: 6.27 us -> 9.23 us  [on_device(): over_core = lambda a: lax.ppermute(a, 'core', SWAP)]
    ppermute x3 -> x2, starting transfers between devices: 8.59 us -> 5.82 us  [on_device(): over_y = lambda a: lax.ppermute(a, 'yh', SWAP)]
    ppermute x5, waiting for transfers between devices: 0.01 us -> 2.59 us  [on_device(): over_core = lambda a: lax.ppermute(a, 'core', SWAP)]
    ppermute x14, starting transfers between devices: 25.1 us -> 23.1 us  [on_device(): hop = lambda a: lax.ppermute(a, ('z', 'core'), hop_pairs)]
    ppermute x3 -> x2, waiting for transfers between devices: 3.1 us -> 1.37 us  [on_device(): over_y = lambda a: lax.ppermute(a, 'yh', SWAP)]
    pallas_call x8 -> x9, Pallas kernels: 24 us -> 24.9 us  [attend(): pl.pallas_call(functools.partial(attend_kernel, len(kvs), base, kind is n...]
  transfers between devices with their start and end apart: 22 -> 21, of which waited for: 8 -> 11; matrix products, arithmetic and copies ran while one was open for 1% -> 0% of each run, Pallas kernels for 26% -> 28%
where the time goes in v3:
time: 99 us; the launch traced here: 98.7 us
  starting transfers between devices  38.1 us (38%)
  Pallas kernels  33.3 us (34%)
  waiting for transfers between devices  13.7 us (14%)
  blocking collectives  10.9 us (11%)
  local copies, waits for them, and re-layouts  1.97 us (2%)
    pallas_call x9, Pallas kernels, attend(): pl.pallas_call(functools.partial(attend_kernel, len(kvs), base, kind is n...  24.9 us
    ppermute x14, starting transfers between devices, on_device(): hop = lambda a: lax.ppermute(a, ('z', 'core'), hop_pairs)  23.1 us
    all_to_all x1, blocking collectives, on_device(): squares = lax.all_to_all(squares, ('yh', 'yl', 'x'), 0, 0, tiled=True)  10.9 us
    ppermute x14, waiting for transfers between devices, on_device(): hop = lambda a: lax.ppermute(a, ('z', 'core'), hop_pairs)  9.69 us
    ppermute x5, starting transfers between devices, on_device(): over_core = lambda a: lax.ppermute(a, 'core', SWAP)  9.23 us
    ppermute x2, starting transfers between devices, on_device(): over_y = lambda a: lax.ppermute(a, 'yh', SWAP)  5.82 us
    pallas_call x1, Pallas kernels, begin(): pl.pallas_call(begin_kernel, out_shape=[jax.ShapeDtypeStruct((rows, 5 * D...  3.73 us
    ppermute x5, waiting for transfers between devices, on_device(): over_core = lambda a: lax.ppermute(a, 'core', SWAP)  2.59 us
  transfers between devices with their start and end apart: 21, of which 11 were waited for; matrix products, arithmetic and copies ran while one was open for 0% of the time, Pallas kernels for 28%

profile of v3, /device:TPU:1, one launch (start us, length us, event | category | flops | bytes accessed | tf_op | source)
XLA Modules:
  0.0 98.7 jit_solution(8398709610473318362)
XLA Ops:
  0.6 2.4 %pack.1 = (bf16[384,512]{1,0:T(8,128)(2,1)}, bf16[384,256]{1,0:T(8,128)(2,1)}, bf16[576,512]{1,0:T(8,128)(2,1)}) custom-call(bf16[384,256]{1,0:T(8,128)(2,1)} %q.1, bf16[384,256]{1,0:T(8,128)(2,1)} %k.1, bf16[384,256]{1,0:T(8,128)(2,1)} %v.1, bf16[384,256]{1,0:T(8,128)(2,1)} %qt.1, bf16[384,256]{1,0:T(8,128)(2,1)} %kt.1, bf16[384,256]{1,0:T(8,128)(2,1)} %vt.1), custom_call_target="tpu_custom_call" | custom-call | bytes 2359296 | tf_op jit(solution)/shard_map/pack/pallas_call | solution.py:58
  3.1 3.3 %collective-permute-start.2 = (bf16[384,512]{1,0:T(8,128)(2,1)}, bf16[384,512]{1,0:T(8,128)(2,1)S(1)}, u32[]{:S(2)}, u32[]{:S(2)}) collective-permute-start(bf16[384,512]{1,0:T(8,128)(2,1)} %get-tuple-element.36.own_kv), channel_id=1, source_target_pairs={{0,8},{8,0},{1,9},{9,1},{2,10},{10,2},{3,11},{11,3},{4,12},{12,4},... | collective-permute-start | bytes 1179656 | tf_op jit(solution)/shard_map/ppermute | solution.py:319
  6.4 3.8 %collective-permute-start = (bf16[384,512]{1,0:T(8,128)(2,1)}, bf16[384,512]{1,0:T(8,128)(2,1)S(1)}, u32[]{:S(2)}, u32[]{:S(2)}) collective-permute-start(bf16[384,512]{1,0:T(8,128)(2,1)} %get-tuple-element.36.own_kv), channel_id=1, source_target_pairs={{0,16},{8,120},{16,32},{24,8},{32,48},{40,24},{48,64},{56,40},{64,... | collective-permute-start | bytes 1179656 | tf_op jit(solution)/shard_map/ppermute | solution.py:317
  10.2 0.0 collective-permute-done.2
  10.2 1.6 %collective-permute-start.3 = (bf16[384,512]{1,0:T(8,128)(2,1)S(1)}, bf16[384,512]{1,0:T(8,128)(2,1)S(1)}, u32[]{:S(2)}, u32[]{:S(2)}) collective-permute-start(bf16[384,512]{1,0:T(8,128)(2,1)S(1)} %collective-permute-done.2), channel_id=1, source_target_pairs={{0,16},{8,120},{16,32},{24,8},{32,48},{40,24},{48,64},{56,40},{64,... | collective-permute-start | bytes 1179656 | tf_op jit(solution)/shard_map/ppermute | solution.py:317
  11.8 2.9 %collective-permute-start.5 = (bf16[576,512]{1,0:T(8,128)(2,1)}, bf16[576,512]{1,0:T(8,128)(2,1)S(1)}, u32[]{:S(2)}, u32[]{:S(2)}) collective-permute-start(bf16[576,512]{1,0:T(8,128)(2,1)} %get-tuple-element.38), channel_id=1, source_target_pairs={{0,128},{128,0},{1,129},{129,1},{2,130},{130,2},{3,131},{131,3},{4... | collective-permute-start | bytes 1769480 | tf_op jit(solution)/shard_map/ppermute | solution.py:318
  14.7 0.6 collective-permute-done.refs_0_
  15.3 3.3 %collective-permute-start.1 = (bf16[384,512]{1,0:T(8,128)(2,1)S(1)}, bf16[384,512]{1,0:T(8,128)(2,1)S(1)}, u32[]{:S(2)}, u32[]{:S(2)}) collective-permute-start(bf16[384,512]{1,0:T(8,128)(2,1)S(1)} %collective-permute-done.refs_0_), channel_id=1, source_target_pairs={{0,16},{8,120},{16,32},{24,8},{32,48},{40,24},{48,64},{56,40},{64,... | collective-permute-start | bytes 1179656 | tf_op jit(solution)/shard_map/ppermute | solution.py:317
  18.6 0.8 collective-permute-done.3.refs_1_
  19.4 3.4 %collective-permute-start.4 = (bf16[384,512]{1,0:T(8,128)(2,1)S(1)}, bf16[384,512]{1,0:T(8,128)(2,1)S(1)}, u32[]{:S(2)}, u32[]{:S(2)}) collective-permute-start(bf16[384,512]{1,0:T(8,128)(2,1)S(1)} %collective-permute-done.3.refs_1_), channel_id=1, source_target_pairs={{0,16},{8,120},{16,32},{24,8},{32,48},{40,24},{48,64},{56,40},{64,... | collective-permute-start | bytes 1179656 | tf_op jit(solution)/shard_map/ppermute | solution.py:317
  22.8 0.0 collective-permute-start.6
  22.8 1.6 %collective-permute-done.6.core_q = bf16[384,256]{1,0:T(8,128)(2,1)S(1)} collective-permute-done((bf16[384,256]{1,0:T(8,128)(2,1)}, bf16[384,256]{1,0:T(8,128)(2,1)S(1)}, u32[]{:S(2)}, u32[]{:S(2)}) %collective-permute-start.6) | collective-permute-done | bytes 196640 | tf_op jit(solution)/shard_map/ppermute | solution.py:319
  24.4 1.4 %collective-permute-done.5.peer = bf16[576,512]{1,0:T(8,128)(2,1)S(1)} collective-permute-done((bf16[576,512]{1,0:T(8,128)(2,1)}, bf16[576,512]{1,0:T(8,128)(2,1)S(1)}, u32[]{:S(2)}, u32[]{:S(2)}) %collective-permute-start.5) | collective-permute-done | bytes 589856 | tf_op jit(solution)/shard_map/ppermute | solution.py:318
  25.8 0.0 collective-permute-done.1.refs_0_
  25.8 2.0 %collective-permute-done.4.refs_1_ = bf16[384,512]{1,0:T(8,128)(2,1)S(1)} collective-permute-done((bf16[384,512]{1,0:T(8,128)(2,1)S(1)}, bf16[384,512]{1,0:T(8,128)(2,1)S(1)}, u32[]{:S(2)}, u32[]{:S(2)}) %collective-permute-start.4) | collective-permute-done | bytes 393248 | tf_op jit(solution)/shard_map/ppermute | solution.py:317
  27.8 2.0 %collective-permute-start.7 = (bf16[576,512]{1,0:T(8,128)(2,1)S(1)}, bf16[576,512]{1,0:T(8,128)(2,1)S(1)}, u32[]{:S(2)}, u32[]{:S(2)}) collective-permute-start(bf16[576,512]{1,0:T(8,128)(2,1)S(1)} %collective-permute-done.5.peer), channel_id=1, source_target_pairs={{0,8},{8,0},{1,9},{9,1},{2,10},{10,2},{3,11},{11,3},{4,12},{12,4},... | collective-permute-start | bytes 1769480 | tf_op jit(solution)/shard_map/ppermute | solution.py:319
  29.8 1.3 %collective-permute-start.8 = (bf16[384,512]{1,0:T(8,128)(2,1)S(1)}, bf16[384,512]{1,0:T(8,128)(2,1)S(1)}, u32[]{:S(2)}, u32[]{:S(2)}) collective-permute-start(bf16[384,512]{1,0:T(8,128)(2,1)S(1)} %slice.6), channel_id=1, source_target_pairs={{0,16},{8,120},{16,32},{24,8},{32,48},{40,24},{48,64},{56,40},{64,... | collective-permute-start | bytes 1179656 | tf_op jit(solution)/shard_map/ppermute | solution.py:317
  31.1 0.3 collective-permute-done.7.peer_core
  31.4 1.6 %collective-permute-start.11 = (bf16[384,512]{1,0:T(8,128)(2,1)S(1)}, bf16[384,512]{1,0:T(8,128)(2,1)S(1)}, u32[]{:S(2)}, u32[]{:S(2)}) collective-permute-start(bf16[384,512]{1,0:T(8,128)(2,1)S(1)} %slice.8), channel_id=1, source_target_pairs={{0,16},{8,120},{16,32},{24,8},{32,48},{40,24},{48,64},{56,40},{64,... | collective-permute-start | bytes 1179656 | tf_op jit(solution)/shard_map/ppermute | solution.py:317
  33.0 0.4 collective-permute-start.10
  33.4 1.7 %collective-permute-start.12 = (bf16[384,512]{1,0:T(8,128)(2,1)S(1)}, bf16[384,512]{1,0:T(8,128)(2,1)S(1)}, u32[]{:S(2)}, u32[]{:S(2)}) collective-permute-start(bf16[384,512]{1,0:T(8,128)(2,1)S(1)} %collective-permute-done.4.refs_1_), channel_id=1, source_target_pairs={{0,16},{8,120},{16,32},{24,8},{32,48},{40,24},{48,64},{56,40},{64,... | collective-permute-start | bytes 1179656 | tf_op jit(solution)/shard_map/ppermute | solution.py:317
  35.1 0.0 copy-start
  35.1 1.0 %copy-done = bf16[384,512]{1,0:T(8,128)(2,1)S(1)} copy-done((bf16[384,512]{1,0:T(8,128)(2,1)S(1)}, bf16[384,512]{1,0:T(8,128)(2,1)}, u32[]{:S(2)}) %copy-start) | copy-done | bytes 393240
  36.1 0.0 copy-start.1
  36.1 0.9 copy-done.1
  37.0 3.7 %begin.1 = (f32[1536,640]{1,0:T(8,128)S(1)}, bf16[1536,256]{1,0:T(8,128)(2,1)S(1)}) custom-call(bf16[384,512]{1,0:T(8,128)(2,1)S(1)} %copy-done, bf16[384,256]{1,0:T(8,128)(2,1)S(1)} %copy-done.1, bf16[384,256]{1,0:T(8,128)(2,1)S(1)} %collective-permute-done.6.core_q, bf16[576,512]{1,0:T(8,128)(2,1)S(1)} %collective-permute-done.5.peer, ...), custom_call_target="tpu_custom_call" | custom-call | flops 1024 | bytes 1024 | tf_op jit(solution)/shard_map/begin/pallas_call | solution.py:208
  40.8 3.5 %attend.9.refs_2_ = f32[1536,640]{1,0:T(8,128)S(1)} custom-call(bf16[1536,256]{1,0:T(8,128)(2,1)S(1)} %get-tuple-element.41.q_ref, bf16[384,512]{1,0:T(8,128)(2,1)S(1)} %collective-permute-done.refs_0_, bf16[384,512]{1,0:T(8,128)(2,1)S(1)} %collective-permute-done.3.refs_1_, f32[1536,640]{1,0:T(8,128)S(1)} %get-tuple-element.44.refs_2_), custom_call_target="tpu_custom_call" | custom-call | flops 1024 | bytes 1024 | tf_op jit(solution)/shard_map/attend/pallas_call | solution.py:228
  44.3 3.3 %attend.10.refs_2_ = f32[1536,640]{1,0:T(8,128)S(1)} custom-call(bf16[1536,256]{1,0:T(8,128)(2,1)S(1)} %get-tuple-element.41.q_ref, bf16[384,512]{1,0:T(8,128)(2,1)S(1)} %collective-permute-done.1.refs_0_, bf16[384,512]{1,0:T(8,128)(2,1)S(1)} %collective-permute-done.4.refs_1_, f32[1536,640]{1,0:T(8,128)S(1)} %attend.9.refs_2_), custom_call_target="tpu_custom_call" | custom-call | flops 1024 | bytes 1024 | tf_op jit(solution)/shard_map/attend/pallas_call | solution.py:228
  47.7 0.0 collective-permute-done.8.refs_0_
  47.7 1.6 %collective-permute-start.9 = (bf16[384,512]{1,0:T(8,128)(2,1)S(1)}, bf16[384,512]{1,0:T(8,128)(2,1)S(1)}, u32[]{:S(2)}, u32[]{:S(2)}) collective-permute-start(bf16[384,512]{1,0:T(8,128)(2,1)S(1)} %collective-permute-done.8.refs_0_), channel_id=1, source_target_pairs={{0,16},{8,120},{16,32},{24,8},{32,48},{40,24},{48,64},{56,40},{64,... | collective-permute-start | bytes 1179656 | tf_op jit(solution)/shard_map/ppermute | solution.py:317
  49.2 0.0 collective-permute-done.11.refs_1_
  49.3 0.1 collective-permute-start.14
  49.3 3.3 %attend.11.refs_2_ = f32[1536,640]{1,0:T(8,128)S(1)} custom-call(bf16[1536,256]{1,0:T(8,128)(2,1)S(1)} %get-tuple-element.41.q_ref, bf16[384,512]{1,0:T(8,128)(2,1)S(1)} %collective-permute-done.8.refs_0_, bf16[384,512]{1,0:T(8,128)(2,1)S(1)} %collective-permute-done.11.refs_1_, f32[1536,640]{1,0:T(8,128)S(1)} %attend.10.refs_2_), custom_call_target="tpu_custom_call" | custom-call | flops 1024 | bytes 1024 | tf_op jit(solution)/shard_map/attend/pallas_call | solution.py:228
  52.7 0.0 collective-permute-done.10.refs_0_
  52.7 0.0 collective-permute-done.12.refs_1_
  52.7 3.3 %attend.12.refs_2_ = f32[1536,640]{1,0:T(8,128)S(1)} custom-call(bf16[1536,256]{1,0:T(8,128)(2,1)S(1)} %get-tuple-element.41.q_ref, bf16[384,512]{1,0:T(8,128)(2,1)S(1)} %collective-permute-done.10.refs_0_, bf16[384,512]{1,0:T(8,128)(2,1)S(1)} %collective-permute-done.12.refs_1_, f32[1536,640]{1,0:T(8,128)S(1)} %attend.11.refs_2_), custom_call_target="tpu_custom_call" | custom-call | flops 1024 | bytes 1024 | tf_op jit(solution)/shard_map/attend/pallas_call | solution.py:228
  56.0 0.0 collective-permute-done.9.refs_0_
  56.0 1.0 %collective-permute-start.13 = (bf16[384,512]{1,0:T(8,128)(2,1)S(1)}, bf16[384,512]{1,0:T(8,128)(2,1)S(1)}, u32[]{:S(2)}, u32[]{:S(2)}) collective-permute-start(bf16[384,512]{1,0:T(8,128)(2,1)S(1)} %collective-permute-done.9.refs_0_), channel_id=1, source_target_pairs={{0,16},{8,120},{16,32},{24,8},{32,48},{40,24},{48,64},{56,40},{64,... | collective-permute-start | bytes 1179656 | tf_op jit(solution)/shard_map/ppermute | solution.py:317
  57.1 1.8 %collective-permute-done.14.refs_1_ = bf16[384,512]{1,0:T(8,128)(2,1)S(1)} collective-permute-done((bf16[384,512]{1,0:T(8,128)(2,1)S(1)}, bf16[384,512]{1,0:T(8,128)(2,1)S(1)}, u32[]{:S(2)}, u32[]{:S(2)}) %collective-permute-start.14) | collective-permute-done | bytes 393248 | tf_op jit(solution)/shard_map/ppermute | solution.py:317
  58.9 2.4 %collective-permute-start.17 = (bf16[384,512]{1,0:T(8,128)(2,1)S(1)}, bf16[384,512]{1,0:T(8,128)(2,1)S(1)}, u32[]{:S(2)}, u32[]{:S(2)}) collective-permute-start(bf16[384,512]{1,0:T(8,128)(2,1)S(1)} %collective-permute-done.14.refs_1_), channel_id=1, source_target_pairs={{0,16},{8,120},{16,32},{24,8},{32,48},{40,24},{48,64},{56,40},{64,... | collective-permute-start | bytes 1179656 | tf_op jit(solution)/shard_map/ppermute | solution.py:317
  61.3 0.0 collective-permute-start.16
  61.3 3.3 %attend.13.refs_2_ = f32[1536,640]{1,0:T(8,128)S(1)} custom-call(bf16[1536,256]{1,0:T(8,128)(2,1)S(1)} %get-tuple-element.41.q_ref, bf16[384,512]{1,0:T(8,128)(2,1)S(1)} %collective-permute-done.9.refs_0_, bf16[384,512]{1,0:T(8,128)(2,1)S(1)} %collective-permute-done.14.refs_1_, f32[1536,640]{1,0:T(8,128)S(1)} %attend.12.refs_2_), custom_call_target="tpu_custom_call" | custom-call | flops 1024 | bytes 1024 | tf_op jit(solution)/shard_map/attend/pallas_call | solution.py:228
  64.7 0.0 collective-permute-done.13.refs_0_
  64.7 0.8 collective-permute-start.15
  65.5 1.8 %collective-permute-done.17.refs_1_ = bf16[384,512]{1,0:T(8,128)(2,1)S(1)} collective-permute-done((bf16[384,512]{1,0:T(8,128)(2,1)S(1)}, bf16[384,512]{1,0:T(8,128)(2,1)S(1)}, u32[]{:S(2)}, u32[]{:S(2)}) %collective-permute-start.17) | collective-permute-done | bytes 393248 | tf_op jit(solution)/shard_map/ppermute | solution.py:317
  67.3 3.3 %attend.14.refs_1_ = f32[1536,640]{1,0:T(8,128)S(1)} custom-call(bf16[1536,256]{1,0:T(8,128)(2,1)S(1)} %get-tuple-element.41.q_ref, bf16[384,512]{1,0:T(8,128)(2,1)S(1)} %collective-permute-done.13.refs_0_, bf16[384,512]{1,0:T(8,128)(2,1)S(1)} %collective-permute-done.17.refs_1_, f32[1536,640]{1,0:T(8,128)S(1)} %attend.13.refs_2_), custom_call_target="tpu_custom_call" | custom-call | flops 1024 | bytes 1024 | tf_op jit(solution)/shard_map/attend/pallas_call | solution.py:228
  70.6 0.9 collective-permute-done.16.refs_0_
  71.5 2.3 %attend.15.refs_1_ = f32[1536,640]{1,0:T(8,128)S(1)} custom-call(bf16[1536,256]{1,0:T(8,128)(2,1)S(1)} %get-tuple-element.41.q_ref, bf16[384,512]{1,0:T(8,128)(2,1)S(1)} %collective-permute-done.16.refs_0_, f32[1536,640]{1,0:T(8,128)S(1)} %attend.14.refs_1_), custom_call_target="tpu_custom_call" | custom-call | flops 1024 | bytes 1024 | tf_op jit(solution)/shard_map/attend/pallas_call | solution.py:228
  73.9 1.9 %collective-permute-done.15.refs_0_ = bf16[384,512]{1,0:T(8,128)(2,1)S(1)} collective-permute-done((bf16[384,512]{1,0:T(8,128)(2,1)S(1)}, bf16[384,512]{1,0:T(8,128)(2,1)S(1)}, u32[]{:S(2)}, u32[]{:S(2)}) %collective-permute-start.15) | collective-permute-done | bytes 393248 | tf_op jit(solution)/shard_map/ppermute | solution.py:317
  75.7 1.2 %attend.17 = (bf16[768,256]{1,0:T(8,128)(2,1)S(1)}, f32[768,128]{1,0:T(8,128)S(1)}) custom-call(bf16[1536,256]{1,0:T(8,128)(2,1)S(1)} %get-tuple-element.41.q_ref, bf16[384,512]{1,0:T(8,128)(2,1)S(1)} %collective-permute-done.15.refs_0_, f32[1536,640]{1,0:T(8,128)S(1)} %attend.15.refs_1_), custom_call_target="tpu_custom_call" | custom-call | flops 1024 | bytes 1024 | tf_op jit(solution)/shard_map/attend/pallas_call | solution.py:228
  77.0 3.8 %collective-permute-start.18 = (bf16[768,256]{1,0:T(8,128)(2,1)S(1)}, bf16[768,256]{1,0:T(8,128)(2,1)S(1)}, u32[]{:S(2)}, u32[]{:S(2)}) collective-permute-start(bf16[768,256]{1,0:T(8,128)(2,1)S(1)} %get-tuple-element.65), channel_id=1, source_target_pairs={{0,8},{8,0},{1,9},{9,1},{2,10},{10,2},{3,11},{11,3},{4,12},{12,4},... | collective-permute-start | bytes 1179656 | tf_op jit(solution)/shard_map/ppermute | solution.py:319
  80.8 0.1 collective-permute-start.19
  80.9 1.2 %attend.16 = (f32[768,256]{1,0:T(8,128)S(1)}, f32[768,128]{1,0:T(8,128)S(1)}) custom-call(bf16[1536,256]{1,0:T(8,128)(2,1)S(1)} %get-tuple-element.41.q_ref, bf16[384,512]{1,0:T(8,128)(2,1)S(1)} %collective-permute-done.15.refs_0_, f32[1536,640]{1,0:T(8,128)S(1)} %attend.15.refs_1_), custom_call_target="tpu_custom_call" | custom-call | flops 1024 | bytes 1024 | tf_op jit(solution)/shard_map/attend/pallas_call | solution.py:228
  82.1 0.0 collective-permute-done.18.other
  82.1 0.6 collective-permute-done.19.other_stat
  82.7 1.0 %join.1 = (f32[384,256]{1,0:T(8,128)S(1)}, bf16[384,256]{1,0:T(8,128)(2,1)S(1)}, f32[16,8,128]{2,1,0:T(8,128)S(1)}) custom-call(f32[768,256]{1,0:T(8,128)S(1)} %get-tuple-element.63.mine, f32[768,128]{1,0:T(8,128)S(1)} %get-tuple-element.64.mine_stat, bf16[768,256]{1,0:T(8,128)(2,1)S(1)} %collective-permute-done.18.other, ...), custom_call_target="tpu_custom_call" | custom-call | tf_op jit(solution)/shard_map/join/pallas_call | solution.py:272
  83.7 2.9 %collective-permute-start.20 = (bf16[384,256]{1,0:T(8,128)(2,1)S(1)}, bf16[384,256]{1,0:T(8,128)(2,1)S(1)}, u32[]{:S(2)}, u32[]{:S(2)}) collective-permute-start(bf16[384,256]{1,0:T(8,128)(2,1)S(1)} %get-tuple-element.68), channel_id=1, source_target_pairs={{0,128},{128,0},{1,129},{129,1},{2,130},{130,2},{3,131},{131,3},{4... | collective-permute-start | bytes 589832 | tf_op jit(solution)/shard_map/ppermute | solution.py:318
  86.6 10.9 %all_to_all.5.squares = f32[16,8,128]{2,1,0:T(8,128)S(1)} all-to-all(f32[16,8,128]{2,1,0:T(8,128)S(1)} %get-tuple-element.69), channel_id=1, replica_groups=mesh['yh'=2,'z'=8,'core'=2,'yl'=2,'x'=4] {'yh','yl','x'}, dimensions={0} | all-to-all | bytes 131072 | tf_op jit(solution)/shard_map/all_to_all | solution.py:363
  97.5 0.0 collective-permute-done.20.come
  97.5 1.2 %finish.1 = (bf16[384,256]{1,0:T(8,128)(2,1)}, bf16[384,256]{1,0:T(8,128)(2,1)}) custom-call(f32[384,256]{1,0:T(8,128)S(1)} %get-tuple-element.67.keep, bf16[384,256]{1,0:T(8,128)(2,1)S(1)} %collective-permute-done.20.come, f32[16,8,128]{2,1,0:T(8,128)S(1)} %all_to_all.5.squares), custom_call_target="tpu_custom_call" | custom-call | tf_op jit(solution)/shard_map/finish/pallas_call | solution.py:311
  (2 shorter events, 0.1 us)
Async XLA Ops:
  3.1 7.2 %collective-permute-start.2 = (bf16[384,512]{1,0:T(8,128)(2,1)}, bf16[384,512]{1,0:T(8,128)(2,1)S(1)}, u32[]{:S(2)}, u32[]{:S(2)}) collective-permute-start(bf16[384,512]{1,0:T(8,128)(2,1)} %get-tuple-element.36.own_kv), channel_id=1, source_target_pairs={{0,8},{8,0},{1,9},{9,1},{2,10},{10,2},{3,11},{11,3},{4,12},{12,4},... | collective-permute-start | bytes 1179656 | tf_op jit(solution)/shard_map/ppermute | solution.py:319
  6.4 8.9 %collective-permute-start = (bf16[384,512]{1,0:T(8,128)(2,1)}, bf16[384,512]{1,0:T(8,128)(2,1)S(1)}, u32[]{:S(2)}, u32[]{:S(2)}) collective-permute-start(bf16[384,512]{1,0:T(8,128)(2,1)} %get-tuple-element.36.own_kv), channel_id=1, source_target_pairs={{0,16},{8,120},{16,32},{24,8},{32,48},{40,24},{48,64},{56,40},{64,... | collective-permute-start | bytes 1179656 | tf_op jit(solution)/shard_map/ppermute | solution.py:317
  10.2 9.1 %collective-permute-start.3 = (bf16[384,512]{1,0:T(8,128)(2,1)S(1)}, bf16[384,512]{1,0:T(8,128)(2,1)S(1)}, u32[]{:S(2)}, u32[]{:S(2)}) collective-permute-start(bf16[384,512]{1,0:T(8,128)(2,1)S(1)} %collective-permute-done.2), channel_id=1, source_target_pairs={{0,16},{8,120},{16,32},{24,8},{32,48},{40,24},{48,64},{56,40},{64,... | collective-permute-start | bytes 1179656 | tf_op jit(solution)/shard_map/ppermute | solution.py:317
  11.8 14.0 %collective-permute-start.5 = (bf16[576,512]{1,0:T(8,128)(2,1)}, bf16[576,512]{1,0:T(8,128)(2,1)S(1)}, u32[]{:S(2)}, u32[]{:S(2)}) collective-permute-start(bf16[576,512]{1,0:T(8,128)(2,1)} %get-tuple-element.38), channel_id=1, source_target_pairs={{0,128},{128,0},{1,129},{129,1},{2,130},{130,2},{3,131},{131,3},{4... | collective-permute-start | bytes 1769480 | tf_op jit(solution)/shard_map/ppermute | solution.py:318
  15.3 10.5 %collective-permute-start.1 = (bf16[384,512]{1,0:T(8,128)(2,1)S(1)}, bf16[384,512]{1,0:T(8,128)(2,1)S(1)}, u32[]{:S(2)}, u32[]{:S(2)}) collective-permute-start(bf16[384,512]{1,0:T(8,128)(2,1)S(1)} %collective-permute-done.refs_0_), channel_id=1, source_target_pairs={{0,16},{8,120},{16,32},{24,8},{32,48},{40,24},{48,64},{56,40},{64,... | collective-permute-start | bytes 1179656 | tf_op jit(solution)/shard_map/ppermute | solution.py:317
  19.4 8.4 %collective-permute-start.4 = (bf16[384,512]{1,0:T(8,128)(2,1)S(1)}, bf16[384,512]{1,0:T(8,128)(2,1)S(1)}, u32[]{:S(2)}, u32[]{:S(2)}) collective-permute-start(bf16[384,512]{1,0:T(8,128)(2,1)S(1)} %collective-permute-done.3.refs_1_), channel_id=1, source_target_pairs={{0,16},{8,120},{16,32},{24,8},{32,48},{40,24},{48,64},{56,40},{64,... | collective-permute-start | bytes 1179656 | tf_op jit(solution)/shard_map/ppermute | solution.py:317
  22.8 1.7 %collective-permute-start.6 = (bf16[384,256]{1,0:T(8,128)(2,1)}, bf16[384,256]{1,0:T(8,128)(2,1)S(1)}, u32[]{:S(2)}, u32[]{:S(2)}) collective-permute-start(bf16[384,256]{1,0:T(8,128)(2,1)} %get-tuple-element.37.own_q), channel_id=1, source_target_pairs={{0,8},{8,0},{1,9},{9,1},{2,10},{10,2},{3,11},{11,3},{4,12},{12,4},... | collective-permute-start | bytes 589832 | tf_op jit(solution)/shard_map/ppermute | solution.py:319
  27.8 3.6 %collective-permute-start.7 = (bf16[576,512]{1,0:T(8,128)(2,1)S(1)}, bf16[576,512]{1,0:T(8,128)(2,1)S(1)}, u32[]{:S(2)}, u32[]{:S(2)}) collective-permute-start(bf16[576,512]{1,0:T(8,128)(2,1)S(1)} %collective-permute-done.5.peer), channel_id=1, source_target_pairs={{0,8},{8,0},{1,9},{9,1},{2,10},{10,2},{3,11},{11,3},{4,12},{12,4},... | collective-permute-start | bytes 1769480 | tf_op jit(solution)/shard_map/ppermute | solution.py:319
  29.8 17.9 %collective-permute-start.8 = (bf16[384,512]{1,0:T(8,128)(2,1)S(1)}, bf16[384,512]{1,0:T(8,128)(2,1)S(1)}, u32[]{:S(2)}, u32[]{:S(2)}) collective-permute-start(bf16[384,512]{1,0:T(8,128)(2,1)S(1)} %slice.6), channel_id=1, source_target_pairs={{0,16},{8,120},{16,32},{24,8},{32,48},{40,24},{48,64},{56,40},{64,... | collective-permute-start | bytes 1179656 | tf_op jit(solution)/shard_map/ppermute | solution.py:317
  31.4 17.8 %collective-permute-start.11 = (bf16[384,512]{1,0:T(8,128)(2,1)S(1)}, bf16[384,512]{1,0:T(8,128)(2,1)S(1)}, u32[]{:S(2)}, u32[]{:S(2)}) collective-permute-start(bf16[384,512]{1,0:T(8,128)(2,1)S(1)} %slice.8), channel_id=1, source_target_pairs={{0,16},{8,120},{16,32},{24,8},{32,48},{40,24},{48,64},{56,40},{64,... | collective-permute-start | bytes 1179656 | tf_op jit(solution)/shard_map/ppermute | solution.py:317
  33.0 19.7 %collective-permute-start.10 = (bf16[384,512]{1,0:T(8,128)(2,1)S(1)}, bf16[384,512]{1,0:T(8,128)(2,1)S(1)}, u32[]{:S(2)}, u32[]{:S(2)}) collective-permute-start(bf16[384,512]{1,0:T(8,128)(2,1)S(1)} %collective-permute-done.1.refs_0_), channel_id=1, source_target_pairs={{0,16},{8,120},{16,32},{24,8},{32,48},{40,24},{48,64},{56,40},{64,... | collective-permute-start | bytes 1179656 | tf_op jit(solution)/shard_map/ppermute | solution.py:317
  33.4 19.3 %collective-permute-start.12 = (bf16[384,512]{1,0:T(8,128)(2,1)S(1)}, bf16[384,512]{1,0:T(8,128)(2,1)S(1)}, u32[]{:S(2)}, u32[]{:S(2)}) collective-permute-start(bf16[384,512]{1,0:T(8,128)(2,1)S(1)} %collective-permute-done.4.refs_1_), channel_id=1, source_target_pairs={{0,16},{8,120},{16,32},{24,8},{32,48},{40,24},{48,64},{56,40},{64,... | collective-permute-start | bytes 1179656 | tf_op jit(solution)/shard_map/ppermute | solution.py:317
  35.1 1.0 %copy-start = (bf16[384,512]{1,0:T(8,128)(2,1)S(1)}, bf16[384,512]{1,0:T(8,128)(2,1)}, u32[]{:S(2)}) copy-start(bf16[384,512]{1,0:T(8,128)(2,1)} %get-tuple-element.36.own_kv) | copy-start | bytes 1179652
  36.1 0.9 copy-start.1
  47.7 8.4 %collective-permute-start.9 = (bf16[384,512]{1,0:T(8,128)(2,1)S(1)}, bf16[384,512]{1,0:T(8,128)(2,1)S(1)}, u32[]{:S(2)}, u32[]{:S(2)}) collective-permute-start(bf16[384,512]{1,0:T(8,128)(2,1)S(1)} %collective-permute-done.8.refs_0_), channel_id=1, source_target_pairs={{0,16},{8,120},{16,32},{24,8},{32,48},{40,24},{48,64},{56,40},{64,... | collective-permute-start | bytes 1179656 | tf_op jit(solution)/shard_map/ppermute | solution.py:317
  49.3 9.6 %collective-permute-start.14 = (bf16[384,512]{1,0:T(8,128)(2,1)S(1)}, bf16[384,512]{1,0:T(8,128)(2,1)S(1)}, u32[]{:S(2)}, u32[]{:S(2)}) collective-permute-start(bf16[384,512]{1,0:T(8,128)(2,1)S(1)} %collective-permute-done.11.refs_1_), channel_id=1, source_target_pairs={{0,16},{8,120},{16,32},{24,8},{32,48},{40,24},{48,64},{56,40},{64,... | collective-permute-start | bytes 1179656 | tf_op jit(solution)/shard_map/ppermute | solution.py:317
  56.0 8.6 %collective-permute-start.13 = (bf16[384,512]{1,0:T(8,128)(2,1)S(1)}, bf16[384,512]{1,0:T(8,128)(2,1)S(1)}, u32[]{:S(2)}, u32[]{:S(2)}) collective-permute-start(bf16[384,512]{1,0:T(8,128)(2,1)S(1)} %collective-permute-done.9.refs_0_), channel_id=1, source_target_pairs={{0,16},{8,120},{16,32},{24,8},{32,48},{40,24},{48,64},{56,40},{64,... | collective-permute-start | bytes 1179656 | tf_op jit(solution)/shard_map/ppermute | solution.py:317
  58.9 8.4 %collective-permute-start.17 = (bf16[384,512]{1,0:T(8,128)(2,1)S(1)}, bf16[384,512]{1,0:T(8,128)(2,1)S(1)}, u32[]{:S(2)}, u32[]{:S(2)}) collective-permute-start(bf16[384,512]{1,0:T(8,128)(2,1)S(1)} %collective-permute-done.14.refs_1_), channel_id=1, source_target_pairs={{0,16},{8,120},{16,32},{24,8},{32,48},{40,24},{48,64},{56,40},{64,... | collective-permute-start | bytes 1179656 | tf_op jit(solution)/shard_map/ppermute | solution.py:317
  61.3 10.2 %collective-permute-start.16 = (bf16[384,512]{1,0:T(8,128)(2,1)S(1)}, bf16[384,512]{1,0:T(8,128)(2,1)S(1)}, u32[]{:S(2)}, u32[]{:S(2)}) collective-permute-start(bf16[384,512]{1,0:T(8,128)(2,1)S(1)} %collective-permute-done.10.refs_0_), channel_id=1, source_target_pairs={{0,16},{8,120},{16,32},{24,8},{32,48},{40,24},{48,64},{56,40},{64,... | collective-permute-start | bytes 1179656 | tf_op jit(solution)/shard_map/ppermute | solution.py:317
  64.7 11.0 %collective-permute-start.15 = (bf16[384,512]{1,0:T(8,128)(2,1)S(1)}, bf16[384,512]{1,0:T(8,128)(2,1)S(1)}, u32[]{:S(2)}, u32[]{:S(2)}) collective-permute-start(bf16[384,512]{1,0:T(8,128)(2,1)S(1)} %collective-permute-done.13.refs_0_), channel_id=1, source_target_pairs={{0,16},{8,120},{16,32},{24,8},{32,48},{40,24},{48,64},{56,40},{64,... | collective-permute-start | bytes 1179656 | tf_op jit(solution)/shard_map/ppermute | solution.py:317
  77.0 5.2 %collective-permute-start.18 = (bf16[768,256]{1,0:T(8,128)(2,1)S(1)}, bf16[768,256]{1,0:T(8,128)(2,1)S(1)}, u32[]{:S(2)}, u32[]{:S(2)}) collective-permute-start(bf16[768,256]{1,0:T(8,128)(2,1)S(1)} %get-tuple-element.65), channel_id=1, source_target_pairs={{0,8},{8,0},{1,9},{9,1},{2,10},{10,2},{3,11},{11,3},{4,12},{12,4},... | collective-permute-start | bytes 1179656 | tf_op jit(solution)/shard_map/ppermute | solution.py:319
  80.8 1.9 %collective-permute-start.19 = (f32[768,128]{1,0:T(8,128)S(1)}, f32[768,128]{1,0:T(8,128)S(1)}, u32[]{:S(2)}, u32[]{:S(2)}) collective-permute-start(f32[768,128]{1,0:T(8,128)S(1)} %get-tuple-element.66), channel_id=1, source_target_pairs={{0,8},{8,0},{1,9},{9,1},{2,10},{10,2},{3,11},{11,3},{4,12},{12,4},... | collective-permute-start | bytes 1179656 | tf_op jit(solution)/shard_map/ppermute | solution.py:319
  83.7 13.9 %collective-permute-start.20 = (bf16[384,256]{1,0:T(8,128)(2,1)S(1)}, bf16[384,256]{1,0:T(8,128)(2,1)S(1)}, u32[]{:S(2)}, u32[]{:S(2)}) collective-permute-start(bf16[384,256]{1,0:T(8,128)(2,1)S(1)} %get-tuple-element.68), channel_id=1, source_target_pairs={{0,128},{128,0},{1,129},{129,1},{2,130},{130,2},{3,131},{131,3},{4... | collective-permute-start | bytes 589832 | tf_op jit(solution)/shard_map/ppermute | solution.py:318

commit v4 on v3

--- a/solution.py
+++ b/solution.py
@@ -325,11 +325,13 @@
     core_kv = over_core(own_kv)
     near = [hop(own_kv), hop(core_kv)]
     core_q = over_core(own_q)
+    near[0], core_q = after(near[0], core_q)
     near_next = [hop(a) for a in near]
-    near_next[0], near_next[1], peer, core_q = lax.optimization_barrier((*near_next, peer, core_q))
+    first, peer = after(near_next[0], peer)
     peer_core = over_core(peer)
-    far = [hop(peer[:tokens]), hop(peer_core[:tokens])]
-    near_three = [hop(a) for a in near_next]
+    second, peer_kv = after(near_next[1], peer[:tokens])
+    near_three = [hop(first), hop(second)]
+    far = [hop(peer_kv), hop(peer_core[:tokens])]
     state, query = begin(own_kv, own_q, core_q, peer, peer_core)
 
     def turn(pair, state, count):

time: 99 us -> 98.8 us (level)
    ppermute x2, waiting for transfers between devices: 1.37 us -> 3.55 us  [on_device(): over_y = lambda a: lax.ppermute(a, 'yh', SWAP)]
    ppermute x5, waiting for transfers between devices: 2.59 us -> 0.6 us  [on_device(): over_core = lambda a: lax.ppermute(a, 'core', SWAP)]
    ppermute x5, starting transfers between devices: 9.23 us -> 10.5 us  [on_device(): over_core = lambda a: lax.ppermute(a, 'core', SWAP)]
  transfers between devices with their start and end apart: 21 -> 21, of which waited for: 11 -> 9; matrix products, arithmetic and copies ran while one was open for 0% -> 0% of each run, Pallas kernels for 28% -> 28%
where the time goes in v4:
time: 98.8 us; the launch traced here: 98.6 us
  starting transfers between devices  38.7 us (39%)
  Pallas kernels  33.2 us (34%)
  waiting for transfers between devices  13 us (13%)
  blocking collectives  10.9 us (11%)
  local copies, waits for them, and re-layouts  1.97 us (2%)
    pallas_call x9, Pallas kernels, attend(): pl.pallas_call(functools.partial(attend_kernel, len(kvs), base, kind is n...  24.9 us
    ppermute x14, starting transfers between devices, on_device(): hop = lambda a: lax.ppermute(a, ('z', 'core'), hop_pairs)  22.4 us
    all_to_all x1, blocking collectives, on_device(): squares = lax.all_to_all(squares, ('yh', 'yl', 'x'), 0, 0, tiled=True)  10.9 us
    ppermute x5, starting transfers between devices, on_device(): over_core = lambda a: lax.ppermute(a, 'core', SWAP)  10.5 us
    ppermute x14, waiting for transfers between devices, on_device(): hop = lambda a: lax.ppermute(a, ('z', 'core'), hop_pairs)  8.86 us
    ppermute x2, starting transfers between devices, on_device(): over_y = lambda a: lax.ppermute(a, 'yh', SWAP)  5.81 us
    pallas_call x1, Pallas kernels, begin(): pl.pallas_call(begin_kernel, out_shape=[jax.ShapeDtypeStruct((rows, 5 * D...  3.74 us
    ppermute x2, waiting for transfers between devices, on_device(): over_y = lambda a: lax.ppermute(a, 'yh', SWAP)  3.55 us
  transfers between devices with their start and end apart: 21, of which 9 were waited for; matrix products, arithmetic and copies ran while one was open for 0% of the time, Pallas kernels for 28%

profile of v4, /device:TPU:1, one launch (start us, length us, event | category | flops | bytes accessed | tf_op | source)
XLA Modules:
  0.0 98.6 jit_solution(9129820254494598826)
XLA Ops:
  0.6 2.4 %pack.1 = (bf16[384,512]{1,0:T(8,128)(2,1)}, bf16[384,256]{1,0:T(8,128)(2,1)}, bf16[576,512]{1,0:T(8,128)(2,1)}) custom-call(bf16[384,256]{1,0:T(8,128)(2,1)} %q.1, bf16[384,256]{1,0:T(8,128)(2,1)} %k.1, bf16[384,256]{1,0:T(8,128)(2,1)} %v.1, bf16[384,256]{1,0:T(8,128)(2,1)} %qt.1, bf16[384,256]{1,0:T(8,128)(2,1)} %kt.1, bf16[384,256]{1,0:T(8,128)(2,1)} %vt.1), custom_call_target="tpu_custom_call" | custom-call | bytes 2359296 | tf_op jit(solution)/shard_map/pack/pallas_call | solution.py:58
  3.1 3.3 %collective-permute-start.5 = (bf16[384,512]{1,0:T(8,128)(2,1)}, bf16[384,512]{1,0:T(8,128)(2,1)S(1)}, u32[]{:S(2)}, u32[]{:S(2)}) collective-permute-start(bf16[384,512]{1,0:T(8,128)(2,1)} %get-tuple-element.38.own_kv), channel_id=1, source_target_pairs={{0,8},{8,0},{1,9},{9,1},{2,10},{10,2},{3,11},{11,3},{4,12},{12,4},... | collective-permute-start | bytes 1179656 | tf_op jit(solution)/shard_map/ppermute | solution.py:319
  6.4 3.8 %collective-permute-start = (bf16[384,512]{1,0:T(8,128)(2,1)}, bf16[384,512]{1,0:T(8,128)(2,1)S(1)}, u32[]{:S(2)}, u32[]{:S(2)}) collective-permute-start(bf16[384,512]{1,0:T(8,128)(2,1)} %get-tuple-element.38.own_kv), channel_id=1, source_target_pairs={{0,16},{8,120},{16,32},{24,8},{32,48},{40,24},{48,64},{56,40},{64,... | collective-permute-start | bytes 1179656 | tf_op jit(solution)/shard_map/ppermute | solution.py:317
  10.2 0.0 collective-permute-start.1
  10.2 2.9 %collective-permute-start.3 = (bf16[576,512]{1,0:T(8,128)(2,1)}, bf16[576,512]{1,0:T(8,128)(2,1)S(1)}, u32[]{:S(2)}, u32[]{:S(2)}) collective-permute-start(bf16[576,512]{1,0:T(8,128)(2,1)} %get-tuple-element.42), channel_id=1, source_target_pairs={{0,128},{128,0},{1,129},{129,1},{2,130},{130,2},{3,131},{131,3},{4... | collective-permute-start | bytes 1769480 | tf_op jit(solution)/shard_map/ppermute | solution.py:318
  13.1 0.0 collective-permute-done.5
  13.2 0.7 collective-permute-start.6
  13.9 0.0 collective-permute-done.1.core_q
  13.9 1.4 %collective-permute-done.refs_0_ = bf16[384,512]{1,0:T(8,128)(2,1)S(1)} collective-permute-done((bf16[384,512]{1,0:T(8,128)(2,1)}, bf16[384,512]{1,0:T(8,128)(2,1)S(1)}, u32[]{:S(2)}, u32[]{:S(2)}) %collective-permute-start) | collective-permute-done | bytes 393248 | tf_op jit(solution)/shard_map/ppermute | solution.py:317
  15.3 3.3 %collective-permute-start.2 = (bf16[384,512]{1,0:T(8,128)(2,1)S(1)}, bf16[384,512]{1,0:T(8,128)(2,1)S(1)}, u32[]{:S(2)}, u32[]{:S(2)}) collective-permute-start(bf16[384,512]{1,0:T(8,128)(2,1)S(1)} %collective-permute-done.refs_0_), channel_id=1, source_target_pairs={{0,16},{8,120},{16,32},{24,8},{32,48},{40,24},{48,64},{56,40},{64,... | collective-permute-start | bytes 1179656 | tf_op jit(solution)/shard_map/ppermute | solution.py:317
  18.6 1.5 %collective-permute-done.6.refs_1_ = bf16[384,512]{1,0:T(8,128)(2,1)S(1)} collective-permute-done((bf16[384,512]{1,0:T(8,128)(2,1)S(1)}, bf16[384,512]{1,0:T(8,128)(2,1)S(1)}, u32[]{:S(2)}, u32[]{:S(2)}) %collective-permute-start.6) | collective-permute-done | bytes 393248 | tf_op jit(solution)/shard_map/ppermute | solution.py:317
  20.1 2.7 %collective-permute-start.7 = (bf16[384,512]{1,0:T(8,128)(2,1)S(1)}, bf16[384,512]{1,0:T(8,128)(2,1)S(1)}, u32[]{:S(2)}, u32[]{:S(2)}) collective-permute-start(bf16[384,512]{1,0:T(8,128)(2,1)S(1)} %collective-permute-done.6.refs_1_), channel_id=1, source_target_pairs={{0,16},{8,120},{16,32},{24,8},{32,48},{40,24},{48,64},{56,40},{64,... | collective-permute-start | bytes 1179656 | tf_op jit(solution)/shard_map/ppermute | solution.py:317
  22.8 3.5 %collective-permute-done.3.peer = bf16[576,512]{1,0:T(8,128)(2,1)S(1)} collective-permute-done((bf16[576,512]{1,0:T(8,128)(2,1)}, bf16[576,512]{1,0:T(8,128)(2,1)S(1)}, u32[]{:S(2)}, u32[]{:S(2)}) %collective-permute-start.3) | collective-permute-done | bytes 589856 | tf_op jit(solution)/shard_map/ppermute | solution.py:318
  26.3 0.0 collective-permute-done.2.refs_0_
  26.3 1.4 %collective-permute-start.4 = (bf16[576,512]{1,0:T(8,128)(2,1)S(1)}, bf16[576,512]{1,0:T(8,128)(2,1)S(1)}, u32[]{:S(2)}, u32[]{:S(2)}) collective-permute-start(bf16[576,512]{1,0:T(8,128)(2,1)S(1)} %collective-permute-done.3.peer), channel_id=1, source_target_pairs={{0,8},{8,0},{1,9},{9,1},{2,10},{10,2},{3,11},{11,3},{4,12},{12,4},... | collective-permute-start | bytes 1769480 | tf_op jit(solution)/shard_map/ppermute | solution.py:319
  27.7 0.8 collective-permute-done.7.refs_1_
  28.5 2.4 %collective-permute-start.8 = (bf16[384,512]{1,0:T(8,128)(2,1)S(1)}, bf16[384,512]{1,0:T(8,128)(2,1)S(1)}, u32[]{:S(2)}, u32[]{:S(2)}) collective-permute-start(bf16[384,512]{1,0:T(8,128)(2,1)S(1)} %slice.6), channel_id=1, source_target_pairs={{0,16},{8,120},{16,32},{24,8},{32,48},{40,24},{48,64},{56,40},{64,... | collective-permute-start | bytes 1179656 | tf_op jit(solution)/shard_map/ppermute | solution.py:317
  30.9 0.0 collective-permute-done.4.peer_core
  31.0 0.1 collective-permute-start.11
  31.0 0.5 collective-permute-start.10
  31.6 0.7 collective-permute-start.12
  32.3 0.0 copy-start
  32.3 1.0 %copy-done = bf16[384,512]{1,0:T(8,128)(2,1)S(1)} copy-done((bf16[384,512]{1,0:T(8,128)(2,1)S(1)}, bf16[384,512]{1,0:T(8,128)(2,1)}, u32[]{:S(2)}) %copy-start) | copy-done | bytes 393240
  33.3 0.0 copy-start.1
  33.3 0.9 copy-done.1
  34.2 3.7 %begin.1 = (f32[1536,640]{1,0:T(8,128)S(1)}, bf16[1536,256]{1,0:T(8,128)(2,1)S(1)}) custom-call(bf16[384,512]{1,0:T(8,128)(2,1)S(1)} %copy-done, bf16[384,256]{1,0:T(8,128)(2,1)S(1)} %copy-done.1, bf16[384,256]{1,0:T(8,128)(2,1)S(1)} %collective-permute-done.1.core_q, bf16[576,512]{1,0:T(8,128)(2,1)S(1)} %collective-permute-done.3.peer, ...), custom_call_target="tpu_custom_call" | custom-call | flops 1024 | bytes 1024 | tf_op jit(solution)/shard_map/begin/pallas_call | solution.py:208
  38.0 3.5 %attend.9.refs_2_ = f32[1536,640]{1,0:T(8,128)S(1)} custom-call(bf16[1536,256]{1,0:T(8,128)(2,1)S(1)} %get-tuple-element.44.q_ref, bf16[384,512]{1,0:T(8,128)(2,1)S(1)} %collective-permute-done.refs_0_, bf16[384,512]{1,0:T(8,128)(2,1)S(1)} %collective-permute-done.6.refs_1_, f32[1536,640]{1,0:T(8,128)S(1)} %get-tuple-element.46.refs_2_), custom_call_target="tpu_custom_call" | custom-call | flops 1024 | bytes 1024 | tf_op jit(solution)/shard_map/attend/pallas_call | solution.py:228
  41.5 3.3 %attend.10.refs_2_ = f32[1536,640]{1,0:T(8,128)S(1)} custom-call(bf16[1536,256]{1,0:T(8,128)(2,1)S(1)} %get-tuple-element.44.q_ref, bf16[384,512]{1,0:T(8,128)(2,1)S(1)} %collective-permute-done.2.refs_0_, bf16[384,512]{1,0:T(8,128)(2,1)S(1)} %collective-permute-done.7.refs_1_, f32[1536,640]{1,0:T(8,128)S(1)} %attend.9.refs_2_), custom_call_target="tpu_custom_call" | custom-call | flops 1024 | bytes 1024 | tf_op jit(solution)/shard_map/attend/pallas_call | solution.py:228
  44.8 0.0 collective-permute-done.8.refs_0_
  44.8 2.5 %collective-permute-start.9 = (bf16[384,512]{1,0:T(8,128)(2,1)S(1)}, bf16[384,512]{1,0:T(8,128)(2,1)S(1)}, u32[]{:S(2)}, u32[]{:S(2)}) collective-permute-start(bf16[384,512]{1,0:T(8,128)(2,1)S(1)} %collective-permute-done.8.refs_0_), channel_id=1, source_target_pairs={{0,16},{8,120},{16,32},{24,8},{32,48},{40,24},{48,64},{56,40},{64,... | collective-permute-start | bytes 1179656 | tf_op jit(solution)/shard_map/ppermute | solution.py:317
  47.4 0.0 collective-permute-done.11.refs_1_
  47.4 0.1 collective-permute-start.14
  47.5 3.3 %attend.11.refs_2_ = f32[1536,640]{1,0:T(8,128)S(1)} custom-call(bf16[1536,256]{1,0:T(8,128)(2,1)S(1)} %get-tuple-element.44.q_ref, bf16[384,512]{1,0:T(8,128)(2,1)S(1)} %collective-permute-done.8.refs_0_, bf16[384,512]{1,0:T(8,128)(2,1)S(1)} %collective-permute-done.11.refs_1_, f32[1536,640]{1,0:T(8,128)S(1)} %attend.10.refs_2_), custom_call_target="tpu_custom_call" | custom-call | flops 1024 | bytes 1024 | tf_op jit(solution)/shard_map/attend/pallas_call | solution.py:228
  50.8 0.0 collective-permute-done.10.refs_0_
  50.8 0.0 collective-permute-done.12.refs_1_
  50.8 3.3 %attend.12.refs_2_ = f32[1536,640]{1,0:T(8,128)S(1)} custom-call(bf16[1536,256]{1,0:T(8,128)(2,1)S(1)} %get-tuple-element.44.q_ref, bf16[384,512]{1,0:T(8,128)(2,1)S(1)} %collective-permute-done.10.refs_0_, bf16[384,512]{1,0:T(8,128)(2,1)S(1)} %collective-permute-done.12.refs_1_, f32[1536,640]{1,0:T(8,128)S(1)} %attend.11.refs_2_), custom_call_target="tpu_custom_call" | custom-call | flops 1024 | bytes 1024 | tf_op jit(solution)/shard_map/attend/pallas_call | solution.py:228
  54.1 0.0 collective-permute-done.9.refs_0_
  54.2 1.4 %collective-permute-start.13 = (bf16[384,512]{1,0:T(8,128)(2,1)S(1)}, bf16[384,512]{1,0:T(8,128)(2,1)S(1)}, u32[]{:S(2)}, u32[]{:S(2)}) collective-permute-start(bf16[384,512]{1,0:T(8,128)(2,1)S(1)} %collective-permute-done.9.refs_0_), channel_id=1, source_target_pairs={{0,16},{8,120},{16,32},{24,8},{32,48},{40,24},{48,64},{56,40},{64,... | collective-permute-start | bytes 1179656 | tf_op jit(solution)/shard_map/ppermute | solution.py:317
  55.6 1.1 %collective-permute-done.14.refs_1_ = bf16[384,512]{1,0:T(8,128)(2,1)S(1)} collective-permute-done((bf16[384,512]{1,0:T(8,128)(2,1)S(1)}, bf16[384,512]{1,0:T(8,128)(2,1)S(1)}, u32[]{:S(2)}, u32[]{:S(2)}) %collective-permute-start.14) | collective-permute-done | bytes 393248 | tf_op jit(solution)/shard_map/ppermute | solution.py:317
  56.7 3.1 %collective-permute-start.17 = (bf16[384,512]{1,0:T(8,128)(2,1)S(1)}, bf16[384,512]{1,0:T(8,128)(2,1)S(1)}, u32[]{:S(2)}, u32[]{:S(2)}) collective-permute-start(bf16[384,512]{1,0:T(8,128)(2,1)S(1)} %collective-permute-done.14.refs_1_), channel_id=1, source_target_pairs={{0,16},{8,120},{16,32},{24,8},{32,48},{40,24},{48,64},{56,40},{64,... | collective-permute-start | bytes 1179656 | tf_op jit(solution)/shard_map/ppermute | solution.py:317
  59.8 0.0 collective-permute-start.16
  59.9 3.3 %attend.13.refs_2_ = f32[1536,640]{1,0:T(8,128)S(1)} custom-call(bf16[1536,256]{1,0:T(8,128)(2,1)S(1)} %get-tuple-element.44.q_ref, bf16[384,512]{1,0:T(8,128)(2,1)S(1)} %collective-permute-done.9.refs_0_, bf16[384,512]{1,0:T(8,128)(2,1)S(1)} %collective-permute-done.14.refs_1_, f32[1536,640]{1,0:T(8,128)S(1)} %attend.12.refs_2_), custom_call_target="tpu_custom_call" | custom-call | flops 1024 | bytes 1024 | tf_op jit(solution)/shard_map/attend/pallas_call | solution.py:228
  63.2 0.0 collective-permute-done.13.refs_0_
  63.2 0.8 collective-permute-start.15
  64.0 1.3 %collective-permute-done.17.refs_1_ = bf16[384,512]{1,0:T(8,128)(2,1)S(1)} collective-permute-done((bf16[384,512]{1,0:T(8,128)(2,1)S(1)}, bf16[384,512]{1,0:T(8,128)(2,1)S(1)}, u32[]{:S(2)}, u32[]{:S(2)}) %collective-permute-start.17) | collective-permute-done | bytes 393248 | tf_op jit(solution)/shard_map/ppermute | solution.py:317
  65.4 3.3 %attend.14.refs_1_ = f32[1536,640]{1,0:T(8,128)S(1)} custom-call(bf16[1536,256]{1,0:T(8,128)(2,1)S(1)} %get-tuple-element.44.q_ref, bf16[384,512]{1,0:T(8,128)(2,1)S(1)} %collective-permute-done.13.refs_0_, bf16[384,512]{1,0:T(8,128)(2,1)S(1)} %collective-permute-done.17.refs_1_, f32[1536,640]{1,0:T(8,128)S(1)} %attend.13.refs_2_), custom_call_target="tpu_custom_call" | custom-call | flops 1024 | bytes 1024 | tf_op jit(solution)/shard_map/attend/pallas_call | solution.py:228
  68.7 0.9 collective-permute-done.16.refs_0_
  69.6 2.3 %attend.15.refs_1_ = f32[1536,640]{1,0:T(8,128)S(1)} custom-call(bf16[1536,256]{1,0:T(8,128)(2,1)S(1)} %get-tuple-element.44.q_ref, bf16[384,512]{1,0:T(8,128)(2,1)S(1)} %collective-permute-done.16.refs_0_, f32[1536,640]{1,0:T(8,128)S(1)} %attend.14.refs_1_), custom_call_target="tpu_custom_call" | custom-call | flops 1024 | bytes 1024 | tf_op jit(solution)/shard_map/attend/pallas_call | solution.py:228
  71.9 1.9 %collective-permute-done.15.refs_0_ = bf16[384,512]{1,0:T(8,128)(2,1)S(1)} collective-permute-done((bf16[384,512]{1,0:T(8,128)(2,1)S(1)}, bf16[384,512]{1,0:T(8,128)(2,1)S(1)}, u32[]{:S(2)}, u32[]{:S(2)}) %collective-permute-start.15) | collective-permute-done | bytes 393248 | tf_op jit(solution)/shard_map/ppermute | solution.py:317
  73.8 1.2 %attend.17 = (bf16[768,256]{1,0:T(8,128)(2,1)S(1)}, f32[768,128]{1,0:T(8,128)S(1)}) custom-call(bf16[1536,256]{1,0:T(8,128)(2,1)S(1)} %get-tuple-element.44.q_ref, bf16[384,512]{1,0:T(8,128)(2,1)S(1)} %collective-permute-done.15.refs_0_, f32[1536,640]{1,0:T(8,128)S(1)} %attend.15.refs_1_), custom_call_target="tpu_custom_call" | custom-call | flops 1024 | bytes 1024 | tf_op jit(solution)/shard_map/attend/pallas_call | solution.py:228
  75.0 5.7 %collective-permute-start.18 = (bf16[768,256]{1,0:T(8,128)(2,1)S(1)}, bf16[768,256]{1,0:T(8,128)(2,1)S(1)}, u32[]{:S(2)}, u32[]{:S(2)}) collective-permute-start(bf16[768,256]{1,0:T(8,128)(2,1)S(1)} %get-tuple-element.69), channel_id=1, source_target_pairs={{0,8},{8,0},{1,9},{9,1},{2,10},{10,2},{3,11},{11,3},{4,12},{12,4},... | collective-permute-start | bytes 1179656 | tf_op jit(solution)/shard_map/ppermute | solution.py:319
  80.7 0.1 collective-permute-start.19
  80.8 1.2 %attend.16 = (f32[768,256]{1,0:T(8,128)S(1)}, f32[768,128]{1,0:T(8,128)S(1)}) custom-call(bf16[1536,256]{1,0:T(8,128)(2,1)S(1)} %get-tuple-element.44.q_ref, bf16[384,512]{1,0:T(8,128)(2,1)S(1)} %collective-permute-done.15.refs_0_, f32[1536,640]{1,0:T(8,128)S(1)} %attend.15.refs_1_), custom_call_target="tpu_custom_call" | custom-call | flops 1024 | bytes 1024 | tf_op jit(solution)/shard_map/attend/pallas_call | solution.py:228
  82.0 0.0 collective-permute-done.18.other
  82.0 0.6 collective-permute-done.19.other_stat
  82.6 1.0 %join.1 = (f32[384,256]{1,0:T(8,128)S(1)}, bf16[384,256]{1,0:T(8,128)(2,1)S(1)}, f32[16,8,128]{2,1,0:T(8,128)S(1)}) custom-call(f32[768,256]{1,0:T(8,128)S(1)} %get-tuple-element.67.mine, f32[768,128]{1,0:T(8,128)S(1)} %get-tuple-element.68.mine_stat, bf16[768,256]{1,0:T(8,128)(2,1)S(1)} %collective-permute-done.18.other, ...), custom_call_target="tpu_custom_call" | custom-call | tf_op jit(solution)/shard_map/join/pallas_call | solution.py:272
  83.6 2.9 %collective-permute-start.20 = (bf16[384,256]{1,0:T(8,128)(2,1)S(1)}, bf16[384,256]{1,0:T(8,128)(2,1)S(1)}, u32[]{:S(2)}, u32[]{:S(2)}) collective-permute-start(bf16[384,256]{1,0:T(8,128)(2,1)S(1)} %get-tuple-element.72), channel_id=1, source_target_pairs={{0,128},{128,0},{1,129},{129,1},{2,130},{130,2},{3,131},{131,3},{4... | collective-permute-start | bytes 589832 | tf_op jit(solution)/shard_map/ppermute | solution.py:318
  86.5 10.9 %all_to_all.5.squares = f32[16,8,128]{2,1,0:T(8,128)S(1)} all-to-all(f32[16,8,128]{2,1,0:T(8,128)S(1)} %get-tuple-element.73), channel_id=1, replica_groups=mesh['yh'=2,'z'=8,'core'=2,'yl'=2,'x'=4] {'yh','yl','x'}, dimensions={0} | all-to-all | bytes 131072 | tf_op jit(solution)/shard_map/all_to_all | solution.py:365
  97.4 0.0 collective-permute-done.20.come
  97.4 1.2 %finish.1 = (bf16[384,256]{1,0:T(8,128)(2,1)}, bf16[384,256]{1,0:T(8,128)(2,1)}) custom-call(f32[384,256]{1,0:T(8,128)S(1)} %get-tuple-element.71.keep, bf16[384,256]{1,0:T(8,128)(2,1)S(1)} %collective-permute-done.20.come, f32[16,8,128]{2,1,0:T(8,128)S(1)} %all_to_all.5.squares), custom_call_target="tpu_custom_call" | custom-call | tf_op jit(solution)/shard_map/finish/pallas_call | solution.py:311
  (2 shorter events, 0.1 us)
Async XLA Ops:
  3.1 10.1 %collective-permute-start.5 = (bf16[384,512]{1,0:T(8,128)(2,1)}, bf16[384,512]{1,0:T(8,128)(2,1)S(1)}, u32[]{:S(2)}, u32[]{:S(2)}) collective-permute-start(bf16[384,512]{1,0:T(8,128)(2,1)} %get-tuple-element.38.own_kv), channel_id=1, source_target_pairs={{0,8},{8,0},{1,9},{9,1},{2,10},{10,2},{3,11},{11,3},{4,12},{12,4},... | collective-permute-start | bytes 1179656 | tf_op jit(solution)/shard_map/ppermute | solution.py:319
  6.4 8.9 %collective-permute-start = (bf16[384,512]{1,0:T(8,128)(2,1)}, bf16[384,512]{1,0:T(8,128)(2,1)S(1)}, u32[]{:S(2)}, u32[]{:S(2)}) collective-permute-start(bf16[384,512]{1,0:T(8,128)(2,1)} %get-tuple-element.38.own_kv), channel_id=1, source_target_pairs={{0,16},{8,120},{16,32},{24,8},{32,48},{40,24},{48,64},{56,40},{64,... | collective-permute-start | bytes 1179656 | tf_op jit(solution)/shard_map/ppermute | solution.py:317
  10.2 3.7 %collective-permute-start.1 = (bf16[384,256]{1,0:T(8,128)(2,1)}, bf16[384,256]{1,0:T(8,128)(2,1)S(1)}, u32[]{:S(2)}, u32[]{:S(2)}) collective-permute-start(bf16[384,256]{1,0:T(8,128)(2,1)} %get-tuple-element.39.own_q), channel_id=1, source_target_pairs={{0,8},{8,0},{1,9},{9,1},{2,10},{10,2},{3,11},{11,3},{4,12},{12,4},... | collective-permute-start | bytes 589832 | tf_op jit(solution)/shard_map/ppermute | solution.py:319
  10.2 16.1 %collective-permute-start.3 = (bf16[576,512]{1,0:T(8,128)(2,1)}, bf16[576,512]{1,0:T(8,128)(2,1)S(1)}, u32[]{:S(2)}, u32[]{:S(2)}) collective-permute-start(bf16[576,512]{1,0:T(8,128)(2,1)} %get-tuple-element.42), channel_id=1, source_target_pairs={{0,128},{128,0},{1,129},{129,1},{2,130},{130,2},{3,131},{131,3},{4... | collective-permute-start | bytes 1769480 | tf_op jit(solution)/shard_map/ppermute | solution.py:318
  13.2 6.9 %collective-permute-start.6 = (bf16[384,512]{1,0:T(8,128)(2,1)S(1)}, bf16[384,512]{1,0:T(8,128)(2,1)S(1)}, u32[]{:S(2)}, u32[]{:S(2)}) collective-permute-start(bf16[384,512]{1,0:T(8,128)(2,1)S(1)} %collective-permute-done.5), channel_id=1, source_target_pairs={{0,16},{8,120},{16,32},{24,8},{32,48},{40,24},{48,64},{56,40},{64,... | collective-permute-start | bytes 1179656 | tf_op jit(solution)/shard_map/ppermute | solution.py:317
  15.3 11.1 %collective-permute-start.2 = (bf16[384,512]{1,0:T(8,128)(2,1)S(1)}, bf16[384,512]{1,0:T(8,128)(2,1)S(1)}, u32[]{:S(2)}, u32[]{:S(2)}) collective-permute-start(bf16[384,512]{1,0:T(8,128)(2,1)S(1)} %collective-permute-done.refs_0_), channel_id=1, source_target_pairs={{0,16},{8,120},{16,32},{24,8},{32,48},{40,24},{48,64},{56,40},{64,... | collective-permute-start | bytes 1179656 | tf_op jit(solution)/shard_map/ppermute | solution.py:317
  20.1 8.4 %collective-permute-start.7 = (bf16[384,512]{1,0:T(8,128)(2,1)S(1)}, bf16[384,512]{1,0:T(8,128)(2,1)S(1)}, u32[]{:S(2)}, u32[]{:S(2)}) collective-permute-start(bf16[384,512]{1,0:T(8,128)(2,1)S(1)} %collective-permute-done.6.refs_1_), channel_id=1, source_target_pairs={{0,16},{8,120},{16,32},{24,8},{32,48},{40,24},{48,64},{56,40},{64,... | collective-permute-start | bytes 1179656 | tf_op jit(solution)/shard_map/ppermute | solution.py:317
  26.3 4.6 %collective-permute-start.4 = (bf16[576,512]{1,0:T(8,128)(2,1)S(1)}, bf16[576,512]{1,0:T(8,128)(2,1)S(1)}, u32[]{:S(2)}, u32[]{:S(2)}) collective-permute-start(bf16[576,512]{1,0:T(8,128)(2,1)S(1)} %collective-permute-done.3.peer), channel_id=1, source_target_pairs={{0,8},{8,0},{1,9},{9,1},{2,10},{10,2},{3,11},{11,3},{4,12},{12,4},... | collective-permute-start | bytes 1769480 | tf_op jit(solution)/shard_map/ppermute | solution.py:319
  28.5 16.3 %collective-permute-start.8 = (bf16[384,512]{1,0:T(8,128)(2,1)S(1)}, bf16[384,512]{1,0:T(8,128)(2,1)S(1)}, u32[]{:S(2)}, u32[]{:S(2)}) collective-permute-start(bf16[384,512]{1,0:T(8,128)(2,1)S(1)} %slice.6), channel_id=1, source_target_pairs={{0,16},{8,120},{16,32},{24,8},{32,48},{40,24},{48,64},{56,40},{64,... | collective-permute-start | bytes 1179656 | tf_op jit(solution)/shard_map/ppermute | solution.py:317
  31.0 16.4 %collective-permute-start.11 = (bf16[384,512]{1,0:T(8,128)(2,1)S(1)}, bf16[384,512]{1,0:T(8,128)(2,1)S(1)}, u32[]{:S(2)}, u32[]{:S(2)}) collective-permute-start(bf16[384,512]{1,0:T(8,128)(2,1)S(1)} %slice.8), channel_id=1, source_target_pairs={{0,16},{8,120},{16,32},{24,8},{32,48},{40,24},{48,64},{56,40},{64,... | collective-permute-start | bytes 1179656 | tf_op jit(solution)/shard_map/ppermute | solution.py:317
  31.0 19.8 %collective-permute-start.10 = (bf16[384,512]{1,0:T(8,128)(2,1)S(1)}, bf16[384,512]{1,0:T(8,128)(2,1)S(1)}, u32[]{:S(2)}, u32[]{:S(2)}) collective-permute-start(bf16[384,512]{1,0:T(8,128)(2,1)S(1)} %collective-permute-done.2.refs_0_), channel_id=1, source_target_pairs={{0,16},{8,120},{16,32},{24,8},{32,48},{40,24},{48,64},{56,40},{64,... | collective-permute-start | bytes 1179656 | tf_op jit(solution)/shard_map/ppermute | solution.py:317
  31.6 19.2 %collective-permute-start.12 = (bf16[384,512]{1,0:T(8,128)(2,1)S(1)}, bf16[384,512]{1,0:T(8,128)(2,1)S(1)}, u32[]{:S(2)}, u32[]{:S(2)}) collective-permute-start(bf16[384,512]{1,0:T(8,128)(2,1)S(1)} %collective-permute-done.7.refs_1_), channel_id=1, source_target_pairs={{0,16},{8,120},{16,32},{24,8},{32,48},{40,24},{48,64},{56,40},{64,... | collective-permute-start | bytes 1179656 | tf_op jit(solution)/shard_map/ppermute | solution.py:317
  32.3 1.0 %copy-start = (bf16[384,512]{1,0:T(8,128)(2,1)S(1)}, bf16[384,512]{1,0:T(8,128)(2,1)}, u32[]{:S(2)}) copy-start(bf16[384,512]{1,0:T(8,128)(2,1)} %get-tuple-element.38.own_kv) | copy-start | bytes 1179652
  33.3 0.9 copy-start.1
  44.8 9.3 %collective-permute-start.9 = (bf16[384,512]{1,0:T(8,128)(2,1)S(1)}, bf16[384,512]{1,0:T(8,128)(2,1)S(1)}, u32[]{:S(2)}, u32[]{:S(2)}) collective-permute-start(bf16[384,512]{1,0:T(8,128)(2,1)S(1)} %collective-permute-done.8.refs_0_), channel_id=1, source_target_pairs={{0,16},{8,120},{16,32},{24,8},{32,48},{40,24},{48,64},{56,40},{64,... | collective-permute-start | bytes 1179656 | tf_op jit(solution)/shard_map/ppermute | solution.py:317
  47.4 9.3 %collective-permute-start.14 = (bf16[384,512]{1,0:T(8,128)(2,1)S(1)}, bf16[384,512]{1,0:T(8,128)(2,1)S(1)}, u32[]{:S(2)}, u32[]{:S(2)}) collective-permute-start(bf16[384,512]{1,0:T(8,128)(2,1)S(1)} %collective-permute-done.11.refs_1_), channel_id=1, source_target_pairs={{0,16},{8,120},{16,32},{24,8},{32,48},{40,24},{48,64},{56,40},{64,... | collective-permute-start | bytes 1179656 | tf_op jit(solution)/shard_map/ppermute | solution.py:317
  54.2 9.0 %collective-permute-start.13 = (bf16[384,512]{1,0:T(8,128)(2,1)S(1)}, bf16[384,512]{1,0:T(8,128)(2,1)S(1)}, u32[]{:S(2)}, u32[]{:S(2)}) collective-permute-start(bf16[384,512]{1,0:T(8,128)(2,1)S(1)} %collective-permute-done.9.refs_0_), channel_id=1, source_target_pairs={{0,16},{8,120},{16,32},{24,8},{32,48},{40,24},{48,64},{56,40},{64,... | collective-permute-start | bytes 1179656 | tf_op jit(solution)/shard_map/ppermute | solution.py:317
  56.7 8.7 %collective-permute-start.17 = (bf16[384,512]{1,0:T(8,128)(2,1)S(1)}, bf16[384,512]{1,0:T(8,128)(2,1)S(1)}, u32[]{:S(2)}, u32[]{:S(2)}) collective-permute-start(bf16[384,512]{1,0:T(8,128)(2,1)S(1)} %collective-permute-done.14.refs_1_), channel_id=1, source_target_pairs={{0,16},{8,120},{16,32},{24,8},{32,48},{40,24},{48,64},{56,40},{64,... | collective-permute-start | bytes 1179656 | tf_op jit(solution)/shard_map/ppermute | solution.py:317
  59.8 9.8 %collective-permute-start.16 = (bf16[384,512]{1,0:T(8,128)(2,1)S(1)}, bf16[384,512]{1,0:T(8,128)(2,1)S(1)}, u32[]{:S(2)}, u32[]{:S(2)}) collective-permute-start(bf16[384,512]{1,0:T(8,128)(2,1)S(1)} %collective-permute-done.10.refs_0_), channel_id=1, source_target_pairs={{0,16},{8,120},{16,32},{24,8},{32,48},{40,24},{48,64},{56,40},{64,... | collective-permute-start | bytes 1179656 | tf_op jit(solution)/shard_map/ppermute | solution.py:317
  63.2 10.6 %collective-permute-start.15 = (bf16[384,512]{1,0:T(8,128)(2,1)S(1)}, bf16[384,512]{1,0:T(8,128)(2,1)S(1)}, u32[]{:S(2)}, u32[]{:S(2)}) collective-permute-start(bf16[384,512]{1,0:T(8,128)(2,1)S(1)} %collective-permute-done.13.refs_0_), channel_id=1, source_target_pairs={{0,16},{8,120},{16,32},{24,8},{32,48},{40,24},{48,64},{56,40},{64,... | collective-permute-start | bytes 1179656 | tf_op jit(solution)/shard_map/ppermute | solution.py:317
  75.0 7.0 %collective-permute-start.18 = (bf16[768,256]{1,0:T(8,128)(2,1)S(1)}, bf16[768,256]{1,0:T(8,128)(2,1)S(1)}, u32[]{:S(2)}, u32[]{:S(2)}) collective-permute-start(bf16[768,256]{1,0:T(8,128)(2,1)S(1)} %get-tuple-element.69), channel_id=1, source_target_pairs={{0,8},{8,0},{1,9},{9,1},{2,10},{10,2},{3,11},{11,3},{4,12},{12,4},... | collective-permute-start | bytes 1179656 | tf_op jit(solution)/shard_map/ppermute | solution.py:319
  80.7 1.9 %collective-permute-start.19 = (f32[768,128]{1,0:T(8,128)S(1)}, f32[768,128]{1,0:T(8,128)S(1)}, u32[]{:S(2)}, u32[]{:S(2)}) collective-permute-start(f32[768,128]{1,0:T(8,128)S(1)} %get-tuple-element.70), channel_id=1, source_target_pairs={{0,8},{8,0},{1,9},{9,1},{2,10},{10,2},{3,11},{11,3},{4,12},{12,4},... | collective-permute-start | bytes 1179656 | tf_op jit(solution)/shard_map/ppermute | solution.py:319
  83.6 13.8 %collective-permute-start.20 = (bf16[384,256]{1,0:T(8,128)(2,1)S(1)}, bf16[384,256]{1,0:T(8,128)(2,1)S(1)}, u32[]{:S(2)}, u32[]{:S(2)}) collective-permute-start(bf16[384,256]{1,0:T(8,128)(2,1)S(1)} %get-tuple-element.72), channel_id=1, source_target_pairs={{0,128},{128,0},{1,129},{129,1},{2,130},{130,2},{3,131},{131,3},{4... | collective-permute-start | bytes 589832 | tf_op jit(solution)/shard_map/ppermute | solution.py:318

commit v5 on v4

--- a/solution.py
+++ b/solution.py
@@ -327,11 +327,12 @@
     core_q = over_core(own_q)
     near[0], core_q = after(near[0], core_q)
     near_next = [hop(a) for a in near]
-    first, peer = after(near_next[0], peer)
+    near_three = [hop(a) for a in near_next]
+    near_three[0], peer = after(near_three[0], peer)
     peer_core = over_core(peer)
-    second, peer_kv = after(near_next[1], peer[:tokens])
-    near_three = [hop(first), hop(second)]
+    near_three[1], peer_kv = after(near_three[1], peer[:tokens])
     far = [hop(peer_kv), hop(peer_core[:tokens])]
+    near_last = hop(near_three[0])
     state, query = begin(own_kv, own_q, core_q, peer, peer_core)
 
     def turn(pair, state, count):
@@ -344,18 +345,14 @@
         return kept, sent, state
 
     state = attend(query, near, state)
+    far, far_two, state = turn(far, state, 2)
     state = attend(query, near_next, state)
-    far, far_next, state = turn(far, state, 2)
+    state = attend(query, near_three + [near_last], state)
+    far_two, far_three, state = turn(far_two, state, 2)
     state = attend(query, far, state)
-    near, near_last, state = turn(near_three, state, 1)
-    state = attend(query, near, state)
-    far, far_next, state = turn(far_next, state, 2)
-    state = attend(query, far, state)
-    far, far_last, state = turn(far_next, state, 1)
-    state = attend(query, far, state)
-    last_near, state = after(near_last[0], state)
-    state = attend(query, [last_near], state)
-    ends = far_last
+    state = attend(query, far_two, state)
+    far_three, ends, state = turn(far_three, state, 1)
+    state = attend(query, far_three, state)
     rows = query.shape[0]
     there, there_stat = attend(query, ends, state, (rows // 2, rows), BF16)
     come, come_stat = over_core(there), over_core(there_stat)

time: 98.8 us -> 102 us (1.032)
  starting transfers between devices: 38.7 us -> 40.6 us
  waiting for transfers between devices: 13 us -> 14.7 us
    ppermute x14, starting transfers between devices: 22.4 us -> 26.1 us  [on_device(): hop = lambda a: lax.ppermute(a, ('z', 'core'), hop_pairs)]
    ppermute x14, waiting for transfers between devices: 8.86 us -> 11.4 us  [on_device(): hop = lambda a: lax.ppermute(a, ('z', 'core'), hop_pairs)]
    ppermute x5, starting transfers between devices: 10.5 us -> 8.67 us  [on_device(): over_core = lambda a: lax.ppermute(a, 'core', SWAP)]
    pallas_call x9 -> x8, Pallas kernels: 24.9 us -> 24.3 us  [attend(): pl.pallas_call(functools.partial(attend_kernel, len(kvs), base, kind is n...]
  transfers between devices with their start and end apart: 21 -> 21, of which waited for: 9 -> 10; matrix products, arithmetic and copies ran while one was open for 0% -> 0% of each run, Pallas kernels for 28% -> 26%
where the time goes in v5:
time: 102 us
  starting transfers between devices  40.6 us (40%)
  Pallas kernels  32.6 us (32%)
  waiting for transfers between devices  14.7 us (14%)
  blocking collectives  10.9 us (11%)
  local copies, waits for them, and re-layouts  1.97 us (2%)
    ppermute x14, starting transfers between devices, on_device(): hop = lambda a: lax.ppermute(a, ('z', 'core'), hop_pairs)  26.1 us
    pallas_call x8, Pallas kernels, attend(): pl.pallas_call(functools.partial(attend_kernel, len(kvs), base, kind is n...  24.3 us
    ppermute x14, waiting for transfers between devices, on_device(): hop = lambda a: lax.ppermute(a, ('z', 'core'), hop_pairs)  11.4 us
    all_to_all x1, blocking collectives, on_device(): squares = lax.all_to_all(squares, ('yh', 'yl', 'x'), 0, 0, tiled=True)  10.9 us
    ppermute x5, starting transfers between devices, on_device(): over_core = lambda a: lax.ppermute(a, 'core', SWAP)  8.67 us
    ppermute x2, starting transfers between devices, on_device(): over_y = lambda a: lax.ppermute(a, 'yh', SWAP)  5.84 us
    pallas_call x1, Pallas kernels, begin(): pl.pallas_call(begin_kernel, out_shape=[jax.ShapeDtypeStruct((rows, 5 * D...  3.74 us
    ppermute x2, waiting for transfers between devices, on_device(): over_y = lambda a: lax.ppermute(a, 'yh', SWAP)  2.59 us
  transfers between devices with their start and end apart: 21, of which 10 were waited for; matrix products, arithmetic and copies ran while one was open for 0% of the time, Pallas kernels for 26%

profile of v5, /device:TPU:1, one launch (start us, length us, event | category | flops | bytes accessed | tf_op | source)
XLA Modules:
  0.0 101.6 jit_solution(17978322925369041082)
XLA Ops:
  0.6 2.4 %pack.1 = (bf16[384,512]{1,0:T(8,128)(2,1)}, bf16[384,256]{1,0:T(8,128)(2,1)}, bf16[576,512]{1,0:T(8,128)(2,1)}) custom-call(bf16[384,256]{1,0:T(8,128)(2,1)} %q.1, bf16[384,256]{1,0:T(8,128)(2,1)} %k.1, bf16[384,256]{1,0:T(8,128)(2,1)} %v.1, bf16[384,256]{1,0:T(8,128)(2,1)} %qt.1, bf16[384,256]{1,0:T(8,128)(2,1)} %kt.1, bf16[384,256]{1,0:T(8,128)(2,1)} %vt.1), custom_call_target="tpu_custom_call" | custom-call | bytes 2359296 | tf_op jit(solution)/shard_map/pack/pallas_call | solution.py:58
  3.1 3.3 %collective-permute-start.6 = (bf16[384,512]{1,0:T(8,128)(2,1)}, bf16[384,512]{1,0:T(8,128)(2,1)S(1)}, u32[]{:S(2)}, u32[]{:S(2)}) collective-permute-start(bf16[384,512]{1,0:T(8,128)(2,1)} %get-tuple-element.32.own_kv), channel_id=1, source_target_pairs={{0,8},{8,0},{1,9},{9,1},{2,10},{10,2},{3,11},{11,3},{4,12},{12,4},... | collective-permute-start | bytes 1179656 | tf_op jit(solution)/shard_map/ppermute | solution.py:319
  6.4 3.8 %collective-permute-start = (bf16[384,512]{1,0:T(8,128)(2,1)}, bf16[384,512]{1,0:T(8,128)(2,1)S(1)}, u32[]{:S(2)}, u32[]{:S(2)}) collective-permute-start(bf16[384,512]{1,0:T(8,128)(2,1)} %get-tuple-element.32.own_kv), channel_id=1, source_target_pairs={{0,16},{8,120},{16,32},{24,8},{32,48},{40,24},{48,64},{56,40},{64,... | collective-permute-start | bytes 1179656 | tf_op jit(solution)/shard_map/ppermute | solution.py:317
  10.2 0.0 collective-permute-start.1
  10.2 0.0 collective-permute-done.6
  10.2 1.6 %collective-permute-start.7 = (bf16[384,512]{1,0:T(8,128)(2,1)S(1)}, bf16[384,512]{1,0:T(8,128)(2,1)S(1)}, u32[]{:S(2)}, u32[]{:S(2)}) collective-permute-start(bf16[384,512]{1,0:T(8,128)(2,1)S(1)} %collective-permute-done.6), channel_id=1, source_target_pairs={{0,16},{8,120},{16,32},{24,8},{32,48},{40,24},{48,64},{56,40},{64,... | collective-permute-start | bytes 1179656 | tf_op jit(solution)/shard_map/ppermute | solution.py:317
  11.8 0.1 collective-permute-done.1.core_q
  11.9 3.4 %collective-permute-done.refs_0_ = bf16[384,512]{1,0:T(8,128)(2,1)S(1)} collective-permute-done((bf16[384,512]{1,0:T(8,128)(2,1)}, bf16[384,512]{1,0:T(8,128)(2,1)S(1)}, u32[]{:S(2)}, u32[]{:S(2)}) %collective-permute-start) | collective-permute-done | bytes 393248 | tf_op jit(solution)/shard_map/ppermute | solution.py:317
  15.3 3.0 %collective-permute-start.2 = (bf16[384,512]{1,0:T(8,128)(2,1)S(1)}, bf16[384,512]{1,0:T(8,128)(2,1)S(1)}, u32[]{:S(2)}, u32[]{:S(2)}) collective-permute-start(bf16[384,512]{1,0:T(8,128)(2,1)S(1)} %collective-permute-done.refs_0_), channel_id=1, source_target_pairs={{0,16},{8,120},{16,32},{24,8},{32,48},{40,24},{48,64},{56,40},{64,... | collective-permute-start | bytes 1179656 | tf_op jit(solution)/shard_map/ppermute | solution.py:317
  18.3 2.9 %collective-permute-start.4 = (bf16[576,512]{1,0:T(8,128)(2,1)}, bf16[576,512]{1,0:T(8,128)(2,1)S(1)}, u32[]{:S(2)}, u32[]{:S(2)}) collective-permute-start(bf16[576,512]{1,0:T(8,128)(2,1)} %get-tuple-element.36), channel_id=1, source_target_pairs={{0,128},{128,0},{1,129},{129,1},{2,130},{130,2},{3,131},{131,3},{4... | collective-permute-start | bytes 1769480 | tf_op jit(solution)/shard_map/ppermute | solution.py:318
  21.2 0.0 collective-permute-done.7.refs_1_
  21.2 1.3 %collective-permute-start.8 = (bf16[384,512]{1,0:T(8,128)(2,1)S(1)}, bf16[384,512]{1,0:T(8,128)(2,1)S(1)}, u32[]{:S(2)}, u32[]{:S(2)}) collective-permute-start(bf16[384,512]{1,0:T(8,128)(2,1)S(1)} %collective-permute-done.7.refs_1_), channel_id=1, source_target_pairs={{0,16},{8,120},{16,32},{24,8},{32,48},{40,24},{48,64},{56,40},{64,... | collective-permute-start | bytes 1179656 | tf_op jit(solution)/shard_map/ppermute | solution.py:317
  22.5 1.1 %collective-permute-done.2.refs_0_ = bf16[384,512]{1,0:T(8,128)(2,1)S(1)} collective-permute-done((bf16[384,512]{1,0:T(8,128)(2,1)S(1)}, bf16[384,512]{1,0:T(8,128)(2,1)S(1)}, u32[]{:S(2)}, u32[]{:S(2)}) %collective-permute-start.2) | collective-permute-done | bytes 393248 | tf_op jit(solution)/shard_map/ppermute | solution.py:317
  23.6 3.4 %collective-permute-start.3 = (bf16[384,512]{1,0:T(8,128)(2,1)S(1)}, bf16[384,512]{1,0:T(8,128)(2,1)S(1)}, u32[]{:S(2)}, u32[]{:S(2)}) collective-permute-start(bf16[384,512]{1,0:T(8,128)(2,1)S(1)} %collective-permute-done.2.refs_0_), channel_id=1, source_target_pairs={{0,16},{8,120},{16,32},{24,8},{32,48},{40,24},{48,64},{56,40},{64,... | collective-permute-start | bytes 1179656 | tf_op jit(solution)/shard_map/ppermute | solution.py:317
  27.0 1.1 %collective-permute-done.8.refs_1_ = bf16[384,512]{1,0:T(8,128)(2,1)S(1)} collective-permute-done((bf16[384,512]{1,0:T(8,128)(2,1)S(1)}, bf16[384,512]{1,0:T(8,128)(2,1)S(1)}, u32[]{:S(2)}, u32[]{:S(2)}) %collective-permute-start.8) | collective-permute-done | bytes 393248 | tf_op jit(solution)/shard_map/ppermute | solution.py:317
  28.1 3.1 %collective-permute-start.9 = (bf16[384,512]{1,0:T(8,128)(2,1)S(1)}, bf16[384,512]{1,0:T(8,128)(2,1)S(1)}, u32[]{:S(2)}, u32[]{:S(2)}) collective-permute-start(bf16[384,512]{1,0:T(8,128)(2,1)S(1)} %collective-permute-done.8.refs_1_), channel_id=1, source_target_pairs={{0,16},{8,120},{16,32},{24,8},{32,48},{40,24},{48,64},{56,40},{64,... | collective-permute-start | bytes 1179656 | tf_op jit(solution)/shard_map/ppermute | solution.py:317
  31.2 2.6 %collective-permute-done.4.peer = bf16[576,512]{1,0:T(8,128)(2,1)S(1)} collective-permute-done((bf16[576,512]{1,0:T(8,128)(2,1)}, bf16[576,512]{1,0:T(8,128)(2,1)S(1)}, u32[]{:S(2)}, u32[]{:S(2)}) %collective-permute-start.4) | collective-permute-done | bytes 589856 | tf_op jit(solution)/shard_map/ppermute | solution.py:318
  33.8 0.0 collective-permute-done.3.refs_0_
  33.8 0.7 collective-permute-start.5
  34.6 2.0 %collective-permute-done.9.refs_1_ = bf16[384,512]{1,0:T(8,128)(2,1)S(1)} collective-permute-done((bf16[384,512]{1,0:T(8,128)(2,1)S(1)}, bf16[384,512]{1,0:T(8,128)(2,1)S(1)}, u32[]{:S(2)}, u32[]{:S(2)}) %collective-permute-start.9) | collective-permute-done | bytes 393248 | tf_op jit(solution)/shard_map/ppermute | solution.py:317
  36.5 2.8 %collective-permute-start.10 = (bf16[384,512]{1,0:T(8,128)(2,1)S(1)}, bf16[384,512]{1,0:T(8,128)(2,1)S(1)}, u32[]{:S(2)}, u32[]{:S(2)}) collective-permute-start(bf16[384,512]{1,0:T(8,128)(2,1)S(1)} %slice.6), channel_id=1, source_target_pairs={{0,16},{8,120},{16,32},{24,8},{32,48},{40,24},{48,64},{56,40},{64,... | collective-permute-start | bytes 1179656 | tf_op jit(solution)/shard_map/ppermute | solution.py:317
  39.3 0.0 collective-permute-done.5.peer_core
  39.4 0.1 collective-permute-start.13
  39.5 0.5 collective-permute-start.12
  40.0 0.0 copy-start
  40.0 1.0 copy-done
  41.0 0.0 copy-start.1
  41.0 0.9 copy-done.1
  41.9 3.7 %begin.1 = (f32[1536,640]{1,0:T(8,128)S(1)}, bf16[1536,256]{1,0:T(8,128)(2,1)S(1)}) custom-call(bf16[384,512]{1,0:T(8,128)(2,1)S(1)} %copy-done, bf16[384,256]{1,0:T(8,128)(2,1)S(1)} %copy-done.1, bf16[384,256]{1,0:T(8,128)(2,1)S(1)} %collective-permute-done.1.core_q, bf16[576,512]{1,0:T(8,128)(2,1)S(1)} %collective-permute-done.4.peer, ...), custom_call_target="tpu_custom_call" | custom-call | flops 1024 | bytes 1024 | tf_op jit(solution)/shard_map/begin/pallas_call | solution.py:208
  45.7 3.3 %attend.8.refs_2_ = f32[1536,640]{1,0:T(8,128)S(1)} custom-call(bf16[1536,256]{1,0:T(8,128)(2,1)S(1)} %get-tuple-element.38.q_ref, bf16[384,512]{1,0:T(8,128)(2,1)S(1)} %collective-permute-done.refs_0_, bf16[384,512]{1,0:T(8,128)(2,1)S(1)} %collective-permute-done.7.refs_1_, f32[1536,640]{1,0:T(8,128)S(1)} %get-tuple-element.40.refs_2_), custom_call_target="tpu_custom_call" | custom-call | flops 1024 | bytes 1024 | tf_op jit(solution)/shard_map/attend/pallas_call | solution.py:228
  49.0 0.0 collective-permute-done.10.refs_0_
  49.0 1.0 collective-permute-start.11
  50.0 0.0 collective-permute-done.13.refs_1_
  50.0 1.4 %collective-permute-start.15 = (bf16[384,512]{1,0:T(8,128)(2,1)S(1)}, bf16[384,512]{1,0:T(8,128)(2,1)S(1)}, u32[]{:S(2)}, u32[]{:S(2)}) collective-permute-start(bf16[384,512]{1,0:T(8,128)(2,1)S(1)} %collective-permute-done.13.refs_1_), channel_id=1, source_target_pairs={{0,16},{8,120},{16,32},{24,8},{32,48},{40,24},{48,64},{56,40},{64,... | collective-permute-start | bytes 1179656 | tf_op jit(solution)/shard_map/ppermute | solution.py:317
  51.4 3.3 %attend.9.refs_3_ = f32[1536,640]{1,0:T(8,128)S(1)} custom-call(bf16[1536,256]{1,0:T(8,128)(2,1)S(1)} %get-tuple-element.38.q_ref, bf16[384,512]{1,0:T(8,128)(2,1)S(1)} %collective-permute-done.2.refs_0_, bf16[384,512]{1,0:T(8,128)(2,1)S(1)} %collective-permute-done.8.refs_1_, f32[1536,640]{1,0:T(8,128)S(1)} %attend.8.refs_2_), custom_call_target="tpu_custom_call" | custom-call | flops 1024 | bytes 1024 | tf_op jit(solution)/shard_map/attend/pallas_call | solution.py:228
  54.7 0.0 collective-permute-done.12.refs_2_
  54.7 5.0 %attend.10.refs_2_ = f32[1536,640]{1,0:T(8,128)S(1)} custom-call(bf16[1536,256]{1,0:T(8,128)(2,1)S(1)} %get-tuple-element.38.q_ref, bf16[384,512]{1,0:T(8,128)(2,1)S(1)} %collective-permute-done.3.refs_0_, bf16[384,512]{1,0:T(8,128)(2,1)S(1)} %collective-permute-done.9.refs_1_, bf16[384,512]{1,0:T(8,128)(2,1)S(1)} %collective-permute-done.12.refs_2_, ...), custom_call_target="tpu_custom_call" | custom-call | flops 1024 | bytes 1024 | tf_op jit(solution)/shard_map/attend/pallas_call | solution.py:228
  59.7 0.0 collective-permute-done.11.refs_0_
  59.7 0.9 collective-permute-start.14
  60.7 0.2 collective-permute-done.15.refs_1_
  60.9 3.1 %collective-permute-start.17 = (bf16[384,512]{1,0:T(8,128)(2,1)S(1)}, bf16[384,512]{1,0:T(8,128)(2,1)S(1)}, u32[]{:S(2)}, u32[]{:S(2)}) collective-permute-start(bf16[384,512]{1,0:T(8,128)(2,1)S(1)} %collective-permute-done.15.refs_1_), channel_id=1, source_target_pairs={{0,16},{8,120},{16,32},{24,8},{32,48},{40,24},{48,64},{56,40},{64,... | collective-permute-start | bytes 1179656 | tf_op jit(solution)/shard_map/ppermute | solution.py:317
  64.0 3.3 %attend.11.refs_2_ = f32[1536,640]{1,0:T(8,128)S(1)} custom-call(bf16[1536,256]{1,0:T(8,128)(2,1)S(1)} %get-tuple-element.38.q_ref, bf16[384,512]{1,0:T(8,128)(2,1)S(1)} %collective-permute-done.10.refs_0_, bf16[384,512]{1,0:T(8,128)(2,1)S(1)} %collective-permute-done.13.refs_1_, f32[1536,640]{1,0:T(8,128)S(1)} %attend.10.refs_2_), custom_call_target="tpu_custom_call" | custom-call | flops 1024 | bytes 1024 | tf_op jit(solution)/shard_map/attend/pallas_call | solution.py:228
  67.4 3.3 %attend.12.refs_2_ = f32[1536,640]{1,0:T(8,128)S(1)} custom-call(bf16[1536,256]{1,0:T(8,128)(2,1)S(1)} %get-tuple-element.38.q_ref, bf16[384,512]{1,0:T(8,128)(2,1)S(1)} %collective-permute-done.11.refs_0_, bf16[384,512]{1,0:T(8,128)(2,1)S(1)} %collective-permute-done.15.refs_1_, f32[1536,640]{1,0:T(8,128)S(1)} %attend.11.refs_2_), custom_call_target="tpu_custom_call" | custom-call | flops 1024 | bytes 1024 | tf_op jit(solution)/shard_map/attend/pallas_call | solution.py:228
  70.7 0.0 collective-permute-done.14.refs_0_
  70.7 0.1 collective-permute-start.16
  70.8 0.2 collective-permute-done.17.refs_1_
  71.0 3.3 %attend.13.refs_1_ = f32[1536,640]{1,0:T(8,128)S(1)} custom-call(bf16[1536,256]{1,0:T(8,128)(2,1)S(1)} %get-tuple-element.38.q_ref, bf16[384,512]{1,0:T(8,128)(2,1)S(1)} %collective-permute-done.14.refs_0_, bf16[384,512]{1,0:T(8,128)(2,1)S(1)} %collective-permute-done.17.refs_1_, f32[1536,640]{1,0:T(8,128)S(1)} %attend.12.refs_2_), custom_call_target="tpu_custom_call" | custom-call | flops 1024 | bytes 1024 | tf_op jit(solution)/shard_map/attend/pallas_call | solution.py:228
  74.3 3.4 %collective-permute-done.16.refs_0_ = bf16[384,512]{1,0:T(8,128)(2,1)S(1)} collective-permute-done((bf16[384,512]{1,0:T(8,128)(2,1)S(1)}, bf16[384,512]{1,0:T(8,128)(2,1)S(1)}, u32[]{:S(2)}, u32[]{:S(2)}) %collective-permute-start.16) | collective-permute-done | bytes 393248 | tf_op jit(solution)/shard_map/ppermute | solution.py:317
  77.7 1.4 %attend.15 = (bf16[768,256]{1,0:T(8,128)(2,1)S(1)}, f32[768,128]{1,0:T(8,128)S(1)}) custom-call(bf16[1536,256]{1,0:T(8,128)(2,1)S(1)} %get-tuple-element.38.q_ref, bf16[384,512]{1,0:T(8,128)(2,1)S(1)} %collective-permute-done.16.refs_0_, f32[1536,640]{1,0:T(8,128)S(1)} %attend.13.refs_1_), custom_call_target="tpu_custom_call" | custom-call | flops 1024 | bytes 1024 | tf_op jit(solution)/shard_map/attend/pallas_call | solution.py:228
  79.2 4.5 %collective-permute-start.18 = (bf16[768,256]{1,0:T(8,128)(2,1)S(1)}, bf16[768,256]{1,0:T(8,128)(2,1)S(1)}, u32[]{:S(2)}, u32[]{:S(2)}) collective-permute-start(bf16[768,256]{1,0:T(8,128)(2,1)S(1)} %get-tuple-element.57), channel_id=1, source_target_pairs={{0,8},{8,0},{1,9},{9,1},{2,10},{10,2},{3,11},{11,3},{4,12},{12,4},... | collective-permute-start | bytes 1179656 | tf_op jit(solution)/shard_map/ppermute | solution.py:319
  83.7 0.1 collective-permute-start.19
  83.8 1.2 %attend.14 = (f32[768,256]{1,0:T(8,128)S(1)}, f32[768,128]{1,0:T(8,128)S(1)}) custom-call(bf16[1536,256]{1,0:T(8,128)(2,1)S(1)} %get-tuple-element.38.q_ref, bf16[384,512]{1,0:T(8,128)(2,1)S(1)} %collective-permute-done.16.refs_0_, f32[1536,640]{1,0:T(8,128)S(1)} %attend.13.refs_1_), custom_call_target="tpu_custom_call" | custom-call | flops 1024 | bytes 1024 | tf_op jit(solution)/shard_map/attend/pallas_call | solution.py:228
  85.0 0.0 collective-permute-done.18.other
  85.0 0.6 collective-permute-done.19.other_stat
  85.6 1.0 join.1
  86.6 2.9 %collective-permute-start.20 = (bf16[384,256]{1,0:T(8,128)(2,1)S(1)}, bf16[384,256]{1,0:T(8,128)(2,1)S(1)}, u32[]{:S(2)}, u32[]{:S(2)}) collective-permute-start(bf16[384,256]{1,0:T(8,128)(2,1)S(1)} %get-tuple-element.60), channel_id=1, source_target_pairs={{0,128},{128,0},{1,129},{129,1},{2,130},{130,2},{3,131},{131,3},{4... | collective-permute-start | bytes 589832 | tf_op jit(solution)/shard_map/ppermute | solution.py:318
  89.5 10.9 %all_to_all.5.squares = f32[16,8,128]{2,1,0:T(8,128)S(1)} all-to-all(f32[16,8,128]{2,1,0:T(8,128)S(1)} %get-tuple-element.61), channel_id=1, replica_groups=mesh['yh'=2,'z'=8,'core'=2,'yl'=2,'x'=4] {'yh','yl','x'}, dimensions={0} | all-to-all | bytes 131072 | tf_op jit(solution)/shard_map/all_to_all | solution.py:362
  100.4 0.0 collective-permute-done.20.come
  100.4 1.2 %finish.1 = (bf16[384,256]{1,0:T(8,128)(2,1)}, bf16[384,256]{1,0:T(8,128)(2,1)}) custom-call(f32[384,256]{1,0:T(8,128)S(1)} %get-tuple-element.59.keep, bf16[384,256]{1,0:T(8,128)(2,1)S(1)} %collective-permute-done.20.come, f32[16,8,128]{2,1,0:T(8,128)S(1)} %all_to_all.5.squares), custom_call_target="tpu_custom_call" | custom-call | tf_op jit(solution)/shard_map/finish/pallas_call | solution.py:311
  (2 shorter events, 0.1 us)
Async XLA Ops:
  3.1 7.2 %collective-permute-start.6 = (bf16[384,512]{1,0:T(8,128)(2,1)}, bf16[384,512]{1,0:T(8,128)(2,1)S(1)}, u32[]{:S(2)}, u32[]{:S(2)}) collective-permute-start(bf16[384,512]{1,0:T(8,128)(2,1)} %get-tuple-element.32.own_kv), channel_id=1, source_target_pairs={{0,8},{8,0},{1,9},{9,1},{2,10},{10,2},{3,11},{11,3},{4,12},{12,4},... | collective-permute-start | bytes 1179656 | tf_op jit(solution)/shard_map/ppermute | solution.py:319
  6.4 8.9 %collective-permute-start = (bf16[384,512]{1,0:T(8,128)(2,1)}, bf16[384,512]{1,0:T(8,128)(2,1)S(1)}, u32[]{:S(2)}, u32[]{:S(2)}) collective-permute-start(bf16[384,512]{1,0:T(8,128)(2,1)} %get-tuple-element.32.own_kv), channel_id=1, source_target_pairs={{0,16},{8,120},{16,32},{24,8},{32,48},{40,24},{48,64},{56,40},{64,... | collective-permute-start | bytes 1179656 | tf_op jit(solution)/shard_map/ppermute | solution.py:317
  10.2 1.7 %collective-permute-start.1 = (bf16[384,256]{1,0:T(8,128)(2,1)}, bf16[384,256]{1,0:T(8,128)(2,1)S(1)}, u32[]{:S(2)}, u32[]{:S(2)}) collective-permute-start(bf16[384,256]{1,0:T(8,128)(2,1)} %get-tuple-element.33.own_q), channel_id=1, source_target_pairs={{0,8},{8,0},{1,9},{9,1},{2,10},{10,2},{3,11},{11,3},{4,12},{12,4},... | collective-permute-start | bytes 589832 | tf_op jit(solution)/shard_map/ppermute | solution.py:319
  10.2 11.0 %collective-permute-start.7 = (bf16[384,512]{1,0:T(8,128)(2,1)S(1)}, bf16[384,512]{1,0:T(8,128)(2,1)S(1)}, u32[]{:S(2)}, u32[]{:S(2)}) collective-permute-start(bf16[384,512]{1,0:T(8,128)(2,1)S(1)} %collective-permute-done.6), channel_id=1, source_target_pairs={{0,16},{8,120},{16,32},{24,8},{32,48},{40,24},{48,64},{56,40},{64,... | collective-permute-start | bytes 1179656 | tf_op jit(solution)/shard_map/ppermute | solution.py:317
  15.3 8.3 %collective-permute-start.2 = (bf16[384,512]{1,0:T(8,128)(2,1)S(1)}, bf16[384,512]{1,0:T(8,128)(2,1)S(1)}, u32[]{:S(2)}, u32[]{:S(2)}) collective-permute-start(bf16[384,512]{1,0:T(8,128)(2,1)S(1)} %collective-permute-done.refs_0_), channel_id=1, source_target_pairs={{0,16},{8,120},{16,32},{24,8},{32,48},{40,24},{48,64},{56,40},{64,... | collective-permute-start | bytes 1179656 | tf_op jit(solution)/shard_map/ppermute | solution.py:317
  18.3 15.5 %collective-permute-start.4 = (bf16[576,512]{1,0:T(8,128)(2,1)}, bf16[576,512]{1,0:T(8,128)(2,1)S(1)}, u32[]{:S(2)}, u32[]{:S(2)}) collective-permute-start(bf16[576,512]{1,0:T(8,128)(2,1)} %get-tuple-element.36), channel_id=1, source_target_pairs={{0,128},{128,0},{1,129},{129,1},{2,130},{130,2},{3,131},{131,3},{4... | collective-permute-start | bytes 1769480 | tf_op jit(solution)/shard_map/ppermute | solution.py:318
  21.2 6.9 %collective-permute-start.8 = (bf16[384,512]{1,0:T(8,128)(2,1)S(1)}, bf16[384,512]{1,0:T(8,128)(2,1)S(1)}, u32[]{:S(2)}, u32[]{:S(2)}) collective-permute-start(bf16[384,512]{1,0:T(8,128)(2,1)S(1)} %collective-permute-done.7.refs_1_), channel_id=1, source_target_pairs={{0,16},{8,120},{16,32},{24,8},{32,48},{40,24},{48,64},{56,40},{64,... | collective-permute-start | bytes 1179656 | tf_op jit(solution)/shard_map/ppermute | solution.py:317
  23.6 10.2 %collective-permute-start.3 = (bf16[384,512]{1,0:T(8,128)(2,1)S(1)}, bf16[384,512]{1,0:T(8,128)(2,1)S(1)}, u32[]{:S(2)}, u32[]{:S(2)}) collective-permute-start(bf16[384,512]{1,0:T(8,128)(2,1)S(1)} %collective-permute-done.2.refs_0_), channel_id=1, source_target_pairs={{0,16},{8,120},{16,32},{24,8},{32,48},{40,24},{48,64},{56,40},{64,... | collective-permute-start | bytes 1179656 | tf_op jit(solution)/shard_map/ppermute | solution.py:317
  28.1 8.4 %collective-permute-start.9 = (bf16[384,512]{1,0:T(8,128)(2,1)S(1)}, bf16[384,512]{1,0:T(8,128)(2,1)S(1)}, u32[]{:S(2)}, u32[]{:S(2)}) collective-permute-start(bf16[384,512]{1,0:T(8,128)(2,1)S(1)} %collective-permute-done.8.refs_1_), channel_id=1, source_target_pairs={{0,16},{8,120},{16,32},{24,8},{32,48},{40,24},{48,64},{56,40},{64,... | collective-permute-start | bytes 1179656 | tf_op jit(solution)/shard_map/ppermute | solution.py:317
  33.8 5.5 %collective-permute-start.5 = (bf16[576,512]{1,0:T(8,128)(2,1)S(1)}, bf16[576,512]{1,0:T(8,128)(2,1)S(1)}, u32[]{:S(2)}, u32[]{:S(2)}) collective-permute-start(bf16[576,512]{1,0:T(8,128)(2,1)S(1)} %collective-permute-done.4.peer), channel_id=1, source_target_pairs={{0,8},{8,0},{1,9},{9,1},{2,10},{10,2},{3,11},{11,3},{4,12},{12,4},... | collective-permute-start | bytes 1769480 | tf_op jit(solution)/shard_map/ppermute | solution.py:319
  36.5 12.5 %collective-permute-start.10 = (bf16[384,512]{1,0:T(8,128)(2,1)S(1)}, bf16[384,512]{1,0:T(8,128)(2,1)S(1)}, u32[]{:S(2)}, u32[]{:S(2)}) collective-permute-start(bf16[384,512]{1,0:T(8,128)(2,1)S(1)} %slice.6), channel_id=1, source_target_pairs={{0,16},{8,120},{16,32},{24,8},{32,48},{40,24},{48,64},{56,40},{64,... | collective-permute-start | bytes 1179656 | tf_op jit(solution)/shard_map/ppermute | solution.py:317
  39.4 10.6 %collective-permute-start.13 = (bf16[384,512]{1,0:T(8,128)(2,1)S(1)}, bf16[384,512]{1,0:T(8,128)(2,1)S(1)}, u32[]{:S(2)}, u32[]{:S(2)}) collective-permute-start(bf16[384,512]{1,0:T(8,128)(2,1)S(1)} %slice.8), channel_id=1, source_target_pairs={{0,16},{8,120},{16,32},{24,8},{32,48},{40,24},{48,64},{56,40},{64,... | collective-permute-start | bytes 1179656 | tf_op jit(solution)/shard_map/ppermute | solution.py:317
  39.5 15.3 %collective-permute-start.12 = (bf16[384,512]{1,0:T(8,128)(2,1)S(1)}, bf16[384,512]{1,0:T(8,128)(2,1)S(1)}, u32[]{:S(2)}, u32[]{:S(2)}) collective-permute-start(bf16[384,512]{1,0:T(8,128)(2,1)S(1)} %collective-permute-done.3.refs_0_), channel_id=1, source_target_pairs={{0,16},{8,120},{16,32},{24,8},{32,48},{40,24},{48,64},{56,40},{64,... | collective-permute-start | bytes 1179656 | tf_op jit(solution)/shard_map/ppermute | solution.py:317
  40.0 1.0 copy-start
  41.0 0.9 copy-start.1
  49.0 10.7 %collective-permute-start.11 = (bf16[384,512]{1,0:T(8,128)(2,1)S(1)}, bf16[384,512]{1,0:T(8,128)(2,1)S(1)}, u32[]{:S(2)}, u32[]{:S(2)}) collective-permute-start(bf16[384,512]{1,0:T(8,128)(2,1)S(1)} %collective-permute-done.10.refs_0_), channel_id=1, source_target_pairs={{0,16},{8,120},{16,32},{24,8},{32,48},{40,24},{48,64},{56,40},{64,... | collective-permute-start | bytes 1179656 | tf_op jit(solution)/shard_map/ppermute | solution.py:317
  50.0 10.9 %collective-permute-start.15 = (bf16[384,512]{1,0:T(8,128)(2,1)S(1)}, bf16[384,512]{1,0:T(8,128)(2,1)S(1)}, u32[]{:S(2)}, u32[]{:S(2)}) collective-permute-start(bf16[384,512]{1,0:T(8,128)(2,1)S(1)} %collective-permute-done.13.refs_1_), channel_id=1, source_target_pairs={{0,16},{8,120},{16,32},{24,8},{32,48},{40,24},{48,64},{56,40},{64,... | collective-permute-start | bytes 1179656 | tf_op jit(solution)/shard_map/ppermute | solution.py:317
  59.7 11.0 %collective-permute-start.14 = (bf16[384,512]{1,0:T(8,128)(2,1)S(1)}, bf16[384,512]{1,0:T(8,128)(2,1)S(1)}, u32[]{:S(2)}, u32[]{:S(2)}) collective-permute-start(bf16[384,512]{1,0:T(8,128)(2,1)S(1)} %collective-permute-done.11.refs_0_), channel_id=1, source_target_pairs={{0,16},{8,120},{16,32},{24,8},{32,48},{40,24},{48,64},{56,40},{64,... | collective-permute-start | bytes 1179656 | tf_op jit(solution)/shard_map/ppermute | solution.py:317
  60.9 10.0 %collective-permute-start.17 = (bf16[384,512]{1,0:T(8,128)(2,1)S(1)}, bf16[384,512]{1,0:T(8,128)(2,1)S(1)}, u32[]{:S(2)}, u32[]{:S(2)}) collective-permute-start(bf16[384,512]{1,0:T(8,128)(2,1)S(1)} %collective-permute-done.15.refs_1_), channel_id=1, source_target_pairs={{0,16},{8,120},{16,32},{24,8},{32,48},{40,24},{48,64},{56,40},{64,... | collective-permute-start | bytes 1179656 | tf_op jit(solution)/shard_map/ppermute | solution.py:317
  70.7 7.0 %collective-permute-start.16 = (bf16[384,512]{1,0:T(8,128)(2,1)S(1)}, bf16[384,512]{1,0:T(8,128)(2,1)S(1)}, u32[]{:S(2)}, u32[]{:S(2)}) collective-permute-start(bf16[384,512]{1,0:T(8,128)(2,1)S(1)} %collective-permute-done.14.refs_0_), channel_id=1, source_target_pairs={{0,16},{8,120},{16,32},{24,8},{32,48},{40,24},{48,64},{56,40},{64,... | collective-permute-start | bytes 1179656 | tf_op jit(solution)/shard_map/ppermute | solution.py:317
  79.2 5.8 %collective-permute-start.18 = (bf16[768,256]{1,0:T(8,128)(2,1)S(1)}, bf16[768,256]{1,0:T(8,128)(2,1)S(1)}, u32[]{:S(2)}, u32[]{:S(2)}) collective-permute-start(bf16[768,256]{1,0:T(8,128)(2,1)S(1)} %get-tuple-element.57), channel_id=1, source_target_pairs={{0,8},{8,0},{1,9},{9,1},{2,10},{10,2},{3,11},{11,3},{4,12},{12,4},... | collective-permute-start | bytes 1179656 | tf_op jit(solution)/shard_map/ppermute | solution.py:319
  83.7 1.9 %collective-permute-start.19 = (f32[768,128]{1,0:T(8,128)S(1)}, f32[768,128]{1,0:T(8,128)S(1)}, u32[]{:S(2)}, u32[]{:S(2)}) collective-permute-start(f32[768,128]{1,0:T(8,128)S(1)} %get-tuple-element.58), channel_id=1, source_target_pairs={{0,8},{8,0},{1,9},{9,1},{2,10},{10,2},{3,11},{11,3},{4,12},{12,4},... | collective-permute-start | bytes 1179656 | tf_op jit(solution)/shard_map/ppermute | solution.py:319
  86.6 13.9 %collective-permute-start.20 = (bf16[384,256]{1,0:T(8,128)(2,1)S(1)}, bf16[384,256]{1,0:T(8,128)(2,1)S(1)}, u32[]{:S(2)}, u32[]{:S(2)}) collective-permute-start(bf16[384,256]{1,0:T(8,128)(2,1)S(1)} %get-tuple-element.60), channel_id=1, source_target_pairs={{0,128},{128,0},{1,129},{129,1},{2,130},{130,2},{3,131},{131,3},{4... | collective-permute-start | bytes 589832 | tf_op jit(solution)/shard_map/ppermute | solution.py:318

commit v6 on v4

--- a/solution.py
+++ b/solution.py
@@ -324,14 +324,13 @@
     peer = over_y(other)
     core_kv = over_core(own_kv)
     near = [hop(own_kv), hop(core_kv)]
-    core_q = over_core(own_q)
-    near[0], core_q = after(near[0], core_q)
     near_next = [hop(a) for a in near]
     first, peer = after(near_next[0], peer)
     peer_core = over_core(peer)
     second, peer_kv = after(near_next[1], peer[:tokens])
     near_three = [hop(first), hop(second)]
     far = [hop(peer_kv), hop(peer_core[:tokens])]
+    core_q = over_core(own_q)
     state, query = begin(own_kv, own_q, core_q, peer, peer_core)
 
     def turn(pair, state, count):

time: 98.8 us -> 98.9 us (level)
    ppermute x14, waiting for transfers between devices: 8.86 us -> 12.2 us  [on_device(): hop = lambda a: lax.ppermute(a, ('z', 'core'), hop_pairs)]
    ppermute x5, starting transfers between devices: 10.5 us -> 7.22 us  [on_device(): over_core = lambda a: lax.ppermute(a, 'core', SWAP)]
    ppermute x2, waiting for transfers between devices: 3.55 us -> 1.11 us  [on_device(): over_y = lambda a: lax.ppermute(a, 'yh', SWAP)]
    ppermute x14, starting transfers between devices: 22.4 us -> 24.8 us  [on_device(): hop = lambda a: lax.ppermute(a, ('z', 'core'), hop_pairs)]
where the time goes in v6:
time: 98.9 us; the launch traced here: 98.6 us
  starting transfers between devices  37.8 us (38%)
  Pallas kernels  33.2 us (34%)
  waiting for transfers between devices  13.9 us (14%)
  blocking collectives  10.9 us (11%)
  local copies, waits for them, and re-layouts  1.98 us (2%)
    pallas_call x9, Pallas kernels, attend(): pl.pallas_call(functools.partial(attend_kernel, len(kvs), base, kind is n...  24.9 us
    ppermute x14, starting transfers between devices, on_device(): hop = lambda a: lax.ppermute(a, ('z', 'core'), hop_pairs)  24.8 us
    ppermute x14, waiting for transfers between devices, on_device(): hop = lambda a: lax.ppermute(a, ('z', 'core'), hop_pairs)  12.2 us
    all_to_all x1, blocking collectives, on_device(): squares = lax.all_to_all(squares, ('yh', 'yl', 'x'), 0, 0, tiled=True)  10.9 us
    ppermute x5, starting transfers between devices, on_device(): over_core = lambda a: lax.ppermute(a, 'core', SWAP)  7.22 us
    ppermute x2, starting transfers between devices, on_device(): over_y = lambda a: lax.ppermute(a, 'yh', SWAP)  5.84 us
    pallas_call x1, Pallas kernels, begin(): pl.pallas_call(begin_kernel, out_shape=[jax.ShapeDtypeStruct((rows, 5 * D...  3.74 us
    pallas_call x1, Pallas kernels, pack(): pl.pallas_call(pack_kernel, grid=(2,), in_specs=[row(2 * DH)] * 6, out_sp...  2.43 us
  transfers between devices with their start and end apart: 21, of which 9 were waited for; matrix products, arithmetic and copies ran while one was open for 0% of the time, Pallas kernels for 28%

profile of v6, /device:TPU:1, one launch (start us, length us, event | category | flops | bytes accessed | tf_op | source)
XLA Modules:
  0.0 98.6 jit_solution(7983654415431212208)
XLA Ops:
  0.6 2.4 %pack.1 = (bf16[384,512]{1,0:T(8,128)(2,1)}, bf16[384,256]{1,0:T(8,128)(2,1)}, bf16[576,512]{1,0:T(8,128)(2,1)}) custom-call(bf16[384,256]{1,0:T(8,128)(2,1)} %q.1, bf16[384,256]{1,0:T(8,128)(2,1)} %k.1, bf16[384,256]{1,0:T(8,128)(2,1)} %v.1, bf16[384,256]{1,0:T(8,128)(2,1)} %qt.1, bf16[384,256]{1,0:T(8,128)(2,1)} %kt.1, bf16[384,256]{1,0:T(8,128)(2,1)} %vt.1), custom_call_target="tpu_custom_call" | custom-call | bytes 2359296 | tf_op jit(solution)/shard_map/pack/pallas_call | solution.py:58
  3.1 3.3 %collective-permute-start.5 = (bf16[384,512]{1,0:T(8,128)(2,1)}, bf16[384,512]{1,0:T(8,128)(2,1)S(1)}, u32[]{:S(2)}, u32[]{:S(2)}) collective-permute-start(bf16[384,512]{1,0:T(8,128)(2,1)} %get-tuple-element.36.own_kv), channel_id=1, source_target_pairs={{0,8},{8,0},{1,9},{9,1},{2,10},{10,2},{3,11},{11,3},{4,12},{12,4},... | collective-permute-start | bytes 1179656 | tf_op jit(solution)/shard_map/ppermute | solution.py:319
  6.4 3.8 %collective-permute-start.1 = (bf16[384,512]{1,0:T(8,128)(2,1)}, bf16[384,512]{1,0:T(8,128)(2,1)S(1)}, u32[]{:S(2)}, u32[]{:S(2)}) collective-permute-start(bf16[384,512]{1,0:T(8,128)(2,1)} %get-tuple-element.36.own_kv), channel_id=1, source_target_pairs={{0,16},{8,120},{16,32},{24,8},{32,48},{40,24},{48,64},{56,40},{64,... | collective-permute-start | bytes 1179656 | tf_op jit(solution)/shard_map/ppermute | solution.py:317
  10.2 2.9 %collective-permute-start.3 = (bf16[576,512]{1,0:T(8,128)(2,1)}, bf16[576,512]{1,0:T(8,128)(2,1)S(1)}, u32[]{:S(2)}, u32[]{:S(2)}) collective-permute-start(bf16[576,512]{1,0:T(8,128)(2,1)} %get-tuple-element.38), channel_id=1, source_target_pairs={{0,128},{128,0},{1,129},{129,1},{2,130},{130,2},{3,131},{131,3},{4... | collective-permute-start | bytes 1769480 | tf_op jit(solution)/shard_map/ppermute | solution.py:318
  13.1 0.0 collective-permute-done.5
  13.1 0.7 collective-permute-start.6
  13.9 1.4 %collective-permute-done.1.refs_0_ = bf16[384,512]{1,0:T(8,128)(2,1)S(1)} collective-permute-done((bf16[384,512]{1,0:T(8,128)(2,1)}, bf16[384,512]{1,0:T(8,128)(2,1)S(1)}, u32[]{:S(2)}, u32[]{:S(2)}) %collective-permute-start.1) | collective-permute-done | bytes 393248 | tf_op jit(solution)/shard_map/ppermute | solution.py:317
  15.3 3.3 %collective-permute-start.2 = (bf16[384,512]{1,0:T(8,128)(2,1)S(1)}, bf16[384,512]{1,0:T(8,128)(2,1)S(1)}, u32[]{:S(2)}, u32[]{:S(2)}) collective-permute-start(bf16[384,512]{1,0:T(8,128)(2,1)S(1)} %collective-permute-done.1.refs_0_), channel_id=1, source_target_pairs={{0,16},{8,120},{16,32},{24,8},{32,48},{40,24},{48,64},{56,40},{64,... | collective-permute-start | bytes 1179656 | tf_op jit(solution)/shard_map/ppermute | solution.py:317
  18.6 1.5 %collective-permute-done.6.refs_1_ = bf16[384,512]{1,0:T(8,128)(2,1)S(1)} collective-permute-done((bf16[384,512]{1,0:T(8,128)(2,1)S(1)}, bf16[384,512]{1,0:T(8,128)(2,1)S(1)}, u32[]{:S(2)}, u32[]{:S(2)}) %collective-permute-start.6) | collective-permute-done | bytes 393248 | tf_op jit(solution)/shard_map/ppermute | solution.py:317
  20.1 2.7 %collective-permute-start.7 = (bf16[384,512]{1,0:T(8,128)(2,1)S(1)}, bf16[384,512]{1,0:T(8,128)(2,1)S(1)}, u32[]{:S(2)}, u32[]{:S(2)}) collective-permute-start(bf16[384,512]{1,0:T(8,128)(2,1)S(1)} %collective-permute-done.6.refs_1_), channel_id=1, source_target_pairs={{0,16},{8,120},{16,32},{24,8},{32,48},{40,24},{48,64},{56,40},{64,... | collective-permute-start | bytes 1179656 | tf_op jit(solution)/shard_map/ppermute | solution.py:317
  22.8 1.1 %collective-permute-done.3.peer = bf16[576,512]{1,0:T(8,128)(2,1)S(1)} collective-permute-done((bf16[576,512]{1,0:T(8,128)(2,1)}, bf16[576,512]{1,0:T(8,128)(2,1)S(1)}, u32[]{:S(2)}, u32[]{:S(2)}) %collective-permute-start.3) | collective-permute-done | bytes 589856 | tf_op jit(solution)/shard_map/ppermute | solution.py:318
  23.9 0.4 collective-permute-done.2.refs_0_
  24.3 1.3 %collective-permute-start.4 = (bf16[576,512]{1,0:T(8,128)(2,1)S(1)}, bf16[576,512]{1,0:T(8,128)(2,1)S(1)}, u32[]{:S(2)}, u32[]{:S(2)}) collective-permute-start(bf16[576,512]{1,0:T(8,128)(2,1)S(1)} %collective-permute-done.3.peer), channel_id=1, source_target_pairs={{0,8},{8,0},{1,9},{9,1},{2,10},{10,2},{3,11},{11,3},{4,12},{12,4},... | collective-permute-start | bytes 1769480 | tf_op jit(solution)/shard_map/ppermute | solution.py:319
  25.6 2.9 %collective-permute-done.7.refs_1_ = bf16[384,512]{1,0:T(8,128)(2,1)S(1)} collective-permute-done((bf16[384,512]{1,0:T(8,128)(2,1)S(1)}, bf16[384,512]{1,0:T(8,128)(2,1)S(1)}, u32[]{:S(2)}, u32[]{:S(2)}) %collective-permute-start.7) | collective-permute-done | bytes 393248 | tf_op jit(solution)/shard_map/ppermute | solution.py:317
  28.5 2.4 %collective-permute-start.8 = (bf16[384,512]{1,0:T(8,128)(2,1)S(1)}, bf16[384,512]{1,0:T(8,128)(2,1)S(1)}, u32[]{:S(2)}, u32[]{:S(2)}) collective-permute-start(bf16[384,512]{1,0:T(8,128)(2,1)S(1)} %slice.6), channel_id=1, source_target_pairs={{0,16},{8,120},{16,32},{24,8},{32,48},{40,24},{48,64},{56,40},{64,... | collective-permute-start | bytes 1179656 | tf_op jit(solution)/shard_map/ppermute | solution.py:317
  30.9 0.0 collective-permute-start
  30.9 0.0 collective-permute-done.4.peer_core
  31.0 1.9 %collective-permute-start.11 = (bf16[384,512]{1,0:T(8,128)(2,1)S(1)}, bf16[384,512]{1,0:T(8,128)(2,1)S(1)}, u32[]{:S(2)}, u32[]{:S(2)}) collective-permute-start(bf16[384,512]{1,0:T(8,128)(2,1)S(1)} %slice.8), channel_id=1, source_target_pairs={{0,16},{8,120},{16,32},{24,8},{32,48},{40,24},{48,64},{56,40},{64,... | collective-permute-start | bytes 1179656 | tf_op jit(solution)/shard_map/ppermute | solution.py:317
  32.8 0.1 collective-permute-start.10
  32.9 0.6 collective-permute-start.12
  33.5 0.0 collective-permute-done.core_q
  33.5 0.0 copy-start
  33.5 1.0 %copy-done = bf16[384,512]{1,0:T(8,128)(2,1)S(1)} copy-done((bf16[384,512]{1,0:T(8,128)(2,1)S(1)}, bf16[384,512]{1,0:T(8,128)(2,1)}, u32[]{:S(2)}) %copy-start) | copy-done | bytes 393240
  34.5 0.0 copy-start.1
  34.5 0.9 copy-done.1
  35.5 3.7 %begin.1 = (f32[1536,640]{1,0:T(8,128)S(1)}, bf16[1536,256]{1,0:T(8,128)(2,1)S(1)}) custom-call(bf16[384,512]{1,0:T(8,128)(2,1)S(1)} %copy-done, bf16[384,256]{1,0:T(8,128)(2,1)S(1)} %copy-done.1, bf16[384,256]{1,0:T(8,128)(2,1)S(1)} %collective-permute-done.core_q, bf16[576,512]{1,0:T(8,128)(2,1)S(1)} %collective-permute-done.3.peer, ...), custom_call_target="tpu_custom_call" | custom-call | flops 1024 | bytes 1024 | tf_op jit(solution)/shard_map/begin/pallas_call | solution.py:208
  39.2 3.5 %attend.9.refs_2_ = f32[1536,640]{1,0:T(8,128)S(1)} custom-call(bf16[1536,256]{1,0:T(8,128)(2,1)S(1)} %get-tuple-element.40.q_ref, bf16[384,512]{1,0:T(8,128)(2,1)S(1)} %collective-permute-done.1.refs_0_, bf16[384,512]{1,0:T(8,128)(2,1)S(1)} %collective-permute-done.6.refs_1_, f32[1536,640]{1,0:T(8,128)S(1)} %get-tuple-element.42.refs_2_), custom_call_target="tpu_custom_call" | custom-call | flops 1024 | bytes 1024 | tf_op jit(solution)/shard_map/attend/pallas_call | solution.py:228
  42.7 3.3 %attend.10.refs_2_ = f32[1536,640]{1,0:T(8,128)S(1)} custom-call(bf16[1536,256]{1,0:T(8,128)(2,1)S(1)} %get-tuple-element.40.q_ref, bf16[384,512]{1,0:T(8,128)(2,1)S(1)} %collective-permute-done.2.refs_0_, bf16[384,512]{1,0:T(8,128)(2,1)S(1)} %collective-permute-done.7.refs_1_, f32[1536,640]{1,0:T(8,128)S(1)} %attend.9.refs_2_), custom_call_target="tpu_custom_call" | custom-call | flops 1024 | bytes 1024 | tf_op jit(solution)/shard_map/attend/pallas_call | solution.py:228
  46.1 0.0 collective-permute-done.8.refs_0_
  46.1 1.6 %collective-permute-start.9 = (bf16[384,512]{1,0:T(8,128)(2,1)S(1)}, bf16[384,512]{1,0:T(8,128)(2,1)S(1)}, u32[]{:S(2)}, u32[]{:S(2)}) collective-permute-start(bf16[384,512]{1,0:T(8,128)(2,1)S(1)} %collective-permute-done.8.refs_0_), channel_id=1, source_target_pairs={{0,16},{8,120},{16,32},{24,8},{32,48},{40,24},{48,64},{56,40},{64,... | collective-permute-start | bytes 1179656 | tf_op jit(solution)/shard_map/ppermute | solution.py:317
  47.6 0.0 collective-permute-done.11.refs_1_
  47.6 2.9 %collective-permute-start.14 = (bf16[384,512]{1,0:T(8,128)(2,1)S(1)}, bf16[384,512]{1,0:T(8,128)(2,1)S(1)}, u32[]{:S(2)}, u32[]{:S(2)}) collective-permute-start(bf16[384,512]{1,0:T(8,128)(2,1)S(1)} %collective-permute-done.11.refs_1_), channel_id=1, source_target_pairs={{0,16},{8,120},{16,32},{24,8},{32,48},{40,24},{48,64},{56,40},{64,... | collective-permute-start | bytes 1179656 | tf_op jit(solution)/shard_map/ppermute | solution.py:317
  50.6 3.3 %attend.11.refs_2_ = f32[1536,640]{1,0:T(8,128)S(1)} custom-call(bf16[1536,256]{1,0:T(8,128)(2,1)S(1)} %get-tuple-element.40.q_ref, bf16[384,512]{1,0:T(8,128)(2,1)S(1)} %collective-permute-done.8.refs_0_, bf16[384,512]{1,0:T(8,128)(2,1)S(1)} %collective-permute-done.11.refs_1_, f32[1536,640]{1,0:T(8,128)S(1)} %attend.10.refs_2_), custom_call_target="tpu_custom_call" | custom-call | flops 1024 | bytes 1024 | tf_op jit(solution)/shard_map/attend/pallas_call | solution.py:228
  53.9 0.0 collective-permute-done.10.refs_0_
  53.9 0.0 collective-permute-done.12.refs_1_
  53.9 3.3 %attend.12.refs_2_ = f32[1536,640]{1,0:T(8,128)S(1)} custom-call(bf16[1536,256]{1,0:T(8,128)(2,1)S(1)} %get-tuple-element.40.q_ref, bf16[384,512]{1,0:T(8,128)(2,1)S(1)} %collective-permute-done.10.refs_0_, bf16[384,512]{1,0:T(8,128)(2,1)S(1)} %collective-permute-done.12.refs_1_, f32[1536,640]{1,0:T(8,128)S(1)} %attend.11.refs_2_), custom_call_target="tpu_custom_call" | custom-call | flops 1024 | bytes 1024 | tf_op jit(solution)/shard_map/attend/pallas_call | solution.py:228
  57.3 0.0 collective-permute-done.9.refs_0_
  57.3 0.2 collective-permute-start.13
  57.5 0.0 collective-permute-done.14.refs_1_
  57.5 2.4 %collective-permute-start.17 = (bf16[384,512]{1,0:T(8,128)(2,1)S(1)}, bf16[384,512]{1,0:T(8,128)(2,1)S(1)}, u32[]{:S(2)}, u32[]{:S(2)}) collective-permute-start(bf16[384,512]{1,0:T(8,128)(2,1)S(1)} %collective-permute-done.14.refs_1_), channel_id=1, source_target_pairs={{0,16},{8,120},{16,32},{24,8},{32,48},{40,24},{48,64},{56,40},{64,... | collective-permute-start | bytes 1179656 | tf_op jit(solution)/shard_map/ppermute | solution.py:317
  59.8 1.6 %collective-permute-start.16 = (bf16[384,512]{1,0:T(8,128)(2,1)S(1)}, bf16[384,512]{1,0:T(8,128)(2,1)S(1)}, u32[]{:S(2)}, u32[]{:S(2)}) collective-permute-start(bf16[384,512]{1,0:T(8,128)(2,1)S(1)} %collective-permute-done.10.refs_0_), channel_id=1, source_target_pairs={{0,16},{8,120},{16,32},{24,8},{32,48},{40,24},{48,64},{56,40},{64,... | collective-permute-start | bytes 1179656 | tf_op jit(solution)/shard_map/ppermute | solution.py:317
  61.4 3.3 %attend.13.refs_2_ = f32[1536,640]{1,0:T(8,128)S(1)} custom-call(bf16[1536,256]{1,0:T(8,128)(2,1)S(1)} %get-tuple-element.40.q_ref, bf16[384,512]{1,0:T(8,128)(2,1)S(1)} %collective-permute-done.9.refs_0_, bf16[384,512]{1,0:T(8,128)(2,1)S(1)} %collective-permute-done.14.refs_1_, f32[1536,640]{1,0:T(8,128)S(1)} %attend.12.refs_2_), custom_call_target="tpu_custom_call" | custom-call | flops 1024 | bytes 1024 | tf_op jit(solution)/shard_map/attend/pallas_call | solution.py:228
  64.8 0.0 collective-permute-done.13.refs_0_
  64.8 0.5 collective-permute-start.15
  65.3 3.2 %collective-permute-done.17.refs_1_ = bf16[384,512]{1,0:T(8,128)(2,1)S(1)} collective-permute-done((bf16[384,512]{1,0:T(8,128)(2,1)S(1)}, bf16[384,512]{1,0:T(8,128)(2,1)S(1)}, u32[]{:S(2)}, u32[]{:S(2)}) %collective-permute-start.17) | collective-permute-done | bytes 393248 | tf_op jit(solution)/shard_map/ppermute | solution.py:317
  68.5 3.3 %attend.14.refs_1_ = f32[1536,640]{1,0:T(8,128)S(1)} custom-call(bf16[1536,256]{1,0:T(8,128)(2,1)S(1)} %get-tuple-element.40.q_ref, bf16[384,512]{1,0:T(8,128)(2,1)S(1)} %collective-permute-done.13.refs_0_, bf16[384,512]{1,0:T(8,128)(2,1)S(1)} %collective-permute-done.17.refs_1_, f32[1536,640]{1,0:T(8,128)S(1)} %attend.13.refs_2_), custom_call_target="tpu_custom_call" | custom-call | flops 1024 | bytes 1024 | tf_op jit(solution)/shard_map/attend/pallas_call | solution.py:228
  71.8 0.9 collective-permute-done.16.refs_0_
  72.7 2.3 %attend.15.refs_1_ = f32[1536,640]{1,0:T(8,128)S(1)} custom-call(bf16[1536,256]{1,0:T(8,128)(2,1)S(1)} %get-tuple-element.40.q_ref, bf16[384,512]{1,0:T(8,128)(2,1)S(1)} %collective-permute-done.16.refs_0_, f32[1536,640]{1,0:T(8,128)S(1)} %attend.14.refs_1_), custom_call_target="tpu_custom_call" | custom-call | flops 1024 | bytes 1024 | tf_op jit(solution)/shard_map/attend/pallas_call | solution.py:228
  75.1 1.9 %collective-permute-done.15.refs_0_ = bf16[384,512]{1,0:T(8,128)(2,1)S(1)} collective-permute-done((bf16[384,512]{1,0:T(8,128)(2,1)S(1)}, bf16[384,512]{1,0:T(8,128)(2,1)S(1)}, u32[]{:S(2)}, u32[]{:S(2)}) %collective-permute-start.15) | collective-permute-done | bytes 393248 | tf_op jit(solution)/shard_map/ppermute | solution.py:317
  76.9 1.2 %attend.17 = (bf16[768,256]{1,0:T(8,128)(2,1)S(1)}, f32[768,128]{1,0:T(8,128)S(1)}) custom-call(bf16[1536,256]{1,0:T(8,128)(2,1)S(1)} %get-tuple-element.40.q_ref, bf16[384,512]{1,0:T(8,128)(2,1)S(1)} %collective-permute-done.15.refs_0_, f32[1536,640]{1,0:T(8,128)S(1)} %attend.15.refs_1_), custom_call_target="tpu_custom_call" | custom-call | flops 1024 | bytes 1024 | tf_op jit(solution)/shard_map/attend/pallas_call | solution.py:228
  78.1 2.5 %collective-permute-start.18 = (bf16[768,256]{1,0:T(8,128)(2,1)S(1)}, bf16[768,256]{1,0:T(8,128)(2,1)S(1)}, u32[]{:S(2)}, u32[]{:S(2)}) collective-permute-start(bf16[768,256]{1,0:T(8,128)(2,1)S(1)} %get-tuple-element.65), channel_id=1, source_target_pairs={{0,8},{8,0},{1,9},{9,1},{2,10},{10,2},{3,11},{11,3},{4,12},{12,4},... | collective-permute-start | bytes 1179656 | tf_op jit(solution)/shard_map/ppermute | solution.py:319
  80.7 0.1 collective-permute-start.19
  80.8 1.2 %attend.16 = (f32[768,256]{1,0:T(8,128)S(1)}, f32[768,128]{1,0:T(8,128)S(1)}) custom-call(bf16[1536,256]{1,0:T(8,128)(2,1)S(1)} %get-tuple-element.40.q_ref, bf16[384,512]{1,0:T(8,128)(2,1)S(1)} %collective-permute-done.15.refs_0_, f32[1536,640]{1,0:T(8,128)S(1)} %attend.15.refs_1_), custom_call_target="tpu_custom_call" | custom-call | flops 1024 | bytes 1024 | tf_op jit(solution)/shard_map/attend/pallas_call | solution.py:228
  82.0 0.0 collective-permute-done.18.other
  82.0 0.6 collective-permute-done.19.other_stat
  82.6 1.0 %join.1 = (f32[384,256]{1,0:T(8,128)S(1)}, bf16[384,256]{1,0:T(8,128)(2,1)S(1)}, f32[16,8,128]{2,1,0:T(8,128)S(1)}) custom-call(f32[768,256]{1,0:T(8,128)S(1)} %get-tuple-element.63.mine, f32[768,128]{1,0:T(8,128)S(1)} %get-tuple-element.64.mine_stat, bf16[768,256]{1,0:T(8,128)(2,1)S(1)} %collective-permute-done.18.other, ...), custom_call_target="tpu_custom_call" | custom-call | tf_op jit(solution)/shard_map/join/pallas_call | solution.py:272
  83.6 2.9 %collective-permute-start.20 = (bf16[384,256]{1,0:T(8,128)(2,1)S(1)}, bf16[384,256]{1,0:T(8,128)(2,1)S(1)}, u32[]{:S(2)}, u32[]{:S(2)}) collective-permute-start(bf16[384,256]{1,0:T(8,128)(2,1)S(1)} %get-tuple-element.68), channel_id=1, source_target_pairs={{0,128},{128,0},{1,129},{129,1},{2,130},{130,2},{3,131},{131,3},{4... | collective-permute-start | bytes 589832 | tf_op jit(solution)/shard_map/ppermute | solution.py:318
  86.5 10.9 %all_to_all.5.squares = f32[16,8,128]{2,1,0:T(8,128)S(1)} all-to-all(f32[16,8,128]{2,1,0:T(8,128)S(1)} %get-tuple-element.69), channel_id=1, replica_groups=mesh['yh'=2,'z'=8,'core'=2,'yl'=2,'x'=4] {'yh','yl','x'}, dimensions={0} | all-to-all | bytes 131072 | tf_op jit(solution)/shard_map/all_to_all | solution.py:364
  97.4 0.0 collective-permute-done.20.come
  97.4 1.2 %finish.1 = (bf16[384,256]{1,0:T(8,128)(2,1)}, bf16[384,256]{1,0:T(8,128)(2,1)}) custom-call(f32[384,256]{1,0:T(8,128)S(1)} %get-tuple-element.67.keep, bf16[384,256]{1,0:T(8,128)(2,1)S(1)} %collective-permute-done.20.come, f32[16,8,128]{2,1,0:T(8,128)S(1)} %all_to_all.5.squares), custom_call_target="tpu_custom_call" | custom-call | tf_op jit(solution)/shard_map/finish/pallas_call | solution.py:311
  (2 shorter events, 0.1 us)
Async XLA Ops:
  3.1 10.1 %collective-permute-start.5 = (bf16[384,512]{1,0:T(8,128)(2,1)}, bf16[384,512]{1,0:T(8,128)(2,1)S(1)}, u32[]{:S(2)}, u32[]{:S(2)}) collective-permute-start(bf16[384,512]{1,0:T(8,128)(2,1)} %get-tuple-element.36.own_kv), channel_id=1, source_target_pairs={{0,8},{8,0},{1,9},{9,1},{2,10},{10,2},{3,11},{11,3},{4,12},{12,4},... | collective-permute-start | bytes 1179656 | tf_op jit(solution)/shard_map/ppermute | solution.py:319
  6.4 8.9 %collective-permute-start.1 = (bf16[384,512]{1,0:T(8,128)(2,1)}, bf16[384,512]{1,0:T(8,128)(2,1)S(1)}, u32[]{:S(2)}, u32[]{:S(2)}) collective-permute-start(bf16[384,512]{1,0:T(8,128)(2,1)} %get-tuple-element.36.own_kv), channel_id=1, source_target_pairs={{0,16},{8,120},{16,32},{24,8},{32,48},{40,24},{48,64},{56,40},{64,... | collective-permute-start | bytes 1179656 | tf_op jit(solution)/shard_map/ppermute | solution.py:317
  10.2 13.7 %collective-permute-start.3 = (bf16[576,512]{1,0:T(8,128)(2,1)}, bf16[576,512]{1,0:T(8,128)(2,1)S(1)}, u32[]{:S(2)}, u32[]{:S(2)}) collective-permute-start(bf16[576,512]{1,0:T(8,128)(2,1)} %get-tuple-element.38), channel_id=1, source_target_pairs={{0,128},{128,0},{1,129},{129,1},{2,130},{130,2},{3,131},{131,3},{4... | collective-permute-start | bytes 1769480 | tf_op jit(solution)/shard_map/ppermute | solution.py:318
  13.1 6.9 %collective-permute-start.6 = (bf16[384,512]{1,0:T(8,128)(2,1)S(1)}, bf16[384,512]{1,0:T(8,128)(2,1)S(1)}, u32[]{:S(2)}, u32[]{:S(2)}) collective-permute-start(bf16[384,512]{1,0:T(8,128)(2,1)S(1)} %collective-permute-done.5), channel_id=1, source_target_pairs={{0,16},{8,120},{16,32},{24,8},{32,48},{40,24},{48,64},{56,40},{64,... | collective-permute-start | bytes 1179656 | tf_op jit(solution)/shard_map/ppermute | solution.py:317
  15.3 9.0 %collective-permute-start.2 = (bf16[384,512]{1,0:T(8,128)(2,1)S(1)}, bf16[384,512]{1,0:T(8,128)(2,1)S(1)}, u32[]{:S(2)}, u32[]{:S(2)}) collective-permute-start(bf16[384,512]{1,0:T(8,128)(2,1)S(1)} %collective-permute-done.1.refs_0_), channel_id=1, source_target_pairs={{0,16},{8,120},{16,32},{24,8},{32,48},{40,24},{48,64},{56,40},{64,... | collective-permute-start | bytes 1179656 | tf_op jit(solution)/shard_map/ppermute | solution.py:317
  20.1 8.4 %collective-permute-start.7 = (bf16[384,512]{1,0:T(8,128)(2,1)S(1)}, bf16[384,512]{1,0:T(8,128)(2,1)S(1)}, u32[]{:S(2)}, u32[]{:S(2)}) collective-permute-start(bf16[384,512]{1,0:T(8,128)(2,1)S(1)} %collective-permute-done.6.refs_1_), channel_id=1, source_target_pairs={{0,16},{8,120},{16,32},{24,8},{32,48},{40,24},{48,64},{56,40},{64,... | collective-permute-start | bytes 1179656 | tf_op jit(solution)/shard_map/ppermute | solution.py:317
  24.3 6.6 %collective-permute-start.4 = (bf16[576,512]{1,0:T(8,128)(2,1)S(1)}, bf16[576,512]{1,0:T(8,128)(2,1)S(1)}, u32[]{:S(2)}, u32[]{:S(2)}) collective-permute-start(bf16[576,512]{1,0:T(8,128)(2,1)S(1)} %collective-permute-done.3.peer), channel_id=1, source_target_pairs={{0,8},{8,0},{1,9},{9,1},{2,10},{10,2},{3,11},{11,3},{4,12},{12,4},... | collective-permute-start | bytes 1769480 | tf_op jit(solution)/shard_map/ppermute | solution.py:319
  28.5 17.6 %collective-permute-start.8 = (bf16[384,512]{1,0:T(8,128)(2,1)S(1)}, bf16[384,512]{1,0:T(8,128)(2,1)S(1)}, u32[]{:S(2)}, u32[]{:S(2)}) collective-permute-start(bf16[384,512]{1,0:T(8,128)(2,1)S(1)} %slice.6), channel_id=1, source_target_pairs={{0,16},{8,120},{16,32},{24,8},{32,48},{40,24},{48,64},{56,40},{64,... | collective-permute-start | bytes 1179656 | tf_op jit(solution)/shard_map/ppermute | solution.py:317
  30.9 2.6 %collective-permute-start = (bf16[384,256]{1,0:T(8,128)(2,1)}, bf16[384,256]{1,0:T(8,128)(2,1)S(1)}, u32[]{:S(2)}, u32[]{:S(2)}) collective-permute-start(bf16[384,256]{1,0:T(8,128)(2,1)} %get-tuple-element.37.own_q), channel_id=1, source_target_pairs={{0,8},{8,0},{1,9},{9,1},{2,10},{10,2},{3,11},{11,3},{4,12},{12,4},... | collective-permute-start | bytes 589832 | tf_op jit(solution)/shard_map/ppermute | solution.py:319
  31.0 16.7 %collective-permute-start.11 = (bf16[384,512]{1,0:T(8,128)(2,1)S(1)}, bf16[384,512]{1,0:T(8,128)(2,1)S(1)}, u32[]{:S(2)}, u32[]{:S(2)}) collective-permute-start(bf16[384,512]{1,0:T(8,128)(2,1)S(1)} %slice.8), channel_id=1, source_target_pairs={{0,16},{8,120},{16,32},{24,8},{32,48},{40,24},{48,64},{56,40},{64,... | collective-permute-start | bytes 1179656 | tf_op jit(solution)/shard_map/ppermute | solution.py:317
  32.8 21.1 %collective-permute-start.10 = (bf16[384,512]{1,0:T(8,128)(2,1)S(1)}, bf16[384,512]{1,0:T(8,128)(2,1)S(1)}, u32[]{:S(2)}, u32[]{:S(2)}) collective-permute-start(bf16[384,512]{1,0:T(8,128)(2,1)S(1)} %collective-permute-done.2.refs_0_), channel_id=1, source_target_pairs={{0,16},{8,120},{16,32},{24,8},{32,48},{40,24},{48,64},{56,40},{64,... | collective-permute-start | bytes 1179656 | tf_op jit(solution)/shard_map/ppermute | solution.py:317
  32.9 21.0 %collective-permute-start.12 = (bf16[384,512]{1,0:T(8,128)(2,1)S(1)}, bf16[384,512]{1,0:T(8,128)(2,1)S(1)}, u32[]{:S(2)}, u32[]{:S(2)}) collective-permute-start(bf16[384,512]{1,0:T(8,128)(2,1)S(1)} %collective-permute-done.7.refs_1_), channel_id=1, source_target_pairs={{0,16},{8,120},{16,32},{24,8},{32,48},{40,24},{48,64},{56,40},{64,... | collective-permute-start | bytes 1179656 | tf_op jit(solution)/shard_map/ppermute | solution.py:317
  33.5 1.0 %copy-start = (bf16[384,512]{1,0:T(8,128)(2,1)S(1)}, bf16[384,512]{1,0:T(8,128)(2,1)}, u32[]{:S(2)}) copy-start(bf16[384,512]{1,0:T(8,128)(2,1)} %get-tuple-element.36.own_kv) | copy-start | bytes 1179652
  34.5 0.9 copy-start.1
  46.1 11.2 %collective-permute-start.9 = (bf16[384,512]{1,0:T(8,128)(2,1)S(1)}, bf16[384,512]{1,0:T(8,128)(2,1)S(1)}, u32[]{:S(2)}, u32[]{:S(2)}) collective-permute-start(bf16[384,512]{1,0:T(8,128)(2,1)S(1)} %collective-permute-done.8.refs_0_), channel_id=1, source_target_pairs={{0,16},{8,120},{16,32},{24,8},{32,48},{40,24},{48,64},{56,40},{64,... | collective-permute-start | bytes 1179656 | tf_op jit(solution)/shard_map/ppermute | solution.py:317
  47.6 9.8 %collective-permute-start.14 = (bf16[384,512]{1,0:T(8,128)(2,1)S(1)}, bf16[384,512]{1,0:T(8,128)(2,1)S(1)}, u32[]{:S(2)}, u32[]{:S(2)}) collective-permute-start(bf16[384,512]{1,0:T(8,128)(2,1)S(1)} %collective-permute-done.11.refs_1_), channel_id=1, source_target_pairs={{0,16},{8,120},{16,32},{24,8},{32,48},{40,24},{48,64},{56,40},{64,... | collective-permute-start | bytes 1179656 | tf_op jit(solution)/shard_map/ppermute | solution.py:317
  57.3 7.5 %collective-permute-start.13 = (bf16[384,512]{1,0:T(8,128)(2,1)S(1)}, bf16[384,512]{1,0:T(8,128)(2,1)S(1)}, u32[]{:S(2)}, u32[]{:S(2)}) collective-permute-start(bf16[384,512]{1,0:T(8,128)(2,1)S(1)} %collective-permute-done.9.refs_0_), channel_id=1, source_target_pairs={{0,16},{8,120},{16,32},{24,8},{32,48},{40,24},{48,64},{56,40},{64,... | collective-permute-start | bytes 1179656 | tf_op jit(solution)/shard_map/ppermute | solution.py:317
  57.5 11.0 %collective-permute-start.17 = (bf16[384,512]{1,0:T(8,128)(2,1)S(1)}, bf16[384,512]{1,0:T(8,128)(2,1)S(1)}, u32[]{:S(2)}, u32[]{:S(2)}) collective-permute-start(bf16[384,512]{1,0:T(8,128)(2,1)S(1)} %collective-permute-done.14.refs_1_), channel_id=1, source_target_pairs={{0,16},{8,120},{16,32},{24,8},{32,48},{40,24},{48,64},{56,40},{64,... | collective-permute-start | bytes 1179656 | tf_op jit(solution)/shard_map/ppermute | solution.py:317
  59.8 12.9 %collective-permute-start.16 = (bf16[384,512]{1,0:T(8,128)(2,1)S(1)}, bf16[384,512]{1,0:T(8,128)(2,1)S(1)}, u32[]{:S(2)}, u32[]{:S(2)}) collective-permute-start(bf16[384,512]{1,0:T(8,128)(2,1)S(1)} %collective-permute-done.10.refs_0_), channel_id=1, source_target_pairs={{0,16},{8,120},{16,32},{24,8},{32,48},{40,24},{48,64},{56,40},{64,... | collective-permute-start | bytes 1179656 | tf_op jit(solution)/shard_map/ppermute | solution.py:317
  64.8 12.2 %collective-permute-start.15 = (bf16[384,512]{1,0:T(8,128)(2,1)S(1)}, bf16[384,512]{1,0:T(8,128)(2,1)S(1)}, u32[]{:S(2)}, u32[]{:S(2)}) collective-permute-start(bf16[384,512]{1,0:T(8,128)(2,1)S(1)} %collective-permute-done.13.refs_0_), channel_id=1, source_target_pairs={{0,16},{8,120},{16,32},{24,8},{32,48},{40,24},{48,64},{56,40},{64,... | collective-permute-start | bytes 1179656 | tf_op jit(solution)/shard_map/ppermute | solution.py:317
  78.1 3.9 %collective-permute-start.18 = (bf16[768,256]{1,0:T(8,128)(2,1)S(1)}, bf16[768,256]{1,0:T(8,128)(2,1)S(1)}, u32[]{:S(2)}, u32[]{:S(2)}) collective-permute-start(bf16[768,256]{1,0:T(8,128)(2,1)S(1)} %get-tuple-element.65), channel_id=1, source_target_pairs={{0,8},{8,0},{1,9},{9,1},{2,10},{10,2},{3,11},{11,3},{4,12},{12,4},... | collective-permute-start | bytes 1179656 | tf_op jit(solution)/shard_map/ppermute | solution.py:319
  80.7 1.9 %collective-permute-start.19 = (f32[768,128]{1,0:T(8,128)S(1)}, f32[768,128]{1,0:T(8,128)S(1)}, u32[]{:S(2)}, u32[]{:S(2)}) collective-permute-start(f32[768,128]{1,0:T(8,128)S(1)} %get-tuple-element.66), channel_id=1, source_target_pairs={{0,8},{8,0},{1,9},{9,1},{2,10},{10,2},{3,11},{11,3},{4,12},{12,4},... | collective-permute-start | bytes 1179656 | tf_op jit(solution)/shard_map/ppermute | solution.py:319
  83.6 13.9 %collective-permute-start.20 = (bf16[384,256]{1,0:T(8,128)(2,1)S(1)}, bf16[384,256]{1,0:T(8,128)(2,1)S(1)}, u32[]{:S(2)}, u32[]{:S(2)}) collective-permute-start(bf16[384,256]{1,0:T(8,128)(2,1)S(1)} %get-tuple-element.68), channel_id=1, source_target_pairs={{0,128},{128,0},{1,129},{129,1},{2,130},{130,2},{3,131},{131,3},{4... | collective-permute-start | bytes 589832 | tf_op jit(solution)/shard_map/ppermute | solution.py:318

commit v7 on v6

--- a/solution.py
+++ b/solution.py
@@ -325,12 +325,12 @@
     core_kv = over_core(own_kv)
     near = [hop(own_kv), hop(core_kv)]
     near_next = [hop(a) for a in near]
-    first, peer = after(near_next[0], peer)
+    core_q = over_core(own_q)
+    first, peer, core_q = lax.optimization_barrier((near_next[0], peer, core_q))
     peer_core = over_core(peer)
     second, peer_kv = after(near_next[1], peer[:tokens])
     near_three = [hop(first), hop(second)]
     far = [hop(peer_kv), hop(peer_core[:tokens])]
-    core_q = over_core(own_q)
     state, query = begin(own_kv, own_q, core_q, peer, peer_core)
 
     def turn(pair, state, count):

time: 98.9 us -> 98.8 us (level)
  starting transfers between devices: 37.8 us -> 38.8 us
  waiting for transfers between devices: 13.9 us -> 12.9 us
    ppermute x5, starting transfers between devices: 7.22 us -> 10.6 us  [on_device(): over_core = lambda a: lax.ppermute(a, 'core', SWAP)]
    ppermute x14, starting transfers between devices: 24.8 us -> 22.4 us  [on_device(): hop = lambda a: lax.ppermute(a, ('z', 'core'), hop_pairs)]
    ppermute x14, waiting for transfers between devices: 12.2 us -> 11.2 us  [on_device(): hop = lambda a: lax.ppermute(a, ('z', 'core'), hop_pairs)]
  transfers between devices with their start and end apart: 21 -> 21, of which waited for: 9 -> 10; matrix products, arithmetic and copies ran while one was open for 0% -> 0% of each run, Pallas kernels for 28% -> 28%
where the time goes in v7:
time: 98.8 us; the launch traced here: 98.6 us
  starting transfers between devices  38.8 us (39%)
  Pallas kernels  33.2 us (34%)
  waiting for transfers between devices  12.9 us (13%)
  blocking collectives  10.9 us (11%)
  local copies, waits for them, and re-layouts  1.97 us (2%)
    pallas_call x9, Pallas kernels, attend(): pl.pallas_call(functools.partial(attend_kernel, len(kvs), base, kind is n...  24.9 us
    ppermute x14, starting transfers between devices, on_device(): hop = lambda a: lax.ppermute(a, ('z', 'core'), hop_pairs)  22.4 us
    ppermute x14, waiting for transfers between devices, on_device(): hop = lambda a: lax.ppermute(a, ('z', 'core'), hop_pairs)  11.2 us
    all_to_all x1, blocking collectives, on_device(): squares = lax.all_to_all(squares, ('yh', 'yl', 'x'), 0, 0, tiled=True)  10.9 us
    ppermute x5, starting transfers between devices, on_device(): over_core = lambda a: lax.ppermute(a, 'core', SWAP)  10.6 us
    ppermute x2, starting transfers between devices, on_device(): over_y = lambda a: lax.ppermute(a, 'yh', SWAP)  5.84 us
    pallas_call x1, Pallas kernels, begin(): pl.pallas_call(begin_kernel, out_shape=[jax.ShapeDtypeStruct((rows, 5 * D...  3.74 us
    pallas_call x1, Pallas kernels, pack(): pl.pallas_call(pack_kernel, grid=(2,), in_specs=[row(2 * DH)] * 6, out_sp...  2.43 us
  transfers between devices with their start and end apart: 21, of which 10 were waited for; matrix products, arithmetic and copies ran while one was open for 0% of the time, Pallas kernels for 28%

profile of v7, /device:TPU:1, one launch (start us, length us, event | category | flops | bytes accessed | tf_op | source)
XLA Modules:
  0.0 98.6 jit_solution(12230401779410980783)
XLA Ops:
  0.6 2.4 %pack.1 = (bf16[384,512]{1,0:T(8,128)(2,1)}, bf16[384,256]{1,0:T(8,128)(2,1)}, bf16[576,512]{1,0:T(8,128)(2,1)}) custom-call(bf16[384,256]{1,0:T(8,128)(2,1)} %q.1, bf16[384,256]{1,0:T(8,128)(2,1)} %k.1, bf16[384,256]{1,0:T(8,128)(2,1)} %v.1, bf16[384,256]{1,0:T(8,128)(2,1)} %qt.1, bf16[384,256]{1,0:T(8,128)(2,1)} %kt.1, bf16[384,256]{1,0:T(8,128)(2,1)} %vt.1), custom_call_target="tpu_custom_call" | custom-call | bytes 2359296 | tf_op jit(solution)/shard_map/pack/pallas_call | solution.py:58
  3.1 3.3 %collective-permute-start.5 = (bf16[384,512]{1,0:T(8,128)(2,1)}, bf16[384,512]{1,0:T(8,128)(2,1)S(1)}, u32[]{:S(2)}, u32[]{:S(2)}) collective-permute-start(bf16[384,512]{1,0:T(8,128)(2,1)} %get-tuple-element.37.own_kv), channel_id=1, source_target_pairs={{0,8},{8,0},{1,9},{9,1},{2,10},{10,2},{3,11},{11,3},{4,12},{12,4},... | collective-permute-start | bytes 1179656 | tf_op jit(solution)/shard_map/ppermute | solution.py:319
  6.4 3.8 %collective-permute-start = (bf16[384,512]{1,0:T(8,128)(2,1)}, bf16[384,512]{1,0:T(8,128)(2,1)S(1)}, u32[]{:S(2)}, u32[]{:S(2)}) collective-permute-start(bf16[384,512]{1,0:T(8,128)(2,1)} %get-tuple-element.37.own_kv), channel_id=1, source_target_pairs={{0,16},{8,120},{16,32},{24,8},{32,48},{40,24},{48,64},{56,40},{64,... | collective-permute-start | bytes 1179656 | tf_op jit(solution)/shard_map/ppermute | solution.py:317
  10.2 2.9 %collective-permute-start.2 = (bf16[576,512]{1,0:T(8,128)(2,1)}, bf16[576,512]{1,0:T(8,128)(2,1)S(1)}, u32[]{:S(2)}, u32[]{:S(2)}) collective-permute-start(bf16[576,512]{1,0:T(8,128)(2,1)} %get-tuple-element.39), channel_id=1, source_target_pairs={{0,128},{128,0},{1,129},{129,1},{2,130},{130,2},{3,131},{131,3},{4... | collective-permute-start | bytes 1769480 | tf_op jit(solution)/shard_map/ppermute | solution.py:318
  13.1 0.0 collective-permute-done.5
  13.1 0.7 collective-permute-start.6
  13.9 1.4 %collective-permute-done.refs_0_ = bf16[384,512]{1,0:T(8,128)(2,1)S(1)} collective-permute-done((bf16[384,512]{1,0:T(8,128)(2,1)}, bf16[384,512]{1,0:T(8,128)(2,1)S(1)}, u32[]{:S(2)}, u32[]{:S(2)}) %collective-permute-start) | collective-permute-done | bytes 393248 | tf_op jit(solution)/shard_map/ppermute | solution.py:317
  15.3 3.3 %collective-permute-start.1 = (bf16[384,512]{1,0:T(8,128)(2,1)S(1)}, bf16[384,512]{1,0:T(8,128)(2,1)S(1)}, u32[]{:S(2)}, u32[]{:S(2)}) collective-permute-start(bf16[384,512]{1,0:T(8,128)(2,1)S(1)} %collective-permute-done.refs_0_), channel_id=1, source_target_pairs={{0,16},{8,120},{16,32},{24,8},{32,48},{40,24},{48,64},{56,40},{64,... | collective-permute-start | bytes 1179656 | tf_op jit(solution)/shard_map/ppermute | solution.py:317
  18.6 0.0 collective-permute-start.3
  18.6 1.5 %collective-permute-done.6.refs_1_ = bf16[384,512]{1,0:T(8,128)(2,1)S(1)} collective-permute-done((bf16[384,512]{1,0:T(8,128)(2,1)S(1)}, bf16[384,512]{1,0:T(8,128)(2,1)S(1)}, u32[]{:S(2)}, u32[]{:S(2)}) %collective-permute-start.6) | collective-permute-done | bytes 393248 | tf_op jit(solution)/shard_map/ppermute | solution.py:317
  20.1 2.7 %collective-permute-start.7 = (bf16[384,512]{1,0:T(8,128)(2,1)S(1)}, bf16[384,512]{1,0:T(8,128)(2,1)S(1)}, u32[]{:S(2)}, u32[]{:S(2)}) collective-permute-start(bf16[384,512]{1,0:T(8,128)(2,1)S(1)} %collective-permute-done.6.refs_1_), channel_id=1, source_target_pairs={{0,16},{8,120},{16,32},{24,8},{32,48},{40,24},{48,64},{56,40},{64,... | collective-permute-start | bytes 1179656 | tf_op jit(solution)/shard_map/ppermute | solution.py:317
  22.8 0.0 collective-permute-done.3.core_q
  22.8 1.1 %collective-permute-done.2.peer = bf16[576,512]{1,0:T(8,128)(2,1)S(1)} collective-permute-done((bf16[576,512]{1,0:T(8,128)(2,1)}, bf16[576,512]{1,0:T(8,128)(2,1)S(1)}, u32[]{:S(2)}, u32[]{:S(2)}) %collective-permute-start.2) | collective-permute-done | bytes 589856 | tf_op jit(solution)/shard_map/ppermute | solution.py:318
  23.9 0.4 collective-permute-done.1.refs_0_
  24.3 1.3 %collective-permute-start.4 = (bf16[576,512]{1,0:T(8,128)(2,1)S(1)}, bf16[576,512]{1,0:T(8,128)(2,1)S(1)}, u32[]{:S(2)}, u32[]{:S(2)}) collective-permute-start(bf16[576,512]{1,0:T(8,128)(2,1)S(1)} %collective-permute-done.2.peer), channel_id=1, source_target_pairs={{0,8},{8,0},{1,9},{9,1},{2,10},{10,2},{3,11},{11,3},{4,12},{12,4},... | collective-permute-start | bytes 1769480 | tf_op jit(solution)/shard_map/ppermute | solution.py:319
  25.6 2.9 %collective-permute-done.7.refs_1_ = bf16[384,512]{1,0:T(8,128)(2,1)S(1)} collective-permute-done((bf16[384,512]{1,0:T(8,128)(2,1)S(1)}, bf16[384,512]{1,0:T(8,128)(2,1)S(1)}, u32[]{:S(2)}, u32[]{:S(2)}) %collective-permute-start.7) | collective-permute-done | bytes 393248 | tf_op jit(solution)/shard_map/ppermute | solution.py:317
  28.5 2.4 %collective-permute-start.8 = (bf16[384,512]{1,0:T(8,128)(2,1)S(1)}, bf16[384,512]{1,0:T(8,128)(2,1)S(1)}, u32[]{:S(2)}, u32[]{:S(2)}) collective-permute-start(bf16[384,512]{1,0:T(8,128)(2,1)S(1)} %slice.6), channel_id=1, source_target_pairs={{0,16},{8,120},{16,32},{24,8},{32,48},{40,24},{48,64},{56,40},{64,... | collective-permute-start | bytes 1179656 | tf_op jit(solution)/shard_map/ppermute | solution.py:317
  30.9 0.0 collective-permute-done.4.peer_core
  31.0 0.1 collective-permute-start.11
  31.0 0.5 collective-permute-start.10
  31.6 0.7 collective-permute-start.12
  32.3 0.0 copy-start
  32.3 1.0 %copy-done = bf16[384,512]{1,0:T(8,128)(2,1)S(1)} copy-done((bf16[384,512]{1,0:T(8,128)(2,1)S(1)}, bf16[384,512]{1,0:T(8,128)(2,1)}, u32[]{:S(2)}) %copy-start) | copy-done | bytes 393240
  33.3 0.0 copy-start.1
  33.3 0.9 copy-done.1
  34.2 3.7 %begin.1 = (f32[1536,640]{1,0:T(8,128)S(1)}, bf16[1536,256]{1,0:T(8,128)(2,1)S(1)}) custom-call(bf16[384,512]{1,0:T(8,128)(2,1)S(1)} %copy-done, bf16[384,256]{1,0:T(8,128)(2,1)S(1)} %copy-done.1, bf16[384,256]{1,0:T(8,128)(2,1)S(1)} %collective-permute-done.3.core_q, bf16[576,512]{1,0:T(8,128)(2,1)S(1)} %collective-permute-done.2.peer, ...), custom_call_target="tpu_custom_call" | custom-call | flops 1024 | bytes 1024 | tf_op jit(solution)/shard_map/begin/pallas_call | solution.py:208
  38.0 3.5 %attend.9.refs_2_ = f32[1536,640]{1,0:T(8,128)S(1)} custom-call(bf16[1536,256]{1,0:T(8,128)(2,1)S(1)} %get-tuple-element.42.q_ref, bf16[384,512]{1,0:T(8,128)(2,1)S(1)} %collective-permute-done.refs_0_, bf16[384,512]{1,0:T(8,128)(2,1)S(1)} %collective-permute-done.6.refs_1_, f32[1536,640]{1,0:T(8,128)S(1)} %get-tuple-element.44.refs_2_), custom_call_target="tpu_custom_call" | custom-call | flops 1024 | bytes 1024 | tf_op jit(solution)/shard_map/attend/pallas_call | solution.py:228
  41.5 3.3 %attend.10.refs_2_ = f32[1536,640]{1,0:T(8,128)S(1)} custom-call(bf16[1536,256]{1,0:T(8,128)(2,1)S(1)} %get-tuple-element.42.q_ref, bf16[384,512]{1,0:T(8,128)(2,1)S(1)} %collective-permute-done.1.refs_0_, bf16[384,512]{1,0:T(8,128)(2,1)S(1)} %collective-permute-done.7.refs_1_, f32[1536,640]{1,0:T(8,128)S(1)} %attend.9.refs_2_), custom_call_target="tpu_custom_call" | custom-call | flops 1024 | bytes 1024 | tf_op jit(solution)/shard_map/attend/pallas_call | solution.py:228
  44.8 0.0 collective-permute-done.8.refs_0_
  44.8 1.0 %collective-permute-start.9 = (bf16[384,512]{1,0:T(8,128)(2,1)S(1)}, bf16[384,512]{1,0:T(8,128)(2,1)S(1)}, u32[]{:S(2)}, u32[]{:S(2)}) collective-permute-start(bf16[384,512]{1,0:T(8,128)(2,1)S(1)} %collective-permute-done.8.refs_0_), channel_id=1, source_target_pairs={{0,16},{8,120},{16,32},{24,8},{32,48},{40,24},{48,64},{56,40},{64,... | collective-permute-start | bytes 1179656 | tf_op jit(solution)/shard_map/ppermute | solution.py:317
  45.8 0.0 collective-permute-done.11.refs_1_
  45.8 0.1 collective-permute-start.14
  45.9 3.3 %attend.11.refs_2_ = f32[1536,640]{1,0:T(8,128)S(1)} custom-call(bf16[1536,256]{1,0:T(8,128)(2,1)S(1)} %get-tuple-element.42.q_ref, bf16[384,512]{1,0:T(8,128)(2,1)S(1)} %collective-permute-done.8.refs_0_, bf16[384,512]{1,0:T(8,128)(2,1)S(1)} %collective-permute-done.11.refs_1_, f32[1536,640]{1,0:T(8,128)S(1)} %attend.10.refs_2_), custom_call_target="tpu_custom_call" | custom-call | flops 1024 | bytes 1024 | tf_op jit(solution)/shard_map/attend/pallas_call | solution.py:228
  49.3 0.0 collective-permute-done.10.refs_0_
  49.3 0.0 collective-permute-done.12.refs_1_
  49.3 3.3 %attend.12.refs_2_ = f32[1536,640]{1,0:T(8,128)S(1)} custom-call(bf16[1536,256]{1,0:T(8,128)(2,1)S(1)} %get-tuple-element.42.q_ref, bf16[384,512]{1,0:T(8,128)(2,1)S(1)} %collective-permute-done.10.refs_0_, bf16[384,512]{1,0:T(8,128)(2,1)S(1)} %collective-permute-done.12.refs_1_, f32[1536,640]{1,0:T(8,128)S(1)} %attend.11.refs_2_), custom_call_target="tpu_custom_call" | custom-call | flops 1024 | bytes 1024 | tf_op jit(solution)/shard_map/attend/pallas_call | solution.py:228
  52.6 0.0 collective-permute-done.9.refs_0_
  52.6 3.0 %collective-permute-start.13 = (bf16[384,512]{1,0:T(8,128)(2,1)S(1)}, bf16[384,512]{1,0:T(8,128)(2,1)S(1)}, u32[]{:S(2)}, u32[]{:S(2)}) collective-permute-start(bf16[384,512]{1,0:T(8,128)(2,1)S(1)} %collective-permute-done.9.refs_0_), channel_id=1, source_target_pairs={{0,16},{8,120},{16,32},{24,8},{32,48},{40,24},{48,64},{56,40},{64,... | collective-permute-start | bytes 1179656 | tf_op jit(solution)/shard_map/ppermute | solution.py:317
  55.6 1.1 %collective-permute-done.14.refs_1_ = bf16[384,512]{1,0:T(8,128)(2,1)S(1)} collective-permute-done((bf16[384,512]{1,0:T(8,128)(2,1)S(1)}, bf16[384,512]{1,0:T(8,128)(2,1)S(1)}, u32[]{:S(2)}, u32[]{:S(2)}) %collective-permute-start.14) | collective-permute-done | bytes 393248 | tf_op jit(solution)/shard_map/ppermute | solution.py:317
  56.7 3.1 %collective-permute-start.17 = (bf16[384,512]{1,0:T(8,128)(2,1)S(1)}, bf16[384,512]{1,0:T(8,128)(2,1)S(1)}, u32[]{:S(2)}, u32[]{:S(2)}) collective-permute-start(bf16[384,512]{1,0:T(8,128)(2,1)S(1)} %collective-permute-done.14.refs_1_), channel_id=1, source_target_pairs={{0,16},{8,120},{16,32},{24,8},{32,48},{40,24},{48,64},{56,40},{64,... | collective-permute-start | bytes 1179656 | tf_op jit(solution)/shard_map/ppermute | solution.py:317
  59.8 0.0 collective-permute-start.16
  59.9 3.3 %attend.13.refs_2_ = f32[1536,640]{1,0:T(8,128)S(1)} custom-call(bf16[1536,256]{1,0:T(8,128)(2,1)S(1)} %get-tuple-element.42.q_ref, bf16[384,512]{1,0:T(8,128)(2,1)S(1)} %collective-permute-done.9.refs_0_, bf16[384,512]{1,0:T(8,128)(2,1)S(1)} %collective-permute-done.14.refs_1_, f32[1536,640]{1,0:T(8,128)S(1)} %attend.12.refs_2_), custom_call_target="tpu_custom_call" | custom-call | flops 1024 | bytes 1024 | tf_op jit(solution)/shard_map/attend/pallas_call | solution.py:228
  63.2 0.0 collective-permute-done.13.refs_0_
  63.2 0.8 collective-permute-start.15
  64.0 1.1 %collective-permute-done.17.refs_1_ = bf16[384,512]{1,0:T(8,128)(2,1)S(1)} collective-permute-done((bf16[384,512]{1,0:T(8,128)(2,1)S(1)}, bf16[384,512]{1,0:T(8,128)(2,1)S(1)}, u32[]{:S(2)}, u32[]{:S(2)}) %collective-permute-start.17) | collective-permute-done | bytes 393248 | tf_op jit(solution)/shard_map/ppermute | solution.py:317
  65.1 3.3 %attend.14.refs_1_ = f32[1536,640]{1,0:T(8,128)S(1)} custom-call(bf16[1536,256]{1,0:T(8,128)(2,1)S(1)} %get-tuple-element.42.q_ref, bf16[384,512]{1,0:T(8,128)(2,1)S(1)} %collective-permute-done.13.refs_0_, bf16[384,512]{1,0:T(8,128)(2,1)S(1)} %collective-permute-done.17.refs_1_, f32[1536,640]{1,0:T(8,128)S(1)} %attend.13.refs_2_), custom_call_target="tpu_custom_call" | custom-call | flops 1024 | bytes 1024 | tf_op jit(solution)/shard_map/attend/pallas_call | solution.py:228
  68.5 0.9 collective-permute-done.16.refs_0_
  69.3 2.3 %attend.15.refs_1_ = f32[1536,640]{1,0:T(8,128)S(1)} custom-call(bf16[1536,256]{1,0:T(8,128)(2,1)S(1)} %get-tuple-element.42.q_ref, bf16[384,512]{1,0:T(8,128)(2,1)S(1)} %collective-permute-done.16.refs_0_, f32[1536,640]{1,0:T(8,128)S(1)} %attend.14.refs_1_), custom_call_target="tpu_custom_call" | custom-call | flops 1024 | bytes 1024 | tf_op jit(solution)/shard_map/attend/pallas_call | solution.py:228
  71.7 1.9 %collective-permute-done.15.refs_0_ = bf16[384,512]{1,0:T(8,128)(2,1)S(1)} collective-permute-done((bf16[384,512]{1,0:T(8,128)(2,1)S(1)}, bf16[384,512]{1,0:T(8,128)(2,1)S(1)}, u32[]{:S(2)}, u32[]{:S(2)}) %collective-permute-start.15) | collective-permute-done | bytes 393248 | tf_op jit(solution)/shard_map/ppermute | solution.py:317
  73.6 1.2 %attend.17 = (bf16[768,256]{1,0:T(8,128)(2,1)S(1)}, f32[768,128]{1,0:T(8,128)S(1)}) custom-call(bf16[1536,256]{1,0:T(8,128)(2,1)S(1)} %get-tuple-element.42.q_ref, bf16[384,512]{1,0:T(8,128)(2,1)S(1)} %collective-permute-done.15.refs_0_, f32[1536,640]{1,0:T(8,128)S(1)} %attend.15.refs_1_), custom_call_target="tpu_custom_call" | custom-call | flops 1024 | bytes 1024 | tf_op jit(solution)/shard_map/attend/pallas_call | solution.py:228
  74.8 5.9 %collective-permute-start.18 = (bf16[768,256]{1,0:T(8,128)(2,1)S(1)}, bf16[768,256]{1,0:T(8,128)(2,1)S(1)}, u32[]{:S(2)}, u32[]{:S(2)}) collective-permute-start(bf16[768,256]{1,0:T(8,128)(2,1)S(1)} %get-tuple-element.67), channel_id=1, source_target_pairs={{0,8},{8,0},{1,9},{9,1},{2,10},{10,2},{3,11},{11,3},{4,12},{12,4},... | collective-permute-start | bytes 1179656 | tf_op jit(solution)/shard_map/ppermute | solution.py:319
  80.7 0.1 collective-permute-start.19
  80.8 1.2 %attend.16 = (f32[768,256]{1,0:T(8,128)S(1)}, f32[768,128]{1,0:T(8,128)S(1)}) custom-call(bf16[1536,256]{1,0:T(8,128)(2,1)S(1)} %get-tuple-element.42.q_ref, bf16[384,512]{1,0:T(8,128)(2,1)S(1)} %collective-permute-done.15.refs_0_, f32[1536,640]{1,0:T(8,128)S(1)} %attend.15.refs_1_), custom_call_target="tpu_custom_call" | custom-call | flops 1024 | bytes 1024 | tf_op jit(solution)/shard_map/attend/pallas_call | solution.py:228
  82.0 0.0 collective-permute-done.18.other
  82.0 0.6 collective-permute-done.19.other_stat
  82.6 1.0 %join.1 = (f32[384,256]{1,0:T(8,128)S(1)}, bf16[384,256]{1,0:T(8,128)(2,1)S(1)}, f32[16,8,128]{2,1,0:T(8,128)S(1)}) custom-call(f32[768,256]{1,0:T(8,128)S(1)} %get-tuple-element.65.mine, f32[768,128]{1,0:T(8,128)S(1)} %get-tuple-element.66.mine_stat, bf16[768,256]{1,0:T(8,128)(2,1)S(1)} %collective-permute-done.18.other, ...), custom_call_target="tpu_custom_call" | custom-call | tf_op jit(solution)/shard_map/join/pallas_call | solution.py:272
  83.6 2.9 %collective-permute-start.20 = (bf16[384,256]{1,0:T(8,128)(2,1)S(1)}, bf16[384,256]{1,0:T(8,128)(2,1)S(1)}, u32[]{:S(2)}, u32[]{:S(2)}) collective-permute-start(bf16[384,256]{1,0:T(8,128)(2,1)S(1)} %get-tuple-element.70), channel_id=1, source_target_pairs={{0,128},{128,0},{1,129},{129,1},{2,130},{130,2},{3,131},{131,3},{4... | collective-permute-start | bytes 589832 | tf_op jit(solution)/shard_map/ppermute | solution.py:318
  86.5 10.9 %all_to_all.5.squares = f32[16,8,128]{2,1,0:T(8,128)S(1)} all-to-all(f32[16,8,128]{2,1,0:T(8,128)S(1)} %get-tuple-element.71), channel_id=1, replica_groups=mesh['yh'=2,'z'=8,'core'=2,'yl'=2,'x'=4] {'yh','yl','x'}, dimensions={0} | all-to-all | bytes 131072 | tf_op jit(solution)/shard_map/all_to_all | solution.py:364
  97.4 0.0 collective-permute-done.20.come
  97.4 1.2 %finish.1 = (bf16[384,256]{1,0:T(8,128)(2,1)}, bf16[384,256]{1,0:T(8,128)(2,1)}) custom-call(f32[384,256]{1,0:T(8,128)S(1)} %get-tuple-element.69.keep, bf16[384,256]{1,0:T(8,128)(2,1)S(1)} %collective-permute-done.20.come, f32[16,8,128]{2,1,0:T(8,128)S(1)} %all_to_all.5.squares), custom_call_target="tpu_custom_call" | custom-call | tf_op jit(solution)/shard_map/finish/pallas_call | solution.py:311
  (2 shorter events, 0.1 us)
Async XLA Ops:
  3.1 10.1 %collective-permute-start.5 = (bf16[384,512]{1,0:T(8,128)(2,1)}, bf16[384,512]{1,0:T(8,128)(2,1)S(1)}, u32[]{:S(2)}, u32[]{:S(2)}) collective-permute-start(bf16[384,512]{1,0:T(8,128)(2,1)} %get-tuple-element.37.own_kv), channel_id=1, source_target_pairs={{0,8},{8,0},{1,9},{9,1},{2,10},{10,2},{3,11},{11,3},{4,12},{12,4},... | collective-permute-start | bytes 1179656 | tf_op jit(solution)/shard_map/ppermute | solution.py:319
  6.4 8.9 %collective-permute-start = (bf16[384,512]{1,0:T(8,128)(2,1)}, bf16[384,512]{1,0:T(8,128)(2,1)S(1)}, u32[]{:S(2)}, u32[]{:S(2)}) collective-permute-start(bf16[384,512]{1,0:T(8,128)(2,1)} %get-tuple-element.37.own_kv), channel_id=1, source_target_pairs={{0,16},{8,120},{16,32},{24,8},{32,48},{40,24},{48,64},{56,40},{64,... | collective-permute-start | bytes 1179656 | tf_op jit(solution)/shard_map/ppermute | solution.py:317
  10.2 13.7 %collective-permute-start.2 = (bf16[576,512]{1,0:T(8,128)(2,1)}, bf16[576,512]{1,0:T(8,128)(2,1)S(1)}, u32[]{:S(2)}, u32[]{:S(2)}) collective-permute-start(bf16[576,512]{1,0:T(8,128)(2,1)} %get-tuple-element.39), channel_id=1, source_target_pairs={{0,128},{128,0},{1,129},{129,1},{2,130},{130,2},{3,131},{131,3},{4... | collective-permute-start | bytes 1769480 | tf_op jit(solution)/shard_map/ppermute | solution.py:318
  13.1 6.9 %collective-permute-start.6 = (bf16[384,512]{1,0:T(8,128)(2,1)S(1)}, bf16[384,512]{1,0:T(8,128)(2,1)S(1)}, u32[]{:S(2)}, u32[]{:S(2)}) collective-permute-start(bf16[384,512]{1,0:T(8,128)(2,1)S(1)} %collective-permute-done.5), channel_id=1, source_target_pairs={{0,16},{8,120},{16,32},{24,8},{32,48},{40,24},{48,64},{56,40},{64,... | collective-permute-start | bytes 1179656 | tf_op jit(solution)/shard_map/ppermute | solution.py:317
  15.3 9.0 %collective-permute-start.1 = (bf16[384,512]{1,0:T(8,128)(2,1)S(1)}, bf16[384,512]{1,0:T(8,128)(2,1)S(1)}, u32[]{:S(2)}, u32[]{:S(2)}) collective-permute-start(bf16[384,512]{1,0:T(8,128)(2,1)S(1)} %collective-permute-done.refs_0_), channel_id=1, source_target_pairs={{0,16},{8,120},{16,32},{24,8},{32,48},{40,24},{48,64},{56,40},{64,... | collective-permute-start | bytes 1179656 | tf_op jit(solution)/shard_map/ppermute | solution.py:317
  18.6 4.2 %collective-permute-start.3 = (bf16[384,256]{1,0:T(8,128)(2,1)}, bf16[384,256]{1,0:T(8,128)(2,1)S(1)}, u32[]{:S(2)}, u32[]{:S(2)}) collective-permute-start(bf16[384,256]{1,0:T(8,128)(2,1)} %get-tuple-element.38.own_q), channel_id=1, source_target_pairs={{0,8},{8,0},{1,9},{9,1},{2,10},{10,2},{3,11},{11,3},{4,12},{12,4},... | collective-permute-start | bytes 589832 | tf_op jit(solution)/shard_map/ppermute | solution.py:319
  20.1 8.4 %collective-permute-start.7 = (bf16[384,512]{1,0:T(8,128)(2,1)S(1)}, bf16[384,512]{1,0:T(8,128)(2,1)S(1)}, u32[]{:S(2)}, u32[]{:S(2)}) collective-permute-start(bf16[384,512]{1,0:T(8,128)(2,1)S(1)} %collective-permute-done.6.refs_1_), channel_id=1, source_target_pairs={{0,16},{8,120},{16,32},{24,8},{32,48},{40,24},{48,64},{56,40},{64,... | collective-permute-start | bytes 1179656 | tf_op jit(solution)/shard_map/ppermute | solution.py:317
  24.3 6.6 %collective-permute-start.4 = (bf16[576,512]{1,0:T(8,128)(2,1)S(1)}, bf16[576,512]{1,0:T(8,128)(2,1)S(1)}, u32[]{:S(2)}, u32[]{:S(2)}) collective-permute-start(bf16[576,512]{1,0:T(8,128)(2,1)S(1)} %collective-permute-done.2.peer), channel_id=1, source_target_pairs={{0,8},{8,0},{1,9},{9,1},{2,10},{10,2},{3,11},{11,3},{4,12},{12,4},... | collective-permute-start | bytes 1769480 | tf_op jit(solution)/shard_map/ppermute | solution.py:319
  28.5 16.3 %collective-permute-start.8 = (bf16[384,512]{1,0:T(8,128)(2,1)S(1)}, bf16[384,512]{1,0:T(8,128)(2,1)S(1)}, u32[]{:S(2)}, u32[]{:S(2)}) collective-permute-start(bf16[384,512]{1,0:T(8,128)(2,1)S(1)} %slice.6), channel_id=1, source_target_pairs={{0,16},{8,120},{16,32},{24,8},{32,48},{40,24},{48,64},{56,40},{64,... | collective-permute-start | bytes 1179656 | tf_op jit(solution)/shard_map/ppermute | solution.py:317
  31.0 14.9 %collective-permute-start.11 = (bf16[384,512]{1,0:T(8,128)(2,1)S(1)}, bf16[384,512]{1,0:T(8,128)(2,1)S(1)}, u32[]{:S(2)}, u32[]{:S(2)}) collective-permute-start(bf16[384,512]{1,0:T(8,128)(2,1)S(1)} %slice.8), channel_id=1, source_target_pairs={{0,16},{8,120},{16,32},{24,8},{32,48},{40,24},{48,64},{56,40},{64,... | collective-permute-start | bytes 1179656 | tf_op jit(solution)/shard_map/ppermute | solution.py:317
  31.0 18.2 %collective-permute-start.10 = (bf16[384,512]{1,0:T(8,128)(2,1)S(1)}, bf16[384,512]{1,0:T(8,128)(2,1)S(1)}, u32[]{:S(2)}, u32[]{:S(2)}) collective-permute-start(bf16[384,512]{1,0:T(8,128)(2,1)S(1)} %collective-permute-done.1.refs_0_), channel_id=1, source_target_pairs={{0,16},{8,120},{16,32},{24,8},{32,48},{40,24},{48,64},{56,40},{64,... | collective-permute-start | bytes 1179656 | tf_op jit(solution)/shard_map/ppermute | solution.py:317
  31.6 17.7 %collective-permute-start.12 = (bf16[384,512]{1,0:T(8,128)(2,1)S(1)}, bf16[384,512]{1,0:T(8,128)(2,1)S(1)}, u32[]{:S(2)}, u32[]{:S(2)}) collective-permute-start(bf16[384,512]{1,0:T(8,128)(2,1)S(1)} %collective-permute-done.7.refs_1_), channel_id=1, source_target_pairs={{0,16},{8,120},{16,32},{24,8},{32,48},{40,24},{48,64},{56,40},{64,... | collective-permute-start | bytes 1179656 | tf_op jit(solution)/shard_map/ppermute | solution.py:317
  32.3 1.0 %copy-start = (bf16[384,512]{1,0:T(8,128)(2,1)S(1)}, bf16[384,512]{1,0:T(8,128)(2,1)}, u32[]{:S(2)}) copy-start(bf16[384,512]{1,0:T(8,128)(2,1)} %get-tuple-element.37.own_kv) | copy-start | bytes 1179652
  33.3 0.9 copy-start.1
  44.8 7.8 %collective-permute-start.9 = (bf16[384,512]{1,0:T(8,128)(2,1)S(1)}, bf16[384,512]{1,0:T(8,128)(2,1)S(1)}, u32[]{:S(2)}, u32[]{:S(2)}) collective-permute-start(bf16[384,512]{1,0:T(8,128)(2,1)S(1)} %collective-permute-done.8.refs_0_), channel_id=1, source_target_pairs={{0,16},{8,120},{16,32},{24,8},{32,48},{40,24},{48,64},{56,40},{64,... | collective-permute-start | bytes 1179656 | tf_op jit(solution)/shard_map/ppermute | solution.py:317
  45.8 10.9 %collective-permute-start.14 = (bf16[384,512]{1,0:T(8,128)(2,1)S(1)}, bf16[384,512]{1,0:T(8,128)(2,1)S(1)}, u32[]{:S(2)}, u32[]{:S(2)}) collective-permute-start(bf16[384,512]{1,0:T(8,128)(2,1)S(1)} %collective-permute-done.11.refs_1_), channel_id=1, source_target_pairs={{0,16},{8,120},{16,32},{24,8},{32,48},{40,24},{48,64},{56,40},{64,... | collective-permute-start | bytes 1179656 | tf_op jit(solution)/shard_map/ppermute | solution.py:317
  52.6 10.6 %collective-permute-start.13 = (bf16[384,512]{1,0:T(8,128)(2,1)S(1)}, bf16[384,512]{1,0:T(8,128)(2,1)S(1)}, u32[]{:S(2)}, u32[]{:S(2)}) collective-permute-start(bf16[384,512]{1,0:T(8,128)(2,1)S(1)} %collective-permute-done.9.refs_0_), channel_id=1, source_target_pairs={{0,16},{8,120},{16,32},{24,8},{32,48},{40,24},{48,64},{56,40},{64,... | collective-permute-start | bytes 1179656 | tf_op jit(solution)/shard_map/ppermute | solution.py:317
  56.7 8.4 %collective-permute-start.17 = (bf16[384,512]{1,0:T(8,128)(2,1)S(1)}, bf16[384,512]{1,0:T(8,128)(2,1)S(1)}, u32[]{:S(2)}, u32[]{:S(2)}) collective-permute-start(bf16[384,512]{1,0:T(8,128)(2,1)S(1)} %collective-permute-done.14.refs_1_), channel_id=1, source_target_pairs={{0,16},{8,120},{16,32},{24,8},{32,48},{40,24},{48,64},{56,40},{64,... | collective-permute-start | bytes 1179656 | tf_op jit(solution)/shard_map/ppermute | solution.py:317
  59.8 9.5 %collective-permute-start.16 = (bf16[384,512]{1,0:T(8,128)(2,1)S(1)}, bf16[384,512]{1,0:T(8,128)(2,1)S(1)}, u32[]{:S(2)}, u32[]{:S(2)}) collective-permute-start(bf16[384,512]{1,0:T(8,128)(2,1)S(1)} %collective-permute-done.10.refs_0_), channel_id=1, source_target_pairs={{0,16},{8,120},{16,32},{24,8},{32,48},{40,24},{48,64},{56,40},{64,... | collective-permute-start | bytes 1179656 | tf_op jit(solution)/shard_map/ppermute | solution.py:317
  63.2 10.4 %collective-permute-start.15 = (bf16[384,512]{1,0:T(8,128)(2,1)S(1)}, bf16[384,512]{1,0:T(8,128)(2,1)S(1)}, u32[]{:S(2)}, u32[]{:S(2)}) collective-permute-start(bf16[384,512]{1,0:T(8,128)(2,1)S(1)} %collective-permute-done.13.refs_0_), channel_id=1, source_target_pairs={{0,16},{8,120},{16,32},{24,8},{32,48},{40,24},{48,64},{56,40},{64,... | collective-permute-start | bytes 1179656 | tf_op jit(solution)/shard_map/ppermute | solution.py:317
  74.8 7.2 %collective-permute-start.18 = (bf16[768,256]{1,0:T(8,128)(2,1)S(1)}, bf16[768,256]{1,0:T(8,128)(2,1)S(1)}, u32[]{:S(2)}, u32[]{:S(2)}) collective-permute-start(bf16[768,256]{1,0:T(8,128)(2,1)S(1)} %get-tuple-element.67), channel_id=1, source_target_pairs={{0,8},{8,0},{1,9},{9,1},{2,10},{10,2},{3,11},{11,3},{4,12},{12,4},... | collective-permute-start | bytes 1179656 | tf_op jit(solution)/shard_map/ppermute | solution.py:319
  80.7 1.9 %collective-permute-start.19 = (f32[768,128]{1,0:T(8,128)S(1)}, f32[768,128]{1,0:T(8,128)S(1)}, u32[]{:S(2)}, u32[]{:S(2)}) collective-permute-start(f32[768,128]{1,0:T(8,128)S(1)} %get-tuple-element.68), channel_id=1, source_target_pairs={{0,8},{8,0},{1,9},{9,1},{2,10},{10,2},{3,11},{11,3},{4,12},{12,4},... | collective-permute-start | bytes 1179656 | tf_op jit(solution)/shard_map/ppermute | solution.py:319
  83.6 13.9 %collective-permute-start.20 = (bf16[384,256]{1,0:T(8,128)(2,1)S(1)}, bf16[384,256]{1,0:T(8,128)(2,1)S(1)}, u32[]{:S(2)}, u32[]{:S(2)}) collective-permute-start(bf16[384,256]{1,0:T(8,128)(2,1)S(1)} %get-tuple-element.70), channel_id=1, source_target_pairs={{0,128},{128,0},{1,129},{129,1},{2,130},{130,2},{3,131},{131,3},{4... | collective-permute-start | bytes 589832 | tf_op jit(solution)/shard_map/ppermute | solution.py:318
